TPU v7x, 256 devices: a whole 4x4x8 slice. The times are simulated.
256 devices in a mesh: inner: 16 (over z, y_hi), outer: 4 (over y_lo, core), head: 4 (over x).
Axes of the slice: x: 4, y: 4 (y_hi: 2, y_lo: 2; y = y_hi * 2 + y_lo), z: 8, core: 2. Of those that a mesh axis runs over, the one named last changes fastest.
Arguments:
- queries: bfloat16 [4, 16384, 128], P('head', ('inner', 'outer')), may hold values from -9 to 9
- key_vectors: bfloat16 [4, 16384, 128], P('head', ('inner', 'outer')), may hold values from -4 to 4
- value_vectors: bfloat16 [4, 16384, 128], P('head', ('inner', 'outer')), may hold values from -5 to 5
- out_grad: bfloat16 [4, 16384, 128], P('head', ('inner', 'outer')), may hold values from -5 to 5
- log_forget: float32 [4, 16384], P('head', ('inner', 'outer')), may hold values from -1.5 to 0
- span_order: int32 [128], replicated, may hold values from 0 to 127, as said below
Outputs:
- query_grad: bfloat16 [4, 16384, 128], P('head', ('inner', 'outer'))
- key_grad: bfloat16 [4, 16384, 128], P('head', ('inner', 'outer'))
- value_grad: bfloat16 [4, 16384, 128], P('head', ('inner', 'outer'))
- forget_grad: float32 [4, 16384], P('head', ('inner', 'outer'))
Inputs may be any that keep to these rules, and one draw needn't show every extreme that they name: `span_order`: a permutation of the span numbers; span c covers positions c * 128 to c * 128 + 127; the two slots of one device's rows hold spans whose numbers add up to 127.
All inputs are finite; a program needn't handle non-finite values.
Results may differ from a plain program's by a relative error of at most 0.0075.
Values may be sent and summed in bfloat16 or wider, within the bound.
No kernel may reach another device: no remote copies, remote signals or barrier semaphores. Data moves between devices by JAX's collectives and lax.ppermute only.
A program may use at most 64 MiB of HBM per device.

v0:
```python
import math

import jax
import jax.numpy as jnp
from jax import lax
from jax.sharding import PartitionSpec as P

masked_score = -1e30
block_rows = 512


def slot_positions(span_order, half_rows):
    span_count = span_order.shape[0]
    offsets = jnp.arange(half_rows, dtype=jnp.int32)
    return (span_order[:, None] * half_rows + offsets[None, :]).reshape(span_count * half_rows)


def gate_prefix(every_gate, span_order, half_rows):
    head_count = every_gate.shape[0]
    span_count = span_order.shape[0]
    within = jnp.cumsum(every_gate.reshape(head_count, span_count, half_rows), axis=2)
    totals = within[:, :, half_rows - 1]
    earlier = (span_order[None, :] < span_order[:, None]).astype(jnp.float32)
    offsets = jnp.sum(earlier[None, :, :] * totals[:, None, :], axis=2)
    return (offsets[:, :, None] + within).reshape(head_count, span_count * half_rows)


def in_blocks(step_fn, carry, piece):
    piece_rows = piece[0].shape[1]

    def single_block(inner_carry, block_index):
        offset = block_index * block_rows
        part_piece = tuple(
            (lax.dynamic_slice_in_dim(member, offset, block_rows, 1) for member in piece)
        )
        return (step_fn(inner_carry, part_piece, offset), None)

    return lax.scan(single_block, carry, jnp.arange(piece_rows // block_rows, dtype=jnp.int32))[0]


def scores_and_mask(
    query_matrix, query_prefix, query_pos, key_rows, key_prefix, key_pos, score_scale
):
    product = jnp.einsum("hqd,hkd->hqk", query_matrix, key_rows, preferred_element_type=jnp.float32)
    scores = product * score_scale + query_prefix[:, :, None] - key_prefix[:, None, :]
    allowed = key_pos[None, None, :] <= query_pos[None, :, None]
    return (scores, allowed)


def score_grads(
    query_matrix,
    grad_rows,
    piece_lse,
    piece_delta,
    query_prefix,
    query_pos,
    key_rows,
    value_rows,
    key_prefix,
    key_pos,
    score_scale,
):
    scores, allowed = scores_and_mask(
        query_matrix, query_prefix, query_pos, key_rows, key_prefix, key_pos, score_scale
    )
    weights = jnp.where(allowed, jnp.exp(scores - piece_lse[:, :, None]), 0.0)
    upstream = jnp.einsum("hqd,hkd->hqk", grad_rows, value_rows, preferred_element_type=jnp.float32)
    score_grad = weights * (upstream - piece_delta[:, :, None])
    return (weights, score_grad)


def local(queries, key_vectors, value_vectors, out_grad, log_forget, span_order):
    head_count, row_count, head_size = queries.shape
    half_rows = row_count // 2
    score_scale = 1.0 / math.sqrt(head_size)
    device_index = lax.axis_index(("inner", "outer"))
    every_gate = lax.all_gather(log_forget, ("inner", "outer"), axis=1, tiled=True)
    every_prefix = gate_prefix(every_gate, span_order, half_rows)
    every_pos = slot_positions(span_order, half_rows)
    first_row = device_index * row_count
    own_pos = lax.dynamic_slice_in_dim(every_pos, first_row, row_count, 0)
    own_prefix = lax.dynamic_slice_in_dim(every_prefix, first_row, row_count, 1)

    def forward_step(carry, piece, start):
        best, total, weighted = carry
        key_rows, value_rows = piece
        piece_rows = key_rows.shape[1]
        key_pos = lax.dynamic_slice_in_dim(every_pos, start, piece_rows, 0)
        key_prefix = lax.dynamic_slice_in_dim(every_prefix, start, piece_rows, 1)
        scores, allowed = scores_and_mask(
            queries, own_prefix, own_pos, key_rows, key_prefix, key_pos, score_scale
        )
        upstream = jnp.einsum(
            "hqd,hkd->hqk", out_grad, value_rows, preferred_element_type=jnp.float32
        )
        new_best = jnp.maximum(best, jnp.max(jnp.where(allowed, scores, masked_score), axis=2))
        factor = jnp.where(allowed, jnp.exp(scores - new_best[:, :, None]), 0.0)
        shrink = jnp.exp(best - new_best)
        return (
            new_best,
            total * shrink + jnp.sum(factor, axis=2),
            weighted * shrink + jnp.sum(factor * upstream, axis=2),
        )

    row_zeros = jnp.zeros((head_count, row_count), jnp.float32)
    best, total, weighted = in_blocks(
        forward_step,
        (row_zeros + masked_score, row_zeros, row_zeros),
        (
            lax.all_gather(key_vectors, ("inner", "outer"), axis=1, tiled=True),
            lax.all_gather(value_vectors, ("inner", "outer"), axis=1, tiled=True),
        ),
    )
    row_lse = best + jnp.log(total)
    row_delta = weighted / total
    block_zeros = jnp.zeros((head_count, row_count, head_size), jnp.float32)
    every_lse, every_delta = (
        lax.all_gather(row_lse, ("inner", "outer"), axis=1, tiled=True),
        lax.all_gather(row_delta, ("inner", "outer"), axis=1, tiled=True),
    )

    def query_step(query_acc, piece, start):
        key_rows, value_rows = piece
        piece_rows = key_rows.shape[1]
        key_pos = lax.dynamic_slice_in_dim(every_pos, start, piece_rows, 0)
        key_prefix = lax.dynamic_slice_in_dim(every_prefix, start, piece_rows, 1)
        weights, score_grad = score_grads(
            queries,
            out_grad,
            row_lse,
            row_delta,
            own_prefix,
            own_pos,
            key_rows,
            value_rows,
            key_prefix,
            key_pos,
            score_scale,
        )
        return query_acc + score_scale * jnp.einsum(
            "hqk,hkd->hqd",
            score_grad.astype(jnp.bfloat16),
            key_rows,
            preferred_element_type=jnp.float32,
        )

    query_acc = in_blocks(
        query_step,
        block_zeros,
        (
            lax.all_gather(key_vectors, ("inner", "outer"), axis=1, tiled=True),
            lax.all_gather(value_vectors, ("inner", "outer"), axis=1, tiled=True),
        ),
    )

    def key_step(carry, piece, start):
        key_acc, value_acc, prefix_acc = carry
        query_matrix, grad_rows = piece
        piece_rows = query_matrix.shape[1]
        query_pos = lax.dynamic_slice_in_dim(every_pos, start, piece_rows, 0)
        query_prefix = lax.dynamic_slice_in_dim(every_prefix, start, piece_rows, 1)
        piece_lse = lax.dynamic_slice_in_dim(every_lse, start, piece_rows, 1)
        piece_delta = lax.dynamic_slice_in_dim(every_delta, start, piece_rows, 1)
        weights, score_grad = score_grads(
            query_matrix,
            grad_rows,
            piece_lse,
            piece_delta,
            query_prefix,
            query_pos,
            key_vectors,
            value_vectors,
            own_prefix,
            own_pos,
            score_scale,
        )
        key_acc = key_acc + score_scale * jnp.einsum(
            "hqk,hqd->hkd",
            score_grad.astype(jnp.bfloat16),
            query_matrix,
            preferred_element_type=jnp.float32,
        )
        value_acc = value_acc + jnp.einsum(
            "hqk,hqd->hkd",
            weights.astype(jnp.bfloat16),
            grad_rows,
            preferred_element_type=jnp.float32,
        )
        prefix_acc = prefix_acc - jnp.sum(score_grad, axis=1)
        return (key_acc, value_acc, prefix_acc)

    key_acc, value_acc, prefix_acc = in_blocks(
        key_step,
        (block_zeros, block_zeros, row_zeros),
        (
            lax.all_gather(queries, ("inner", "outer"), axis=1, tiled=True),
            lax.all_gather(out_grad, ("inner", "outer"), axis=1, tiled=True),
        ),
    )
    span_count = span_order.shape[0]
    own_ids = lax.dynamic_slice_in_dim(span_order, device_index * 2, 2, 0)
    slot_ids = jnp.arange(span_count, dtype=jnp.int32)
    halves = prefix_acc.reshape(head_count, 2, half_rows)
    later_within = jnp.flip(jnp.cumsum(jnp.flip(halves, axis=2), axis=2), axis=2)
    placing = (slot_ids[None, :] == own_ids[:, None]).astype(jnp.float32)
    placed = jnp.sum(later_within[:, :, 0][:, :, None] * placing[None, :, :], axis=1)
    every_total = lax.psum(placed, ("inner", "outer"))
    beyond = (slot_ids[None, :] > own_ids[:, None]).astype(jnp.float32)
    offsets = jnp.sum(beyond[None, :, :] * every_total[:, None, :], axis=2)
    forget_grad = (offsets[:, :, None] + later_within).reshape(head_count, row_count)
    return (
        query_acc.astype(jnp.bfloat16),
        key_acc.astype(jnp.bfloat16),
        value_acc.astype(jnp.bfloat16),
        forget_grad,
    )


def solution(mesh):
    placed = (
        P("head", ("inner", "outer"), None),
        P("head", ("inner", "outer"), None),
        P("head", ("inner", "outer"), None),
        P("head", ("inner", "outer"), None),
        P("head", ("inner", "outer")),
        P(),
    )
    return jax.shard_map(
        local,
        mesh=mesh,
        in_specs=placed,
        out_specs=(
            P("head", ("inner", "outer"), None),
            P("head", ("inner", "outer"), None),
            P("head", ("inner", "outer"), None),
            P("head", ("inner", "outer")),
        ),
        check_vma=False,
    )
```

profile of v0, /device:TPU:1, one launch (start us, length us, event | category | flops | bytes accessed | tf_op | source)
XLA Modules:
  0.0 846.8 jit_solution(15471067687946854950)
XLA Ops:
  10.0 48.4 %all_gather.24 = f32[1,16384]{1,0:T(1,128)S(1)} all-gather(f32[1,256]{1,0:T(1,128)} %param.16), channel_id=1, replica_groups=mesh['inner'=16,'outer'=4,'head'=4] {'inner','outer'}, dimensions={1}, use_global_device_ids=true | all-gather | bytes 66560 | tf_op jit(solution)/shard_map/all_gather | solution.py:77
  61.5 32.6 %all-gather.5.cloned.1.call-done = bf16[1,16384,128]{2,1,0:T(8,128)(2,1)} async-done(((bf16[1,256,128]{2,1,0:T(8,128)(2,1)}), bf16[1,16384,128]{2,1,0:T(8,128)(2,1)}) %all-gather.5.cloned.1.call-update) | async-done | bytes 4194320 | tf_op jit(solution)/shard_map/all_gather | solution.py:151
  94.1 79.1 %all-gather.7.cloned.1.call-done = bf16[1,16384,128]{2,1,0:T(8,128)(2,1)} async-done(((bf16[1,256,128]{2,1,0:T(8,128)(2,1)}), bf16[1,16384,128]{2,1,0:T(8,128)(2,1)}) %all-gather.7.cloned.1.call-update) | async-done | bytes 4194320 | tf_op jit(solution)/shard_map/all_gather | solution.py:152
  173.2 125.8 %while.41 = (s32[]{:T(128)}, f32[1,256]{1,0:T(1,128)S(1)}, f32[1,256]{1,0:T(1,128)S(1)}, f32[1,256]{1,0:T(1,128)S(1)}, s32[32]{0:T(128)S(1)}, /*index=5*/s32[163...) while((s32[]{:T(128)}, f32[1,256]{1,0:T(1,128)S(1)}, ...), condition=%wide.region_6.7_spmd.clone, body=%wide.region_2.6_spmd.clone.sunk | while | flops 69076736 | bytes 2005242 | solution.py:38
  299.0 42.4 %all_gather.27 = f32[1,16384]{1,0:T(1,128)S(1)} all-gather(f32[1,256]{1,0:T(1,128)S(1)} %get-tuple-element.777), channel_id=1, replica_groups=mesh['inner'=16,'outer'=4,'head'=4] {'inner','outer'}, dimensions={1}, use_global_device_ids=true | all-gather | bytes 66560 | tf_op jit(solution)/shard_map/all_gather | solution.py:118
  341.5 41.7 %all_gather.29 = f32[1,16384]{1,0:T(1,128)S(1)} all-gather(f32[1,256]{1,0:T(1,128)S(1)} %get-tuple-element.780), channel_id=1, replica_groups=mesh['inner'=16,'outer'=4,'head'=4] {'inner','outer'}, dimensions={1}, use_global_device_ids=true | all-gather | bytes 66560 | tf_op jit(solution)/shard_map/all_gather | solution.py:119
  383.2 200.1 %while.43 = (s32[]{:T(128)}, f32[1,256,128]{2,1,0:T(8,128)S(1)}, f32[1,256,128]{2,1,0:T(8,128)S(1)}, f32[1,256]{1,0:T(1,128)S(1)}, s32[256]{0:T(256)S(1)}, /*ind...) while((s32[]{:T(128)}, f32[1,256,128]{2,1,0:T(8,128)S(1)}, ...), condition=%wide.region_11.12_spmd.clone, body=%wide.region_9.11_spmd.clone.sunk | while | flops 135823616 | bytes 3307799 | solution.py:38
  584.0 129.9 %while.42 = (s32[]{:T(128)}, f32[1,256,128]{2,1,0:T(8,128)S(1)}, s32[32]{0:T(128)S(1)}, s32[16384]{0:T(1024)S(1)}, s32[256]{0:T(256)S(1)}, /*index=5*/bf16[1,163...) while((s32[]{:T(128)}, f32[1,256,128]{2,1,0:T(8,128)S(1)}, ...), condition=%wide.region_8.9_spmd.clone, body=%wide.region_7.8_spmd.clone.sunk | while | flops 101941248 | bytes 1853172 | solution.py:38
  586.5 1.6 fusion.124
  594.6 1.6 fusion.124
  598.7 1.6 fusion.124
  602.8 1.6 fusion.124
  606.8 1.6 fusion.124
  610.9 1.6 fusion.124
  614.9 1.6 fusion.124
  619.0 1.6 fusion.124
  623.1 1.6 fusion.124
  631.2 1.6 fusion.124
  651.5 1.6 fusion.124
  663.6 1.6 fusion.124
  683.9 1.6 fusion.124
  696.1 1.6 fusion.124
  708.3 1.6 fusion.124
  715.9 123.6 %psum.7 = f32[128]{0:T(128)S(1)} all-reduce(f32[128]{0:T(128)S(1)} %fusion.82), channel_id=1, replica_groups=mesh['inner'=16,'outer'=4,'head'=4] {'inner','outer'}, use_global_device_ids=true, to_apply=%region_14.15 | all-reduce | flops 128 | bytes 1024 | tf_op jit(solution)/shard_map/psum | solution.py:207
  (772 shorter events, 374.0 us)
Async XLA Ops:
  7.2 86.9 %all-gather.5.cloned.1.call-start = ((), (), s32[]{:S(2)}) async-start(), calls=%async_computation | async-start | bytes 4259840 | tf_op jit(solution)/shard_map/all_gather | solution.py:151
  7.9 165.3 %all-gather.7.cloned.1.call-start = ((), (), s32[]{:S(2)}) async-start(), calls=%async_computation.1 | async-start | bytes 4259840 | tf_op jit(solution)/shard_map/all_gather | solution.py:152
  8.6 374.5 %all-gather.9.cloned.1.call-start = ((), (), s32[]{:S(2)}) async-start(), calls=%async_computation.2 | async-start | bytes 4259840 | tf_op jit(solution)/shard_map/all_gather | solution.py:196
  9.4 373.8 %all-gather.11.cloned.1.call-start = ((), (), s32[]{:S(2)}) async-start(), calls=%async_computation.3 | async-start | bytes 4259840 | tf_op jit(solution)/shard_map/all_gather | solution.py:197
  173.2 210.0 %copy-start = (bf16[1,256,128]{2,1,0:T(8,128)(2,1)S(1)}, bf16[1,256,128]{2,1,0:T(8,128)(2,1)}, u32[]{:S(2)}) copy-start(bf16[1,256,128]{2,1,0:T(8,128)(2,1)} %param.14) | copy-start | bytes 196612
  173.2 210.0 %copy-start.2 = (bf16[1,256,128]{2,1,0:T(8,128)(2,1)S(1)}, bf16[1,256,128]{2,1,0:T(8,128)(2,1)}, u32[]{:S(2)}) copy-start(bf16[1,256,128]{2,1,0:T(8,128)(2,1)} %param.13) | copy-start | bytes 196612
  383.2 200.8 %copy-start.1 = (bf16[1,256,128]{2,1,0:T(8,128)(2,1)S(1)}, bf16[1,256,128]{2,1,0:T(8,128)(2,1)}, u32[]{:S(2)}) copy-start(bf16[1,256,128]{2,1,0:T(8,128)(2,1)} %get-tuple-element.884) | copy-start | bytes 196612
  383.2 200.8 %copy-start.3 = (bf16[1,256,128]{2,1,0:T(8,128)(2,1)S(1)}, bf16[1,256,128]{2,1,0:T(8,128)(2,1)}, u32[]{:S(2)}) copy-start(bf16[1,256,128]{2,1,0:T(8,128)(2,1)} %get-tuple-element.897) | copy-start | bytes 196612
Sparse Core Ops, SparseCore 0:
  10.8 83.2 all-gather.4
  96.8 76.2 all-gather.6
  175.9 76.3 all-gather.8
  254.9 76.4 all-gather.10
where the time goes:
time: 854 us; the launch traced here: 847 us
  matrix products  317 us (37%)
  blocking collectives  256 us (30%)
  waiting for transfers between devices  114 us (13%)
  loops' own time  67.7 us (8%)
  local copies, waits for them, and re-layouts  66.5 us (8%)
  between operations  14 us (2%)
  other arithmetic  11 us (1%)
    psum x1, blocking collectives, local(): every_total = lax.psum(placed, ('inner', 'outer'))  124 us
    all_gather x1, waiting for transfers between devices, local(): lax.all_gather(value_vectors, ('inner', 'outer'), axis=1, tiled=True)  79.1 us
    dot_general x64, matrix products, scores_and_mask(): jnp.einsum('hqd,hkd->hqk', query_matrix, key_rows, preferred_element_type...  77 us
    dot_general x64, matrix products, score_grads(): jnp.einsum('hqd,hkd->hqk', grad_rows, value_rows, preferred_element_type=...  74.5 us
    another operation x3, loops' own time, in_blocks(): lax.scan(single_block, carry, jnp.arange(piece_rows // block_rows, dtype=...  67.7 us
    dynamic_slice x96, local copies, waits for them, and re-layouts, in_blocks(): lax.scan(single_block, carry, jnp.arange(piece_rows // block_rows, dtype=...  56.3 us
    dot_general x32, matrix products, query_step(): jnp.einsum('hqk,hkd->hqd', score_grad.astype(jnp.bfloat16), key_rows, pre...  49.7 us
    all_gather x1, blocking collectives, local(): lax.all_gather(log_forget, ('inner', 'outer'), axis=1, tiled=True)  48.4 us
  transfers between devices with their start and end apart: 4, of which 2 were waited for; matrix products, arithmetic and copies ran while one was open for 13% of the time, Pallas kernels for 0%

commit v1 on v0

v1 whole, which is shorter than its diff:
```python
import math

import jax
import jax.numpy as jnp
from jax import lax
from jax.experimental import pallas as pl
from jax.experimental.pallas import tpu as pltpu
from jax.sharding import Mesh, PartitionSpec as P

F32 = jnp.float32
BF16 = jnp.bfloat16
LOG2E = 1.4426950408889634
NEG = -1e30
GROUP = 8
HALF = 128
ROWS = 256
AUX = 16
PACK = ROWS + AUX
NEAR = (0, 1, -1, 2, -2, 3, -3, 4)
Z, Y, C = "z", ("y_hi", "y_lo"), "core"
COLUMN = ("y_hi", "y_lo", "core")
VMEM_LIMIT = 48 * 1024 * 1024
vmem = pl.BlockSpec(memory_space=pltpu.VMEM)
smem = pl.BlockSpec(memory_space=pltpu.SMEM)
hbm = pl.BlockSpec(memory_space=pl.ANY)


def call(kernel, outs, in_specs, scratch=(), flops=0):
    return pl.pallas_call(
        kernel,
        out_shape=outs,
        in_specs=in_specs,
        out_specs=jax.tree.map(lambda _: vmem, outs),
        scratch_shapes=list(scratch),
        compiler_params=pltpu.CompilerParams(vmem_limit_bytes=VMEM_LIMIT),
        cost_estimate=pl.CostEstimate(flops=flops, bytes_accessed=4 << 20, transcendentals=0),
    )


def dot(a, b, ca, cb):
    return lax.dot_general(a, b, (((ca,), (cb,)), ((), ())), preferred_element_type=F32)


def split_rows(row, first=0):
    high = row.astype(BF16).astype(F32)
    middle = (row - high).astype(BF16).astype(F32)
    low = row - high - middle
    at = lax.broadcasted_iota(jnp.int32, (AUX, row.shape[1]), 0) - first
    return jnp.where(at == 0, high, jnp.where(at == 1, middle, jnp.where(at == 2, low, 0.0)))


def join_rows(rows, first=0):
    rows = rows.astype(F32)
    return rows[first : first + 1] + rows[first + 1 : first + 2] + rows[first + 2 : first + 3]


def running_sum(row):
    lane = lax.broadcasted_iota(jnp.int32, row.shape, 1)
    step = 1
    while step < HALF:
        row = row + jnp.where(lane >= step, pltpu.roll(row, step, 1), 0.0)
        step *= 2
    return row


def pack_kernel(swap_ref, q_ref, k_ref, v_ref, g_ref, f_ref, qg_ref, kv_ref):
    swap = swap_ref[0]
    for half in range(2):
        source = pl.ds(pl.multiple_of(HALF * (half ^ swap), HALF), HALF)
        target = pl.ds(HALF * half, HALF)
        qg_ref[target, 0:HALF] = q_ref[source, :]
        qg_ref[target, HALF:ROWS] = g_ref[source, :]
        kv_ref[target, 0:HALF] = k_ref[source, :]
        kv_ref[target, HALF:ROWS] = v_ref[source, :]
    gates = [f_ref[0:1, 0:HALF], f_ref[0:1, HALF:ROWS]]
    for half in range(2):
        gate = jnp.where(swap == 1, gates[1 - half], gates[half])
        rows = split_rows(running_sum(gate)).astype(BF16)
        qg_ref[ROWS:PACK, HALF * half : HALF * (half + 1)] = rows
        kv_ref[ROWS:PACK, HALF * half : HALF * (half + 1)] = rows


def totals_kernel(*refs):
    blocks, out_ref, aux, sems = refs[:8], refs[8], refs[9], refs[10]
    copies = []
    for at, block in enumerate(blocks):
        last = block.shape[0] - AUX
        copies.append(pltpu.make_async_copy(block.at[pl.ds(last, AUX), :], aux.at[at], sems.at[at]))
    for copy in copies:
        copy.start()
    lane = lax.broadcasted_iota(jnp.int32, (1, HALF), 1)
    total = jnp.zeros((1, HALF), F32)
    for at, copy in enumerate(copies):
        copy.wait()
        row = join_rows(aux[at])
        for half in range(2):
            value = row[:, HALF * (half + 1) - 1 : HALF * (half + 1)]
            total = jnp.where(lane == 2 * at + half, value, total)
    out_ref[...] = total


def load_blocks(index_ref, query_refs, key_refs, qs, ks, sems):
    copies = []

    def add(source, target):
        copies.append(pltpu.make_async_copy(source, target, sems.at[len(copies)]))

    for at, ref in enumerate(query_refs):
        add(ref, qs.at[index_ref[16 + at]])
    for at, ref in enumerate(key_refs[:7]):
        add(ref, ks.at[at])
    add(key_refs[7], ks.at[7, pl.ds(HALF, HALF + AUX), :])
    add(key_refs[8], ks.at[7, pl.ds(0, HALF), :])
    for copy in copies:
        copy.start()
    for copy in copies:
        copy.wait()


def span_gates(qs, wq):
    for d in range(GROUP):
        row = join_rows(qs[d, ROWS:PACK, :]) * LOG2E
        wq[0, d : d + 1, :] = row[:, 0:HALF]
        wq[1, d : d + 1, :] = row[:, HALF:ROWS]


def gate_columns(ks, e, columns):
    row = join_rows(ks[e, ROWS:PACK, :]) * LOG2E
    for half in range(2):
        part = row[:, HALF * half : HALF * (half + 1)]
        columns[half] = jnp.transpose(jnp.broadcast_to(part, (HALF, HALF)))


def half_rows(half):
    return pl.ds(pl.multiple_of(HALF * half, HALF), HALF)


def stats_kernel(scale, index_ref, *refs):
    query_refs, key_refs = refs[:8], refs[8:17]
    one_ref, two_ref, own_ref = refs[17:20]
    qs, ks, wq, columns, sems = refs[20:]
    load_blocks(index_ref, query_refs, key_refs, qs, ks, sems)
    span_gates(qs, wq)
    own = index_ref[24]
    ahead = lax.broadcasted_iota(jnp.int32, (HALF, HALF), 0) - lax.broadcasted_iota(
        jnp.int32, (HALF, HALF), 1
    )

    def tile_stats(scores, upstream):
        best = jnp.max(scores, axis=0, keepdims=True)
        factor = jnp.exp2(scores - best)
        return (
            best,
            jnp.sum(factor, axis=0, keepdims=True),
            jnp.sum(factor * upstream, axis=0, keepdims=True),
        )

    def key_block(e, carry):
        gate_columns(ks, e, columns)
        key_low, value_low = ks[e, 0:HALF, 0:HALF], ks[e, 0:HALF, HALF:ROWS]
        column = columns[0]
        for pair in range(GROUP // 2):
            q = jnp.concatenate([qs[2 * pair + i, HALF:ROWS, 0:HALF] for i in range(2)], 0)
            g = jnp.concatenate([qs[2 * pair + i, HALF:ROWS, HALF:ROWS] for i in range(2)], 0)
            w = jnp.concatenate([wq[1, 2 * pair + i : 2 * pair + i + 1, :] for i in range(2)], 1)
            column2 = jnp.concatenate([column, column], 1)
            scores = dot(key_low, q, 1, 1) * scale + (w - column2)
            upstream = dot(value_low, g, 1, 1)
            for at, row in enumerate(tile_stats(scores, upstream)):
                one_ref[e, at : at + 1, pl.ds(2 * HALF * pair, 2 * HALF)] = row
        for d in range(GROUP):
            half = (index_ref[8 + e] > index_ref[d]).astype(jnp.int32)
            rows = half_rows(half)
            limit = jnp.where((e == 0) & (own == d), 0, HALF)
            scores = dot(ks[e, rows, 0:HALF], qs[d, rows, 0:HALF], 1, 1) * scale + (
                wq[half, d : d + 1, :] - columns[half]
            )
            scores = jnp.where(ahead <= limit, scores, NEG)
            upstream = dot(ks[e, rows, HALF:ROWS], qs[d, rows, HALF:ROWS], 1, 1)
            for at, row in enumerate(tile_stats(scores, upstream)):
                two_ref[e, at : at + 1, pl.ds(HALF * d, HALF)] = row
        return carry

    lax.fori_loop(0, GROUP, key_block, 0)
    gate_columns(ks, 0, columns)
    w = wq[1, pl.ds(own, 1), :]
    scores = dot(ks[0, HALF:ROWS, 0:HALF], qs[own, HALF:ROWS, 0:HALF], 1, 1) * scale + (
        w - columns[1]
    )
    scores = jnp.where(ahead <= 0, scores, NEG)
    upstream = dot(ks[0, HALF:ROWS, HALF:ROWS], qs[own, HALF:ROWS, HALF:ROWS], 1, 1)
    for at, row in enumerate(tile_stats(scores, upstream)):
        own_ref[at : at + 1, :] = row


def merge_kernel(
    index_ref, spans_ref, ids_ref, t0, t1, t2, t3, one_ref, two_ref, own_ref, out_ref, place_ref
):
    own = index_ref[24]
    ids = ids_ref[...]
    totals = jnp.concatenate([t0[...], t1[...], t2[...], t3[...]], 0)
    places = []
    for at in range(4 * GROUP):
        before = jnp.where((ids >= 0) & (ids < spans_ref[at]), totals, 0.0)
        place = jnp.sum(jnp.sum(before, axis=0, keepdims=True), axis=1, keepdims=True) * LOG2E
        places.append(jnp.broadcast_to(place, (1, HALF)))
        place_ref[at : at + 1, :] = places[-1]
    key_low = jnp.concatenate(places[0:8], 0)
    key_high = jnp.concatenate(places[8:16], 0)
    sub = lax.broadcasted_iota(jnp.int32, (GROUP, HALF), 0)
    key_rank = jnp.zeros((GROUP, HALF), jnp.int32)
    for e in range(GROUP):
        key_rank = jnp.where(sub == e, index_ref[8 + e], key_rank)

    def finish(best, total, weighted, at, d):
        some = total > 0.0
        safe = jnp.where(some, total, 1.0)
        lse = jnp.where(some, best + jnp.log2(safe), NEG)
        delta = jnp.where(some, weighted / safe, 0.0)
        for copy in range(GROUP):
            out_ref[copy, at + d : at + d + 1, :] = lse
            out_ref[copy, at + 8 + d : at + 9 + d, :] = delta

    def down(x):
        return jnp.sum(x, axis=0, keepdims=True)

    for d in range(GROUP):
        lanes = slice(HALF * d, HALF * (d + 1))
        high = key_rank > index_ref[d]
        query_low, query_high = places[16 + d], places[24 + d]
        first = one_ref[:, 0, lanes] + (query_high - key_low)
        second = two_ref[:, 0, lanes] + jnp.where(high, query_high - key_high, query_low - key_low)
        mine = own == d
        third = jnp.where(mine, own_ref[0:1, :], NEG)
        best = jnp.maximum(
            jnp.max(jnp.maximum(first, jnp.where(high, second, NEG)), axis=0, keepdims=True), third
        )
        first_weight = jnp.exp2(first - best)
        second_weight = jnp.where(high, jnp.exp2(second - best), 0.0)
        third_weight = jnp.where(mine, jnp.exp2(third - best), 0.0)
        sums = [
            down(one_ref[:, at, lanes] * first_weight + two_ref[:, at, lanes] * second_weight)
            + own_ref[at : at + 1, :] * third_weight
            for at in (1, 2)
        ]
        finish(best, sums[0], sums[1], 0, d)
        low = jnp.where(high, NEG, second)
        best = jnp.max(low, axis=0, keepdims=True)
        weight = jnp.where(high, 0.0, jnp.exp2(low - best))
        sums = [down(two_ref[:, at, lanes] * weight) for at in (1, 2)]
        finish(best, sums[0], sums[1], 16, d)


def grads_kernel(scale, index_ref, stats_ref, place_ref, *refs):
    query_refs, key_refs = refs[:8], refs[8:17]
    dq_ref, dkv_ref, aux_ref = refs[17:20]
    qs, ks, wq, columns, delta, dqt, dk, dv, pg, totals, sems = refs[20:]
    load_blocks(index_ref, query_refs, key_refs, qs, ks, sems)
    span_gates(qs, wq)
    own = index_ref[24]
    ahead = lax.broadcasted_iota(jnp.int32, (HALF, HALF), 0) - lax.broadcasted_iota(
        jnp.int32, (HALF, HALF), 1
    )
    for half, at in ((1, 0), (0, 16)):
        lse = [stats_ref[b, at : at + 8, :] for b in range(GROUP)]
        best = lse[0]
        for b in range(1, GROUP):
            best = jnp.maximum(best, lse[b])
        total = jnp.zeros((GROUP, HALF), F32)
        weighted = jnp.zeros((GROUP, HALF), F32)
        for b in range(GROUP):
            weight = jnp.exp2(lse[b] - best)
            total = total + weight
            weighted = weighted + weight * stats_ref[b, at + 8 : at + 16, :]
        wq[half] = wq[half] - (best + jnp.log2(total))
        delta[half] = weighted / total
    dqt[...] = jnp.zeros_like(dqt)
    totals[...] = jnp.zeros_like(totals)
    lane = lax.broadcasted_iota(jnp.int32, (1, HALF), 1)
    inverse = 1.0 / math.sqrt(HALF)

    def query_gate(half, d, key_place):
        place = place_ref[pl.ds(16 + 8 * half + d, 1), :]
        return wq[half, d : d + 1, :] + (place - key_place)

    def key_block(e, carry):
        gate_columns(ks, e, columns)
        dk[...] = jnp.zeros_like(dk)
        dv[...] = jnp.zeros_like(dv)
        pg[...] = jnp.zeros_like(pg)
        key_low, value_low = ks[e, 0:HALF, 0:HALF], ks[e, 0:HALF, HALF:ROWS]
        turned = jnp.transpose(key_low)
        column = columns[0]
        column2 = jnp.concatenate([column, column], 1)
        place = place_ref[pl.ds(e, 1), :]
        for pair in range(GROUP // 2):
            both = (2 * pair, 2 * pair + 1)
            q = jnp.concatenate([qs[d, HALF:ROWS, 0:HALF] for d in both], 0)
            g = jnp.concatenate([qs[d, HALF:ROWS, HALF:ROWS] for d in both], 0)
            w = jnp.concatenate([query_gate(1, d, place) for d in both], 1)
            shift = jnp.concatenate([delta[1, d : d + 1, :] for d in both], 1)
            probs = jnp.exp2(dot(key_low, q, 1, 1) * scale + (w - column2))
            grads = probs * (dot(value_low, g, 1, 1) - shift)
            low_grads = grads.astype(BF16)
            dv[0] += dot(probs.astype(BF16), g, 1, 0)
            dk[0] += dot(low_grads, q, 1, 0)
            part = dot(turned, low_grads, 1, 0)
            dqt[1, both[0]] += part[:, 0:HALF]
            dqt[1, both[1]] += part[:, HALF:ROWS]
            pg[0] += grads[:, 0:HALF] + grads[:, HALF:ROWS]

        def tile(rows, half, d, limit):
            k, v = ks[e, rows, 0:HALF], ks[e, rows, HALF:ROWS]
            q, g = qs[d, rows, 0:HALF], qs[d, rows, HALF:ROWS]
            w = query_gate(half, d, place_ref[pl.ds(8 * half + e, 1), :])
            scores = dot(k, q, 1, 1) * scale + (w - columns[half])
            probs = jnp.where(ahead <= limit, jnp.exp2(scores), 0.0)
            grads = probs * (dot(v, g, 1, 1) - delta[half, pl.ds(d, 1), :])
            low_grads = grads.astype(BF16)
            dv[half] += dot(probs.astype(BF16), g, 1, 0)
            dk[half] += dot(low_grads, q, 1, 0)
            dqt[half, d] += dot(k, low_grads, 0, 0)
            pg[half] += grads

        for d in range(GROUP):
            half = (index_ref[8 + e] > index_ref[d]).astype(jnp.int32)
            tile(half_rows(half), half, d, jnp.where((e == 0) & (own == d), 0, HALF))

        @pl.when(e == 0)
        def _():
            k, v = ks[e, HALF:ROWS, 0:HALF], ks[e, HALF:ROWS, HALF:ROWS]
            q, g = qs[own, HALF:ROWS, 0:HALF], qs[own, HALF:ROWS, HALF:ROWS]
            scores = dot(k, q, 1, 1) * scale + (wq[1, pl.ds(own, 1), :] - columns[1])
            probs = jnp.where(ahead <= 0, jnp.exp2(scores), 0.0)
            grads = probs * (dot(v, g, 1, 1) - delta[1, pl.ds(own, 1), :])
            low_grads = grads.astype(BF16)
            dv[1] += dot(probs.astype(BF16), g, 1, 0)
            dk[1] += dot(low_grads, q, 1, 0)
            dqt[1, own] += dot(k, low_grads, 0, 0)
            pg[1] += grads

        slot = index_ref[25 + e]
        for half in range(2):
            rows = slice(HALF * half, HALF * (half + 1))
            dkv_ref[slot, rows, 0:HALF] = (dk[half] * inverse).astype(BF16)
            dkv_ref[slot, rows, HALF:ROWS] = dv[half].astype(BF16)
            row = -jnp.sum(jnp.transpose(pg[half]), axis=0, keepdims=True)
            aux_ref[slot, :, rows] = split_rows(row)
            total = jnp.sum(row, axis=1, keepdims=True)
            totals[...] = jnp.where(lane == 2 * e + half, total, totals[...])
        return carry

    lax.fori_loop(0, GROUP, key_block, 0)
    rows = split_rows(totals[...]).astype(BF16)
    for d in range(GROUP):
        for half in range(2):
            part = jnp.transpose(dqt[half, d]) * inverse
            dq_ref[d, HALF * half : HALF * (half + 1), :] = part.astype(BF16)
        dq_ref[d, ROWS:PACK, :] = rows


def query_kernel(index_ref, spans_ref, ids_ref, parts_ref, aux_ref, dq_ref, out_ref):
    swap = index_ref[33]
    for half in range(2):
        rows = slice(HALF * half, HALF * (half + 1))
        total = parts_ref[0, rows, :].astype(F32)
        for b in range(1, GROUP):
            total = total + parts_ref[b, rows, :].astype(F32)
        dq_ref[half_rows(half ^ swap), :] = total.astype(BF16)
    totals = jnp.concatenate([join_rows(parts_ref[b, ROWS:PACK, :]) for b in range(GROUP)], 0)
    ids = ids_ref[...]
    for e in range(GROUP):
        slot = index_ref[25 + e]
        for half in range(2):
            lanes = slice(HALF * half, HALF * (half + 1))
            beyond = jnp.where(ids > spans_ref[8 * half + e], totals, 0.0)
            value = jnp.sum(jnp.sum(beyond, axis=0, keepdims=True), axis=1, keepdims=True)
            row = jnp.broadcast_to(value, (1, HALF))
            out_ref[slot, :, lanes] = (aux_ref[slot, :, lanes] + split_rows(row, 3)).astype(BF16)


def key_kernel(index_ref, parts_ref, dk_ref, dv_ref, f_ref):
    swap = index_ref[33]
    for half in range(2):
        rows = slice(HALF * half, HALF * (half + 1))
        total = parts_ref[0, rows, :].astype(F32)
        for z in range(1, GROUP):
            total = total + parts_ref[z, rows, :].astype(F32)
        total = total.astype(BF16)
        dk_ref[half_rows(half ^ swap), :] = total[:, 0:HALF]
        dv_ref[half_rows(half ^ swap), :] = total[:, HALF:ROWS]
    aux = parts_ref[0, ROWS:PACK, :].astype(F32)
    for z in range(1, GROUP):
        aux = aux + parts_ref[z, ROWS:PACK, :].astype(F32)
    halves = []
    for half in range(2):
        lanes = slice(HALF * half, HALF * (half + 1))
        row = join_rows(aux[:, lanes])
        total = jnp.sum(row, axis=1, keepdims=True)
        halves.append(total - running_sum(row) + row + join_rows(aux[:, lanes], 3))
    for half in range(2):
        lanes = slice(HALF * half, HALF * (half + 1))
        f_ref[:, lanes] = jnp.where(swap == 1, halves[1 - half], halves[half])


def fetch(x, axis, size, offset):
    return lax.ppermute(x, axis, [((i + offset) % size, i) for i in range(size)])


def local(queries, key_vectors, value_vectors, out_grad, log_forget, span_order):
    scale = LOG2E / math.sqrt(HALF)
    z, y, core = lax.axis_index(Z), lax.axis_index(Y), lax.axis_index(C)
    column = y * 2 + core
    pairs = span_order.reshape(64, 2)
    lows, highs = jnp.min(pairs, axis=1), jnp.max(pairs, axis=1)
    swaps = (pairs[:, 0] > pairs[:, 1]).astype(jnp.int32)
    device = jnp.arange(64, dtype=jnp.int32)

    def pick(table, which):
        match = which[..., None] == device
        return jnp.sum(jnp.where(match, table, 0), axis=-1)

    near = jnp.array(NEAR, jnp.int32)
    z_slots = (z + near) % GROUP
    y_order = (y + jnp.array([0, 1, -1, 2], jnp.int32)) % 4
    core_order = jnp.stack([core, 1 - core])
    columns = y_order[:, None] * 2 + core_order[None, :]
    every = jnp.arange(GROUP, dtype=jnp.int32)
    query_devices, key_devices = z * GROUP + every, z_slots * GROUP + column
    swap = pick(swaps, z * GROUP + column)[None]
    index = jnp.concatenate(
        [
            pick(lows, query_devices),
            pick(lows, key_devices),
            columns.T.reshape(GROUP),
            column[None],
            z_slots,
            swap,
        ]
    ).astype(jnp.int32)
    spans = jnp.concatenate(
        [pick(t, which) for which in (key_devices, query_devices) for t in (lows, highs)]
    )

    def span_ids(order):
        which = z_slots[None, :] * GROUP + order[:, None]
        ids = jnp.stack([pick(lows, which), pick(highs, which)], axis=2).reshape(GROUP, 16)
        return jnp.pad(ids, ((0, 0), (0, HALF - 16)), constant_values=-1)

    near_ids, every_ids = span_ids(columns.reshape(GROUP)), span_ids(every)

    packed = jax.ShapeDtypeStruct((PACK, ROWS), BF16)
    qg, kv = call(pack_kernel, (packed, packed), [smem] + [vmem] * 5)(
        swap, queries[0], key_vectors[0], value_vectors[0], out_grad[0], log_forget
    )
    up1, down1, up2, down2 = [fetch(kv, Z, 8, o) for o in (1, -1, 2, -2)]
    mine = [qg] + [fetch(qg, Y, 4, o) for o in (1, -1, 2)]
    up3, down3 = fetch(up2, Z, 8, 1), fetch(down2, Z, 8, -1)
    across = [fetch(block, C, 2, 1) for block in mine]
    far_low = fetch(down2[:HALF], Z, 8, -2)
    far_high = fetch(up2[HALF:], Z, 8, 2)
    query_blocks = mine + across
    key_blocks = [kv, up1, down1, up2, down2, up3, down3, far_high, far_low]

    total = call(
        totals_kernel,
        jax.ShapeDtypeStruct((1, HALF), F32),
        [hbm] * 8,
        [pltpu.VMEM((8, AUX, ROWS), BF16), pltpu.SemaphoreType.DMA((8,))],
    )(*key_blocks[:8])
    chip_totals = jnp.concatenate([total, fetch(total, C, 2, 1)], 0)
    totals = [chip_totals] + [fetch(chip_totals, Y, 4, o) for o in (1, -1, 2)]

    blocks = [
        pltpu.VMEM((GROUP, PACK, ROWS), BF16),
        pltpu.VMEM((GROUP, PACK, ROWS), BF16),
        pltpu.VMEM((2, GROUP, HALF), F32),
        pltpu.VMEM((2, HALF, HALF), F32),
    ]
    sems = pltpu.SemaphoreType.DMA((17,))
    tiles = jax.ShapeDtypeStruct((GROUP, 3, GROUP * HALF), F32)
    one, two, own = call(
        lambda *refs: stats_kernel(scale, *refs),
        (tiles, tiles, jax.ShapeDtypeStruct((GROUP, HALF), F32)),
        [smem] + [hbm] * 17,
        blocks + [sems],
        flops=1 << 31,
    )(index, *query_blocks, *key_blocks)
    stats, place = call(
        merge_kernel,
        (
            jax.ShapeDtypeStruct((GROUP, 32, HALF), F32),
            jax.ShapeDtypeStruct((32, HALF), F32),
        ),
        [smem, smem] + [vmem] * 8,
    )(index, spans, near_ids, *totals, one, two, own)
    stats = lax.all_to_all(stats, COLUMN, 0, 0, tiled=True)
    dq_parts, dkv_parts, aux = call(
        lambda *refs: grads_kernel(scale, *refs),
        (
            jax.ShapeDtypeStruct((GROUP, PACK, HALF), BF16),
            jax.ShapeDtypeStruct((GROUP, PACK, ROWS), BF16),
            jax.ShapeDtypeStruct((GROUP, AUX, ROWS), F32),
        ),
        [smem, vmem, vmem] + [hbm] * 17,
        blocks
        + [
            pltpu.VMEM((2, GROUP, HALF), F32),
            pltpu.VMEM((2, GROUP, HALF, HALF), F32),
            pltpu.VMEM((2, HALF, HALF), F32),
            pltpu.VMEM((2, HALF, HALF), F32),
            pltpu.VMEM((2, HALF, HALF), F32),
            pltpu.VMEM((1, HALF), F32),
            sems,
        ],
        flops=1 << 32,
    )(index, stats, place, *query_blocks, *key_blocks)
    dq_parts = lax.all_to_all(dq_parts, COLUMN, 0, 0, tiled=True)
    dq, aux = call(
        query_kernel,
        (
            jax.ShapeDtypeStruct((ROWS, HALF), BF16),
            jax.ShapeDtypeStruct((GROUP, AUX, ROWS), BF16),
        ),
        [smem, smem] + [vmem] * 3,
    )(index, spans, every_ids, dq_parts, aux)
    dkv_parts = lax.dynamic_update_slice(dkv_parts, aux, (0, ROWS, 0))
    dkv_parts = lax.all_to_all(dkv_parts, Z, 0, 0, tiled=True)
    rows = jax.ShapeDtypeStruct((ROWS, HALF), BF16)
    dk, dv, forget = call(
        key_kernel, (rows, rows, jax.ShapeDtypeStruct((1, ROWS), F32)), [smem, vmem]
    )(index, dkv_parts)
    return dq[None], dk[None], dv[None], forget


def solution(mesh):
    fine = Mesh(mesh.devices.reshape(8, 2, 2, 2, 4), ("z", "y_hi", "y_lo", "core", "head"))
    rows = ("z", "y_hi", "y_lo", "core")
    wide, thin = P("head", rows, None), P("head", rows)
    return jax.shard_map(
        local,
        mesh=fine,
        in_specs=(wide, wide, wide, wide, thin, P()),
        out_specs=(wide, wide, wide, thin),
        check_vma=False,
    )
```

time: 854 us -> 148 us (0.17)
  matrix products: 317 us -> 0 us
  blocking collectives: 256 us -> 42.2 us
  waiting for transfers between devices: 114 us -> 13.8 us
  loops' own time: 67.7 us -> 0 us
  local copies, waits for them, and re-layouts: 66.5 us -> 6.04 us
  Pallas kernels: 0 us -> 41.4 us
  starting transfers between devices: 0.15 us -> 38.7 us
  between operations: 14 us -> 0.81 us
    dot_general x256 -> x0, matrix products: 317 us -> none  [the longest x64 77 us: scores_and_mask(): jnp.einsum('hqd,hkd->hqk', query_matrix, key_rows, preferred_element_type...]
    all_gather x3 -> x0, blocking collectives: 133 us -> none  [the longest x1 48.4 us: local(): lax.all_gather(log_forget, ('inner', 'outer'), axis=1, tiled=True)]
    psum x1 -> x0, blocking collectives: 124 us -> none  [local(): every_total = lax.psum(placed, ('inner', 'outer'))]
    all_gather x4 -> x0, waiting for transfers between devices: 112 us -> none  [the longest x1 79.1 us: local(): lax.all_gather(value_vectors, ('inner', 'outer'), axis=1, tiled=True)]
    another operation x3 -> x0, loops' own time: 67.7 us -> none  [in_blocks(): lax.scan(single_block, carry, jnp.arange(piece_rows // block_rows, dtype=...]
    dynamic_slice x323 -> x0, local copies, waits for them, and re-layouts: 65.8 us -> none  [the longest x96 56.3 us: in_blocks(): lax.scan(single_block, carry, jnp.arange(piece_rows // block_rows, dtype=...]
    all_to_all x0 -> x2, blocking collectives: none -> 42.2 us  [the longest x1 33.5 us: local(): dkv_parts = lax.all_to_all(dkv_parts, Z, 0, 0, tiled=True)]
    pallas_call x0 -> x7, Pallas kernels: none -> 41.4 us  [the longest x1 25.8 us: local(): call(lambda *refs: grads_kernel(scale, *refs), (jax.ShapeDtypeStruct((GRO...]
  transfers between devices with their start and end apart: 4 -> 20, of which waited for: 2 -> 4; matrix products, arithmetic and copies ran while one was open for 13% -> 3% of each run, Pallas kernels for 0% -> 7%
where the time goes in v1:
time: 148 us; the launch traced here: 146 us
  blocking collectives  42.2 us (29%)
  Pallas kernels  41.4 us (28%)
  starting transfers between devices  38.7 us (26%)
  waiting for transfers between devices  13.8 us (9%)
  local copies, waits for them, and re-layouts  6.04 us (4%)
  other arithmetic  3.54 us (2%)
    ppermute x19, starting transfers between devices, fetch(): lax.ppermute(x, axis, [((i + offset) % size, i) for i in range(size)])  34.4 us
    all_to_all x1, blocking collectives, local(): dkv_parts = lax.all_to_all(dkv_parts, Z, 0, 0, tiled=True)  33.5 us
    pallas_call x1, Pallas kernels, local(): call(lambda *refs: grads_kernel(scale, *refs), (jax.ShapeDtypeStruct((GRO...  25.8 us
    pallas_call x1, Pallas kernels, local(): call(lambda *refs: stats_kernel(scale, *refs), (tiles, tiles, jax.ShapeDt...  9.79 us
    all_to_all x1, waiting for transfers between devices, local(): dq_parts = lax.all_to_all(dq_parts, COLUMN, 0, 0, tiled=True)  9.69 us
    all_to_all x1, blocking collectives, local(): stats = lax.all_to_all(stats, COLUMN, 0, 0, tiled=True)  8.77 us
    all_to_all x1, starting transfers between devices, local(): dq_parts = lax.all_to_all(dq_parts, COLUMN, 0, 0, tiled=True)  4.33 us
    ppermute x19, waiting for transfers between devices, fetch(): lax.ppermute(x, axis, [((i + offset) % size, i) for i in range(size)])  4.12 us
  transfers between devices with their start and end apart: 20, of which 4 were waited for; matrix products, arithmetic and copies ran while one was open for 3% of the time, Pallas kernels for 7%

profile of v1, /device:TPU:1, one launch (start us, length us, event | category | flops | bytes accessed | tf_op | source)
XLA Modules:
  0.0 146.5 jit_solution(16013424268125446574)
XLA Ops:
  2.3 0.8 copy-done
  3.1 0.8 copy-done.1
  6.3 1.1 shard_map.111
  7.4 3.8 %collective-permute-start.13 = (bf16[272,256]{1,0:T(8,128)(2,1)S(1)}, bf16[272,256]{1,0:T(8,128)(2,1)S(1)}, u32[]{:S(2)}, u32[]{:S(2)}) collective-permute-start(bf16[272,256]{1,0:T(8,128)(2,1)S(1)} %get-tuple-element.20.refs_1_.refs_3_), channel_id=1, source_target_pairs={{16,0},{24,8},{0,16},{8,24},{17,1},{25,9},{1,17},{9,25},{18,2},{26... | collective-permute-start | bytes 417800 | tf_op jit(solution)/shard_map/ppermute | solution.py:407
  11.7 2.3 %collective-permute-start.11 = (bf16[272,256]{1,0:T(8,128)(2,1)S(1)}, bf16[272,256]{1,0:T(8,128)(2,1)S(1)}, u32[]{:S(2)}, u32[]{:S(2)}) collective-permute-start(bf16[272,256]{1,0:T(8,128)(2,1)S(1)} %get-tuple-element.20.refs_1_.refs_3_), channel_id=1, source_target_pairs={{8,0},{16,8},{24,16},{0,24},{9,1},{17,9},{25,17},{1,25},{10,2},{18... | collective-permute-start | bytes 417800 | tf_op jit(solution)/shard_map/ppermute | solution.py:407
  13.9 3.0 %collective-permute-start.3 = (bf16[272,256]{1,0:T(8,128)(2,1)S(1)}, bf16[272,256]{1,0:T(8,128)(2,1)S(1)}, u32[]{:S(2)}, u32[]{:S(2)}) collective-permute-start(bf16[272,256]{1,0:T(8,128)(2,1)S(1)} %get-tuple-element.19.refs_0_.refs_9_.refs_11_), channel_id=1, source_target_pairs={{192,0},{224,32},{0,64},{32,96},{64,128},{96,160},{128,192},{160,2... | collective-permute-start | bytes 417800 | tf_op jit(solution)/shard_map/ppermute | solution.py:407
  16.9 3.0 %collective-permute-start.2 = (bf16[272,256]{1,0:T(8,128)(2,1)S(1)}, bf16[272,256]{1,0:T(8,128)(2,1)S(1)}, u32[]{:S(2)}, u32[]{:S(2)}) collective-permute-start(bf16[272,256]{1,0:T(8,128)(2,1)S(1)} %get-tuple-element.19.refs_0_.refs_9_.refs_11_), channel_id=1, source_target_pairs={{64,0},{96,32},{128,64},{160,96},{192,128},{224,160},{0,192},{32,2... | collective-permute-start | bytes 417800 | tf_op jit(solution)/shard_map/ppermute | solution.py:407
  23.3 1.9 %collective-permute-start = (bf16[272,256]{1,0:T(8,128)(2,1)S(1)}, bf16[272,256]{1,0:T(8,128)(2,1)S(1)}, u32[]{:S(2)}, u32[]{:S(2)}) collective-permute-start(bf16[272,256]{1,0:T(8,128)(2,1)S(1)} %get-tuple-element.19.refs_0_.refs_9_.refs_11_), channel_id=1, source_target_pairs={{32,0},{64,32},{96,64},{128,96},{160,128},{192,160},{224,192},{0,2... | collective-permute-start | bytes 417800 | tf_op jit(solution)/shard_map/ppermute | solution.py:407
  25.3 2.0 %collective-permute-start.5 = (bf16[272,256]{1,0:T(8,128)(2,1)S(1)}, bf16[272,256]{1,0:T(8,128)(2,1)S(1)}, u32[]{:S(2)}, u32[]{:S(2)}) collective-permute-start(bf16[272,256]{1,0:T(8,128)(2,1)S(1)} %collective-permute-done.3.refs_4_.refs_13_.refs_15_), channel_id=1, source_target_pairs={{224,0},{0,32},{32,64},{64,96},{96,128},{128,160},{160,192},{192,2... | collective-permute-start | bytes 417800 | tf_op jit(solution)/shard_map/ppermute | solution.py:407
  28.7 1.3 collective-permute-start.6
  30.0 2.8 %collective-permute-start.14 = (bf16[272,256]{1,0:T(8,128)(2,1)S(1)}, bf16[272,256]{1,0:T(8,128)(2,1)S(1)}, u32[]{:S(2)}, u32[]{:S(2)}) collective-permute-start(bf16[272,256]{1,0:T(8,128)(2,1)S(1)} %get-tuple-element.20.refs_1_.refs_3_), channel_id=1, source_target_pairs={{4,0},{0,4},{5,1},{1,5},{6,2},{2,6},{7,3},{3,7},{12,8},{8,12},{13,... | collective-permute-start | bytes 417800 | tf_op jit(solution)/shard_map/ppermute | solution.py:407
  33.5 4.3 %collective-permute-start.16 = (bf16[272,256]{1,0:T(8,128)(2,1)S(1)}, bf16[272,256]{1,0:T(8,128)(2,1)S(1)}, u32[]{:S(2)}, u32[]{:S(2)}) collective-permute-start(bf16[272,256]{1,0:T(8,128)(2,1)S(1)} %collective-permute-done.12.refs_3_.refs_5_), channel_id=1, source_target_pairs={{4,0},{0,4},{5,1},{1,5},{6,2},{2,6},{7,3},{3,7},{12,8},{8,12},{13,... | collective-permute-start | bytes 417800 | tf_op jit(solution)/shard_map/ppermute | solution.py:407
  40.2 4.3 %collective-permute-start.18 = (bf16[128,256]{1,0:T(8,128)(2,1)S(1)}, bf16[128,256]{1,0:T(8,128)(2,1)S(1)}, u32[]{:S(2)}, u32[]{:S(2)}) collective-permute-start(bf16[128,256]{1,0:T(8,128)(2,1)S(1)} %slice.19), channel_id=1, source_target_pairs={{192,0},{224,32},{0,64},{32,96},{64,128},{96,160},{128,192},{160,2... | collective-permute-start | bytes 196616 | tf_op jit(solution)/shard_map/ppermute | solution.py:407
  44.8 3.1 %collective-permute-done.18.refs_17_.refs_19_ = bf16[128,256]{1,0:T(8,128)(2,1)S(1)} collective-permute-done((bf16[128,256]{1,0:T(8,128)(2,1)S(1)}, bf16[128,256]{1,0:T(8,128)(2,1)S(1)}, u32[]{:S(2)}, u32[]{:S(2)}) %collective-permute-start.18) | collective-permute-done | bytes 65568 | tf_op jit(solution)/shard_map/ppermute | solution.py:407
  47.9 2.7 %collective-permute-start.8 = (f32[2,128]{1,0:T(2,128)S(1)}, f32[2,128]{1,0:T(2,128)S(1)}, u32[]{:S(2)}, u32[]{:S(2)}) collective-permute-start(f32[2,128]{1,0:T(2,128)S(1)} %pad_maximum_fusion.t0), channel_id=1, source_target_pairs={{8,0},{16,8},{24,16},{0,24},{9,1},{17,9},{25,17},{1,25},{10,2},{18... | collective-permute-start | bytes 3080 | tf_op jit(solution)/shard_map/ppermute | solution.py:407
  50.6 9.8 %shard_map.113 = (f32[8,3,1024]{2,1,0:T(4,128)S(1)}, f32[8,3,1024]{2,1,0:T(4,128)S(1)}, f32[8,128]{1,0:T(8,128)S(1)}) custom-call(s32[34]{0:T(128)S(1)} %concatenate.9.refs_0_.index_ref, bf16[272,256]{1,0:T(8,128)(2,1)S(1)} %get-tuple-element.20.refs_1_.refs_3_, bf16[272,256]{1,0:T(8,128)(2,1)S(1)} %collective-permute-done.11.refs_2_.refs_4_, ...), custom_call_target="tpu_custom_call" | custom-call | flops 2147483648 | bytes 4194304 | tf_op jit(solution)/shard_map/pallas_call | solution.py:482
  60.4 0.9 shard_map.114
  61.3 8.8 %all_to_all.15.refs_1_ = f32[8,32,128]{2,1,0:T(8,128)S(1)} all-to-all(f32[8,32,128]{2,1,0:T(8,128)S(1)} %get-tuple-element.24), channel_id=1, replica_groups=mesh['z'=8,'y_hi'=2,'y_lo'=2,'core'=2,'head'=4] {'y_hi','y_lo','core'}, dimensions={0} | all-to-all | bytes 262144 | tf_op jit(solution)/shard_map/all_to_all | solution.py:497
  70.0 25.8 %shard_map.115 = (bf16[8,272,128]{2,1,0:T(8,128)(2,1)}, bf16[8,272,256]{2,1,0:T(8,128)(2,1)S(1)}, f32[8,16,256]{2,1,0:T(8,128)S(1)}) custom-call(s32[34]{0:T(128)S(1)} %concatenate.9.refs_0_.index_ref, f32[8,32,128]{2,1,0:T(8,128)S(1)} %all_to_all.15.refs_1_, f32[32,128]{1,0:T(8,128)S(1)} %get-tuple-element.25.refs_2_, ...), custom_call_target="tpu_custom_call" | custom-call | flops 4294967296 | bytes 4194304 | tf_op jit(solution)/shard_map/pallas_call | solution.py:498
  95.8 4.3 %all-to-all-start.1 = ((bf16[8,272,128]{2,1,0:T(8,128)(2,1)}), bf16[8,272,128]{2,1,0:T(8,128)(2,1)S(1)}, u32[]{:S(2)}, u32[]{:S(2)}) async-start(bf16[8,272,128]{2,1,0:T(8,128)(2,1)} %get-tuple-element.26), calls=%async_computation.1 | async-start | bytes 1114112 | tf_op jit(solution)/shard_map/all_to_all | solution.py:518
  100.3 9.7 %all-to-all-done.1.parts_ref = bf16[8,272,128]{2,1,0:T(8,128)(2,1)S(1)} async-done(((bf16[8,272,128]{2,1,0:T(8,128)(2,1)}), bf16[8,272,128]{2,1,0:T(8,128)(2,1)S(1)}, u32[]{:S(2)}, u32[]{:S(2)}) %all-to-all-start.1) | async-done | bytes 557088 | tf_op jit(solution)/shard_map/all_to_all | solution.py:518
  110.0 1.3 shard_map.116
  111.3 33.5 %all_to_all.16.parts_ref = bf16[8,272,256]{2,1,0:T(8,128)(2,1)S(1)} all-to-all(bf16[8,272,256]{2,1,0:T(8,128)(2,1)S(1)} %constant_dynamic-update-slice_fusion), channel_id=1, replica_groups=mesh['z'=8,'y_hi'=2,'y_lo'=2,'core'=2,'head'=4] {'z'}, dimensions={0} | all-to-all | bytes 2228224 | tf_op jit(solution)/shard_map/all_to_all | solution.py:528
  144.8 1.7 %shard_map.117 = (bf16[256,128]{1,0:T(8,128)(2,1)}, bf16[256,128]{1,0:T(8,128)(2,1)}, f32[1,256]{1,0:T(1,128)}) custom-call(s32[34]{0:T(128)S(1)} %concatenate.9.refs_0_.index_ref, bf16[8,272,256]{2,1,0:T(8,128)(2,1)S(1)} %all_to_all.16.parts_ref), custom_call_target="tpu_custom_call" | custom-call | bytes 4194304 | tf_op jit(solution)/shard_map/pallas_call | solution.py:530
  (64 shorter events, 12.6 us)
Async XLA Ops:
  2.3 0.8 copy-start
  3.1 0.8 copy-start.1
  3.9 0.8 copy-start.2
  4.8 0.8 copy-start.3
  7.4 15.1 %collective-permute-start.13 = (bf16[272,256]{1,0:T(8,128)(2,1)S(1)}, bf16[272,256]{1,0:T(8,128)(2,1)S(1)}, u32[]{:S(2)}, u32[]{:S(2)}) collective-permute-start(bf16[272,256]{1,0:T(8,128)(2,1)S(1)} %get-tuple-element.20.refs_1_.refs_3_), channel_id=1, source_target_pairs={{16,0},{24,8},{0,16},{8,24},{17,1},{25,9},{1,17},{9,25},{18,2},{26... | collective-permute-start | bytes 417800 | tf_op jit(solution)/shard_map/ppermute | solution.py:407
  11.3 12.0 %collective-permute-start.12 = (bf16[272,256]{1,0:T(8,128)(2,1)S(1)}, bf16[272,256]{1,0:T(8,128)(2,1)S(1)}, u32[]{:S(2)}, u32[]{:S(2)}) collective-permute-start(bf16[272,256]{1,0:T(8,128)(2,1)S(1)} %get-tuple-element.20.refs_1_.refs_3_), channel_id=1, source_target_pairs={{24,0},{0,8},{8,16},{16,24},{25,1},{1,9},{9,17},{17,25},{26,2},{2,... | collective-permute-start | bytes 417800 | tf_op jit(solution)/shard_map/ppermute | solution.py:407
  11.7 17.0 %collective-permute-start.11 = (bf16[272,256]{1,0:T(8,128)(2,1)S(1)}, bf16[272,256]{1,0:T(8,128)(2,1)S(1)}, u32[]{:S(2)}, u32[]{:S(2)}) collective-permute-start(bf16[272,256]{1,0:T(8,128)(2,1)S(1)} %get-tuple-element.20.refs_1_.refs_3_), channel_id=1, source_target_pairs={{8,0},{16,8},{24,16},{0,24},{9,1},{17,9},{25,17},{1,25},{10,2},{18... | collective-permute-start | bytes 417800 | tf_op jit(solution)/shard_map/ppermute | solution.py:407
  13.9 11.3 %collective-permute-start.3 = (bf16[272,256]{1,0:T(8,128)(2,1)S(1)}, bf16[272,256]{1,0:T(8,128)(2,1)S(1)}, u32[]{:S(2)}, u32[]{:S(2)}) collective-permute-start(bf16[272,256]{1,0:T(8,128)(2,1)S(1)} %get-tuple-element.19.refs_0_.refs_9_.refs_11_), channel_id=1, source_target_pairs={{192,0},{224,32},{0,64},{32,96},{64,128},{96,160},{128,192},{160,2... | collective-permute-start | bytes 417800 | tf_op jit(solution)/shard_map/ppermute | solution.py:407
  16.9 10.8 %collective-permute-start.2 = (bf16[272,256]{1,0:T(8,128)(2,1)S(1)}, bf16[272,256]{1,0:T(8,128)(2,1)S(1)}, u32[]{:S(2)}, u32[]{:S(2)}) collective-permute-start(bf16[272,256]{1,0:T(8,128)(2,1)S(1)} %get-tuple-element.19.refs_0_.refs_9_.refs_11_), channel_id=1, source_target_pairs={{64,0},{96,32},{128,64},{160,96},{192,128},{224,160},{0,192},{32,2... | collective-permute-start | bytes 417800 | tf_op jit(solution)/shard_map/ppermute | solution.py:407
  22.5 7.5 %collective-permute-start.1 = (bf16[272,256]{1,0:T(8,128)(2,1)S(1)}, bf16[272,256]{1,0:T(8,128)(2,1)S(1)}, u32[]{:S(2)}, u32[]{:S(2)}) collective-permute-start(bf16[272,256]{1,0:T(8,128)(2,1)S(1)} %get-tuple-element.19.refs_0_.refs_9_.refs_11_), channel_id=1, source_target_pairs={{224,0},{0,32},{32,64},{64,96},{96,128},{128,160},{160,192},{192,2... | collective-permute-start | bytes 417800 | tf_op jit(solution)/shard_map/ppermute | solution.py:407
  23.3 9.5 %collective-permute-start = (bf16[272,256]{1,0:T(8,128)(2,1)S(1)}, bf16[272,256]{1,0:T(8,128)(2,1)S(1)}, u32[]{:S(2)}, u32[]{:S(2)}) collective-permute-start(bf16[272,256]{1,0:T(8,128)(2,1)S(1)} %get-tuple-element.19.refs_0_.refs_9_.refs_11_), channel_id=1, source_target_pairs={{32,0},{64,32},{96,64},{128,96},{160,128},{192,160},{224,192},{0,2... | collective-permute-start | bytes 417800 | tf_op jit(solution)/shard_map/ppermute | solution.py:407
  25.3 12.5 %collective-permute-start.5 = (bf16[272,256]{1,0:T(8,128)(2,1)S(1)}, bf16[272,256]{1,0:T(8,128)(2,1)S(1)}, u32[]{:S(2)}, u32[]{:S(2)}) collective-permute-start(bf16[272,256]{1,0:T(8,128)(2,1)S(1)} %collective-permute-done.3.refs_4_.refs_13_.refs_15_), channel_id=1, source_target_pairs={{224,0},{0,32},{32,64},{64,96},{96,128},{128,160},{160,192},{192,2... | collective-permute-start | bytes 417800 | tf_op jit(solution)/shard_map/ppermute | solution.py:407
  27.7 10.1 %collective-permute-start.4 = (bf16[272,256]{1,0:T(8,128)(2,1)S(1)}, bf16[272,256]{1,0:T(8,128)(2,1)S(1)}, u32[]{:S(2)}, u32[]{:S(2)}) collective-permute-start(bf16[272,256]{1,0:T(8,128)(2,1)S(1)} %collective-permute-done.2.refs_3_.refs_12_.refs_14_), channel_id=1, source_target_pairs={{32,0},{64,32},{96,64},{128,96},{160,128},{192,160},{224,192},{0,2... | collective-permute-start | bytes 417800 | tf_op jit(solution)/shard_map/ppermute | solution.py:407
  28.7 4.8 %collective-permute-start.6 = (bf16[144,256]{1,0:T(8,128)(2,1)S(1)}, bf16[144,256]{1,0:T(8,128)(2,1)S(1)}, u32[]{:S(2)}, u32[]{:S(2)}) collective-permute-start(bf16[144,256]{1,0:T(8,128)(2,1)S(1)} %slice.18), channel_id=1, source_target_pairs={{64,0},{96,32},{128,64},{160,96},{192,128},{224,160},{0,192},{32,2... | collective-permute-start | bytes 221192 | tf_op jit(solution)/shard_map/ppermute | solution.py:407
  30.0 14.5 %collective-permute-start.14 = (bf16[272,256]{1,0:T(8,128)(2,1)S(1)}, bf16[272,256]{1,0:T(8,128)(2,1)S(1)}, u32[]{:S(2)}, u32[]{:S(2)}) collective-permute-start(bf16[272,256]{1,0:T(8,128)(2,1)S(1)} %get-tuple-element.20.refs_1_.refs_3_), channel_id=1, source_target_pairs={{4,0},{0,4},{5,1},{1,5},{6,2},{2,6},{7,3},{3,7},{12,8},{8,12},{13,... | collective-permute-start | bytes 417800 | tf_op jit(solution)/shard_map/ppermute | solution.py:407
  32.8 15.1 %collective-permute-start.17 = (bf16[272,256]{1,0:T(8,128)(2,1)S(1)}, bf16[272,256]{1,0:T(8,128)(2,1)S(1)}, u32[]{:S(2)}, u32[]{:S(2)}) collective-permute-start(bf16[272,256]{1,0:T(8,128)(2,1)S(1)} %collective-permute-done.13.refs_4_.refs_6_), channel_id=1, source_target_pairs={{4,0},{0,4},{5,1},{1,5},{6,2},{2,6},{7,3},{3,7},{12,8},{8,12},{13,... | collective-permute-start | bytes 417800 | tf_op jit(solution)/shard_map/ppermute | solution.py:407
  33.5 17.1 %collective-permute-start.16 = (bf16[272,256]{1,0:T(8,128)(2,1)S(1)}, bf16[272,256]{1,0:T(8,128)(2,1)S(1)}, u32[]{:S(2)}, u32[]{:S(2)}) collective-permute-start(bf16[272,256]{1,0:T(8,128)(2,1)S(1)} %collective-permute-done.12.refs_3_.refs_5_), channel_id=1, source_target_pairs={{4,0},{0,4},{5,1},{1,5},{6,2},{2,6},{7,3},{3,7},{12,8},{8,12},{13,... | collective-permute-start | bytes 417800 | tf_op jit(solution)/shard_map/ppermute | solution.py:407
  37.8 12.8 %collective-permute-start.15 = (bf16[272,256]{1,0:T(8,128)(2,1)S(1)}, bf16[272,256]{1,0:T(8,128)(2,1)S(1)}, u32[]{:S(2)}, u32[]{:S(2)}) collective-permute-start(bf16[272,256]{1,0:T(8,128)(2,1)S(1)} %collective-permute-done.11.refs_2_.refs_4_), channel_id=1, source_target_pairs={{4,0},{0,4},{5,1},{1,5},{6,2},{2,6},{7,3},{3,7},{12,8},{8,12},{13,... | collective-permute-start | bytes 417800 | tf_op jit(solution)/shard_map/ppermute | solution.py:407
  38.6 1.6 %collective-permute-start.7 = (f32[1,128]{1,0:T(1,128)S(1)}, f32[1,128]{1,0:T(1,128)S(1)}, u32[]{:S(2)}, u32[]{:S(2)}) collective-permute-start(f32[1,128]{1,0:T(1,128)S(1)} %shard_map.112), channel_id=1, source_target_pairs={{4,0},{0,4},{5,1},{1,5},{6,2},{2,6},{7,3},{3,7},{12,8},{8,12},{13,... | collective-permute-start | bytes 1544 | tf_op jit(solution)/shard_map/ppermute | solution.py:407
  40.2 7.6 %collective-permute-start.18 = (bf16[128,256]{1,0:T(8,128)(2,1)S(1)}, bf16[128,256]{1,0:T(8,128)(2,1)S(1)}, u32[]{:S(2)}, u32[]{:S(2)}) collective-permute-start(bf16[128,256]{1,0:T(8,128)(2,1)S(1)} %slice.19), channel_id=1, source_target_pairs={{192,0},{224,32},{0,64},{32,96},{64,128},{96,160},{128,192},{160,2... | collective-permute-start | bytes 196616 | tf_op jit(solution)/shard_map/ppermute | solution.py:407
  44.5 15.8 %collective-permute-start.10 = (f32[2,128]{1,0:T(2,128)S(1)}, f32[2,128]{1,0:T(2,128)S(1)}, u32[]{:S(2)}, u32[]{:S(2)}) collective-permute-start(f32[2,128]{1,0:T(2,128)S(1)} %pad_maximum_fusion.t0), channel_id=1, source_target_pairs={{16,0},{24,8},{0,16},{8,24},{17,1},{25,9},{1,17},{9,25},{18,2},{26... | collective-permute-start | bytes 3080 | tf_op jit(solution)/shard_map/ppermute | solution.py:407
  47.9 12.5 %collective-permute-start.9 = (f32[2,128]{1,0:T(2,128)S(1)}, f32[2,128]{1,0:T(2,128)S(1)}, u32[]{:S(2)}, u32[]{:S(2)}) collective-permute-start(f32[2,128]{1,0:T(2,128)S(1)} %pad_maximum_fusion.t0), channel_id=1, source_target_pairs={{24,0},{0,8},{8,16},{16,24},{25,1},{1,9},{9,17},{17,25},{26,2},{2,... | collective-permute-start | bytes 3080 | tf_op jit(solution)/shard_map/ppermute | solution.py:407
  47.9 12.5 %collective-permute-start.8 = (f32[2,128]{1,0:T(2,128)S(1)}, f32[2,128]{1,0:T(2,128)S(1)}, u32[]{:S(2)}, u32[]{:S(2)}) collective-permute-start(f32[2,128]{1,0:T(2,128)S(1)} %pad_maximum_fusion.t0), channel_id=1, source_target_pairs={{8,0},{16,8},{24,16},{0,24},{9,1},{17,9},{25,17},{1,25},{10,2},{18... | collective-permute-start | bytes 3080 | tf_op jit(solution)/shard_map/ppermute | solution.py:407
  95.8 14.2 %all-to-all-start.1 = ((bf16[8,272,128]{2,1,0:T(8,128)(2,1)}), bf16[8,272,128]{2,1,0:T(8,128)(2,1)S(1)}, u32[]{:S(2)}, u32[]{:S(2)}) async-start(bf16[8,272,128]{2,1,0:T(8,128)(2,1)} %get-tuple-element.26), calls=%async_computation.1 | async-start | bytes 1114112 | tf_op jit(solution)/shard_map/all_to_all | solution.py:518
  (1 other events, 0.7 us)

commit v2 on v1

v2 whole, which is shorter than its diff:
```python
import math

import jax
import jax.numpy as jnp
from jax import lax
from jax.experimental import pallas as pl
from jax.experimental.pallas import tpu as pltpu
from jax.sharding import Mesh, PartitionSpec as P

F32 = jnp.float32
BF16 = jnp.bfloat16
LOG2E = 1.4426950408889634
NEG = -1e30
GROUP = 8
HALF = 128
ROWS = 256
AUX = 16
PACK = ROWS + AUX
NEAR = (0, 1, -1, 2, -2, 3, -3, 4)
Z, Y, C = "z", ("y_hi", "y_lo"), "core"
COLUMN = ("y_hi", "y_lo", "core")
VMEM_LIMIT = 20 * 1024 * 1024
vmem = pl.BlockSpec(memory_space=pltpu.VMEM)
smem = pl.BlockSpec(memory_space=pltpu.SMEM)
hbm = pl.BlockSpec(memory_space=pl.ANY)


def call(kernel, outs, in_specs, scratch=(), flops=0, out_spec=None, limit=VMEM_LIMIT):
    return pl.pallas_call(
        kernel,
        out_shape=outs,
        in_specs=in_specs,
        out_specs=out_spec or jax.tree.map(lambda _: vmem, outs),
        scratch_shapes=list(scratch),
        compiler_params=pltpu.CompilerParams(vmem_limit_bytes=limit),
        cost_estimate=pl.CostEstimate(flops=flops, bytes_accessed=4 << 20, transcendentals=0),
    )


def dot(a, b, ca, cb):
    return lax.dot_general(a, b, (((ca,), (cb,)), ((), ())), preferred_element_type=F32)


def split_rows(row, first=0):
    high = row.astype(BF16).astype(F32)
    middle = (row - high).astype(BF16).astype(F32)
    low = row - high - middle
    at = lax.broadcasted_iota(jnp.int32, (AUX, row.shape[1]), 0) - first
    return jnp.where(at == 0, high, jnp.where(at == 1, middle, jnp.where(at == 2, low, 0.0)))


def join_rows(rows, first=0):
    rows = rows.astype(F32)
    return rows[first : first + 1] + rows[first + 1 : first + 2] + rows[first + 2 : first + 3]


def running_sum(row):
    lane = lax.broadcasted_iota(jnp.int32, row.shape, 1)
    step = 1
    while step < HALF:
        row = row + jnp.where(lane >= step, pltpu.roll(row, step, 1), 0.0)
        step *= 2
    return row


def place_of():
    z, y, core = lax.axis_index(Z), lax.axis_index("y_hi") * 2 + lax.axis_index("y_lo"), lax.axis_index(C)
    return z, y, core, y * 2 + core


def slot_low(span_ref, slot):
    return jnp.minimum(span_ref[2 * slot], span_ref[2 * slot + 1])


def own_swap(span_ref):
    z, _, _, column = place_of()
    slot = 2 * (z * GROUP + column)
    return (span_ref[slot] > span_ref[slot + 1]).astype(jnp.int32)


def near_z(z, e):
    return lax.rem(z + (NEAR[e] + GROUP), GROUP)


def near_column(y, core, at):
    offset, other = (0, 1, 3, 2)[at // 2], at % 2
    return lax.rem(y + offset, 4) * 2 + (1 - core if other else core)


def half_rows(half):
    return pl.ds(pl.multiple_of(HALF * half, HALF), HALF)


def table_lanes(table, z, own, low, high):
    sub = lax.broadcasted_iota(jnp.int32, (GROUP, HALF), 0)
    lane = lax.broadcasted_iota(jnp.int32, (GROUP, HALF), 1)
    table = jnp.where((sub == z) & (lane == 2 * own), low, table)
    return jnp.where((sub == z) & (lane == 2 * own + 1), high, table)


def pack_kernel(
    span_ref, q_ref, k_ref, v_ref, g_ref, f_ref, qg_ref, kv_ref, qg, kv, sems
):
    swap = own_swap(span_ref)
    copies = []
    for half in range(2):
        source = half_rows(jnp.bitwise_xor(half, swap))
        target = pl.ds(HALF * half, HALF)
        for ref, out, lanes in (
            (k_ref, kv, pl.ds(0, HALF)),
            (v_ref, kv, pl.ds(HALF, HALF)),
            (q_ref, qg, pl.ds(0, HALF)),
            (g_ref, qg, pl.ds(HALF, HALF)),
        ):
            copies.append((ref.at[source, :], out.at[target, lanes]))
    copies = [pltpu.make_async_copy(a, b, sems.at[i]) for i, (a, b) in enumerate(copies)]
    for copy in copies:
        copy.start()
    gates = [f_ref[0:1, 0:HALF], f_ref[0:1, HALF:ROWS]]
    for half in range(2):
        gate = running_sum(jnp.where(swap == 1, gates[1 - half], gates[half]))
        rows = split_rows(gate).astype(BF16)
        qg[ROWS:PACK, HALF * half : HALF * (half + 1)] = rows
        kv[ROWS:PACK, HALF * half : HALF * (half + 1)] = rows
    for copy in copies:
        copy.wait()
    run_copies([(kv, kv_ref), (qg, qg_ref)], sems)


def totals_kernel(*refs):
    blocks, out_ref, aux, sems = refs[:8], refs[8], refs[9], refs[10]
    z, _, _, own = place_of()
    copies = []
    for at, block in enumerate(blocks):
        last = block.shape[0] - AUX
        copies.append((block.at[pl.ds(last, AUX), :], aux.at[at]))
    run_copies(copies, sems)
    table = jnp.zeros((GROUP, HALF), F32)
    for e in range(GROUP):
        row = join_rows(aux[e])
        ends = [row[:, HALF * (half + 1) - 1 : HALF * (half + 1)] for half in range(2)]
        table = table_lanes(table, near_z(z, e), own, *ends)
    out_ref[...] = table


def ids_kernel(span_ref, out_ref):
    table = jnp.zeros((GROUP, HALF), jnp.int32)
    for z in range(GROUP):
        for b in range(GROUP):
            low = slot_low(span_ref, z * GROUP + b)
            table = table_lanes(table, z, b, low, 127 - low)
    out_ref[...] = table


def run_copies(copies, sems):
    copies = [pltpu.make_async_copy(a, b, sems.at[i]) for i, (a, b) in enumerate(copies)]
    for copy in copies:
        copy.start()
    for copy in copies:
        copy.wait()


def key_copies(key_refs, ks):
    copies, at = [], 0
    for ref in key_refs:
        if ref.shape[0] == HALF + AUX:
            copies.append((ref, ks.at[at, pl.ds(HALF, HALF + AUX), :]))
        elif ref.shape[0] == HALF:
            copies.append((ref, ks.at[at, pl.ds(0, HALF), :]))
            at += 1
        else:
            copies.append((ref, ks.at[at]))
            at += 1
    return copies


def gate_columns(ks, e, columns):
    row = join_rows(ks[e, ROWS:PACK, :]) * LOG2E
    for half in range(2):
        part = row[:, HALF * half : HALF * (half + 1)]
        columns[half] = jnp.transpose(jnp.broadcast_to(part, (HALF, HALF)))


def ahead_of():
    return lax.broadcasted_iota(jnp.int32, (HALF, HALF), 0) - lax.broadcasted_iota(
        jnp.int32, (HALF, HALF), 1
    )


def lanes_of(d):
    return pl.ds(pl.multiple_of(HALF * d, HALF), HALF)


def load_queries(query_refs, y, core, qs, gates):
    copies = []
    for at, ref in enumerate(query_refs):
        d = near_column(y, core, at)
        for half in range(2):
            copies.append((ref.at[pl.ds(HALF * half, HALF), :], qs.at[half, lanes_of(d), :]))
        copies.append((ref.at[pl.ds(ROWS, AUX), :], gates.at[d]))
    return copies


def stats_kernel(scale, first, span_ref, *refs):
    z, y, core, own = place_of()
    if first:
        qt, wq = refs[:2]
        rest, refs = refs[2:], ()
        count = 3
        key_refs, (one_ref, two_ref), (ks, columns, sems) = rest[:4], rest[4:6], rest[6:]
        run_copies(key_copies(key_refs, ks), sems)
    else:
        count = 5
        query_refs, key_refs = refs[:8], refs[8:13]
        one_ref, two_ref, own_ref, qs, qt, wq, ks, columns, gates, sems = refs[13:]
        run_copies(load_queries(query_refs, y, core, qs, gates) + key_copies(key_refs, ks), sems)
        for d in range(GROUP):
            rows = slice(HALF * d, HALF * (d + 1))
            row = join_rows(gates[d]) * LOG2E
            wq[0, d : d + 1, :] = row[:, 0:HALF]
            wq[1, d : d + 1, :] = row[:, HALF:ROWS]
            for half in range(2):
                qt[0, half, :, rows] = jnp.transpose(qs[half, rows, 0:HALF])
                qt[1, half, :, rows] = jnp.transpose(qs[half, rows, HALF:ROWS])
    ahead = ahead_of()
    lows = [slot_low(span_ref, z * GROUP + d) for d in range(GROUP)]

    def tile_stats(scores, upstream):
        best = jnp.max(scores, axis=0, keepdims=True)
        factor = jnp.exp2(scores - best)
        return (
            best,
            jnp.sum(factor, axis=0, keepdims=True),
            jnp.sum(factor * upstream, axis=0, keepdims=True),
        )

    for e in range(count):
        gate_columns(ks, e, columns)
        key_span = slot_low(span_ref, near_z(z, first + e) * GROUP + own)
        key_low, value_low = ks[e, 0:HALF, 0:HALF], ks[e, 0:HALF, HALF:ROWS]
        column = columns[0]
        column2 = jnp.concatenate([column, column], 1)
        for pair in range(GROUP // 2):
            lanes = slice(ROWS * pair, ROWS * (pair + 1))
            w = jnp.concatenate([wq[1, 2 * pair + i : 2 * pair + i + 1, :] for i in range(2)], 1)
            scores = dot(key_low, qt[0, 1, :, lanes], 1, 0) * scale + (w - column2)
            upstream = dot(value_low, qt[1, 1, :, lanes], 1, 0)
            for at, row in enumerate(tile_stats(scores, upstream)):
                one_ref[e, at : at + 1, lanes] = row
        for d in range(GROUP):
            half = (key_span > lows[d]).astype(jnp.int32)
            rows, lanes = half_rows(half), slice(HALF * d, HALF * (d + 1))
            scores = dot(ks[e, rows, 0:HALF], qt[0, half, :, lanes], 1, 0) * scale + (
                wq[half, d : d + 1, :] - columns[half]
            )
            if first + e == 0:
                scores = jnp.where(ahead <= jnp.where(own == d, 0, HALF), scores, NEG)
            upstream = dot(ks[e, rows, HALF:ROWS], qt[1, half, :, lanes], 1, 0)
            for at, row in enumerate(tile_stats(scores, upstream)):
                two_ref[e, at : at + 1, lanes] = row
        if first + e == 0:
            w, lanes = wq[1, pl.ds(own, 1), :], lanes_of(own)
            scores = dot(ks[0, HALF:ROWS, 0:HALF], qt[0, 1, :, lanes], 1, 0) * scale
            scores = jnp.where(ahead <= 0, scores + (w - columns[1]), NEG)
            upstream = dot(ks[0, HALF:ROWS, HALF:ROWS], qt[1, 1, :, lanes], 1, 0)
            for at, row in enumerate(tile_stats(scores, upstream)):
                own_ref[at : at + 1, :] = row


def down(x):
    return jnp.sum(x, axis=0, keepdims=True)


def key_ranks(span_ref, z, own):
    sub = lax.broadcasted_iota(jnp.int32, (GROUP, HALF), 0)
    rank = jnp.zeros((GROUP, HALF), jnp.int32)
    for e in range(GROUP):
        rank = jnp.where(sub == e, slot_low(span_ref, near_z(z, e) * GROUP + own), rank)
    return rank


def tile_rows(near_ref, far_ref, at, lanes):
    return jnp.concatenate([near_ref[:, at, lanes], far_ref[:, at, lanes]], 0)


def merge_kernel(
    span_ref, ids_ref, t0, t1, t2, t3, near1, near2, own_ref, far1, far2, out_ref, place_ref
):
    z, y, core, own = place_of()
    ids, totals = ids_ref[...], t0[...] + t1[...] + t2[...] + t3[...]
    lows = [slot_low(span_ref, near_z(z, e) * GROUP + own) for e in range(GROUP)]
    lows += [slot_low(span_ref, z * GROUP + d) for d in range(GROUP)]
    places = {}
    for at in range(2 * GROUP):
        for half in range(2):
            span = 127 - lows[at] if half else lows[at]
            before = jnp.where(ids < span, totals, 0.0)
            place = jnp.sum(down(before), axis=1, keepdims=True) * LOG2E
            row = 2 * GROUP * (at // GROUP) + GROUP * half + at % GROUP
            places[row] = jnp.broadcast_to(place, (1, HALF))
            place_ref[row : row + 1, :] = places[row]
    key_low = jnp.concatenate([places[i] for i in range(0, 8)], 0)
    key_high = jnp.concatenate([places[i] for i in range(8, 16)], 0)
    ranks = key_ranks(span_ref, z, own)

    def finish(best, total, weighted, at, d):
        some = total > 0.0
        safe = jnp.where(some, total, 1.0)
        lse = jnp.where(some, best + jnp.log2(safe), NEG)
        delta = jnp.where(some, weighted / safe, 0.0)
        for copy in range(GROUP):
            out_ref[copy, at + d : at + d + 1, :] = lse
            out_ref[copy, at + 8 + d : at + 9 + d, :] = delta

    for d in range(GROUP):
        lanes = slice(HALF * d, HALF * (d + 1))
        one = [tile_rows(near1, far1, at, lanes) for at in range(3)]
        two = [tile_rows(near2, far2, at, lanes) for at in range(3)]
        high = ranks > lows[GROUP + d]
        query_low, query_high = places[16 + d], places[24 + d]
        first = one[0] + (query_high - key_low)
        second = two[0] + jnp.where(high, query_high - key_high, query_low - key_low)
        mine = own == d
        third = jnp.where(mine, own_ref[0:1, :], NEG)
        best = jnp.maximum(
            jnp.max(jnp.maximum(first, jnp.where(high, second, NEG)), axis=0, keepdims=True), third
        )
        first_weight = jnp.exp2(first - best)
        second_weight = jnp.where(high, jnp.exp2(second - best), 0.0)
        third_weight = jnp.where(mine, jnp.exp2(third - best), 0.0)
        sums = [
            down(one[at] * first_weight + two[at] * second_weight)
            + own_ref[at : at + 1, :] * third_weight
            for at in (1, 2)
        ]
        finish(best, sums[0], sums[1], 0, d)
        low = jnp.where(high, NEG, second)
        best = jnp.max(low, axis=0, keepdims=True)
        weight = jnp.where(high, 0.0, jnp.exp2(low - best))
        sums = [down(two[at] * weight) for at in (1, 2)]
        finish(best, sums[0], sums[1], 16, d)


def combine_kernel(
    span_ref, stats_ref, place_ref, wq_ref, near1, near2, own_ref, far1, far2, gate_ref, delta_ref, out_ref
):
    z, y, core, own = place_of()
    lses, deltas = [None, None], [None, None]
    for half, at in ((1, 0), (0, 16)):
        lse = [stats_ref[b, at : at + 8, :] for b in range(GROUP)]
        best = lse[0]
        for b in range(1, GROUP):
            best = jnp.maximum(best, lse[b])
        total = jnp.zeros((GROUP, HALF), F32)
        weighted = jnp.zeros((GROUP, HALF), F32)
        for b in range(GROUP):
            weight = jnp.exp2(lse[b] - best)
            total = total + weight
            weighted = weighted + weight * stats_ref[b, at + 8 : at + 16, :]
        lses[half] = best + jnp.log2(total)
        deltas[half] = weighted / total
        gate_ref[half] = wq_ref[half] - lses[half]
        delta_ref[half] = deltas[half]
    key_low, key_high = place_ref[0:8, :], place_ref[8:16, :]
    ranks = key_ranks(span_ref, z, own)
    sub = lax.broadcasted_iota(jnp.int32, (GROUP, HALF), 0)
    low_sum = jnp.zeros((GROUP, HALF), F32)
    high_sum = jnp.zeros((GROUP, HALF), F32)
    for d in range(GROUP):
        lanes = slice(HALF * d, HALF * (d + 1))
        one = [tile_rows(near1, far1, at, lanes) for at in range(3)]
        two = [tile_rows(near2, far2, at, lanes) for at in range(3)]
        high = ranks > slot_low(span_ref, z * GROUP + d)
        lse_low, lse_high = lses[0][d : d + 1, :], lses[1][d : d + 1, :]
        delta_low, delta_high = deltas[0][d : d + 1, :], deltas[1][d : d + 1, :]
        query_low, query_high = place_ref[16 + d : 17 + d, :], place_ref[24 + d : 25 + d, :]
        first = jnp.exp2(one[0] + (query_high - key_low) - lse_high)
        first = first * (one[2] - delta_high * one[1])
        shift = jnp.where(high, query_high - key_high - lse_high, query_low - key_low - lse_low)
        second = jnp.exp2(two[0] + shift)
        second = second * (two[2] - jnp.where(high, delta_high, delta_low) * two[1])
        third = jnp.exp2(own_ref[0:1, :] - lse_high)
        third = third * (own_ref[2:3, :] - delta_high * own_ref[1:2, :])
        low_sum = low_sum + first + jnp.where(high, 0.0, second)
        high_sum = high_sum + jnp.where(high, second, 0.0)
        high_sum = high_sum + jnp.where((sub == 0) & (own == d), third, 0.0)
    low_sum = -jnp.sum(low_sum, axis=1, keepdims=True)
    high_sum = -jnp.sum(high_sum, axis=1, keepdims=True)
    table = jnp.zeros((GROUP, HALF), F32)
    for e in range(GROUP):
        row = slice(e, e + 1)
        table = table_lanes(table, near_z(z, e), own, low_sum[row, :], high_sum[row, :])
    for copy in range(GROUP):
        out_ref[copy] = table


def beyond_kernel(span_ref, ids_ref, tables_ref, a_ref, b_ref, c_ref, out_ref, a_out, b_out, c_out):
    z, y, core, own = place_of()
    table = tables_ref[0]
    for b in range(1, GROUP):
        table = table + tables_ref[b]
    ids = ids_ref[...]
    lane = lax.broadcasted_iota(jnp.int32, (1, ROWS), 1)
    rows = []
    for e in range(GROUP):
        low = slot_low(span_ref, near_z(z, e) * GROUP + own)
        row = jnp.zeros((1, ROWS), F32)
        for half, span in ((0, low), (1, 127 - low)):
            value = jnp.sum(down(jnp.where(ids > span, table, 0.0)), axis=1, keepdims=True)
            row = jnp.where(lane == HALF * (half + 1) - 1, value, row)
        rows.append(row)
        out_ref[e : e + 1, :] = row
    for row, source, target in zip(rows[5:], (a_ref, b_ref, c_ref), (a_out, b_out, c_out)):
        last = source.shape[0] - AUX
        target[0:last, :] = source[0:last, :]
        aux = join_rows(source[last : last + AUX, :]) + row
        target[last : last + AUX, :] = split_rows(aux).astype(BF16)


def grads_kernel(scale, first, count, pieces, span_ref, qs, qt, gate_ref, delta_ref, place_ref, *refs):
    z, y, core, own = place_of()
    key_refs, refs = refs[:pieces], refs[pieces:]
    if first == 5:
        dqt, refs = refs[0], refs[1:]
        dqt[...] = jnp.zeros_like(dqt)
        outs, scratch = refs[:4], refs[4:]
    elif first == 0:
        before, beyond, dqt, refs = refs[0], refs[1], refs[2], refs[3:]
        dqt[...] = before[...]
        outs, scratch = refs[:3], refs[3:]
    else:
        before, beyond, up3, down3, up4, down4, dq_ref = refs[:7]
        outs, scratch = refs[7:9], refs[9:]
        dqt, scratch = scratch[0], scratch[1:]
        dqt[...] = before[...]
    ks, columns, pg, sems = scratch
    run_copies(key_copies(key_refs, ks), sems)
    ahead = ahead_of()
    inverse = 1.0 / math.sqrt(HALF)
    lows = [slot_low(span_ref, z * GROUP + d) for d in range(GROUP)]

    def query_gate(half, d, key_place):
        place = place_ref[pl.ds(16 + 8 * half + d, 1), :]
        return gate_ref[half, d : d + 1, :] + (place - key_place)

    for e in range(count):
        number = first + e
        gate_columns(ks, e, columns)
        key_span = slot_low(span_ref, near_z(z, number) * GROUP + own)
        key_low, value_low = ks[e, 0:HALF, 0:HALF], ks[e, 0:HALF, HALF:ROWS]
        turned = jnp.transpose(ks[e, :ROWS, 0:HALF])
        column = columns[0]
        column2 = jnp.concatenate([column, column], 1)
        place = place_ref[number : number + 1, :]
        probs1, grads1, probs2, grads2 = [], [], ([], []), ([], [])
        total = jnp.zeros((HALF, HALF), F32)
        for pair in range(GROUP // 2):
            both, lanes = (2 * pair, 2 * pair + 1), slice(ROWS * pair, ROWS * (pair + 1))
            w = jnp.concatenate([query_gate(1, d, place) for d in both], 1)
            shift = jnp.concatenate([delta_ref[1, d : d + 1, :] for d in both], 1)
            probs = jnp.exp2(dot(key_low, qt[0, 1, :, lanes], 1, 0) * scale + (w - column2))
            grads = probs * (dot(value_low, qt[1, 1, :, lanes], 1, 0) - shift)
            probs1.append(probs.astype(BF16))
            grads1.append(grads.astype(BF16))
            total = total + grads[:, 0:HALF] + grads[:, HALF:ROWS]
        pg[0] = total
        pg[1] = jnp.zeros((HALF, HALF), F32)
        chosen = []
        for d in range(GROUP):
            half = (key_span > lows[d]).astype(jnp.int32)
            rows, lanes = half_rows(half), slice(HALF * d, HALF * (d + 1))
            chosen.append(qs[half, lanes, :])
            w = query_gate(half, d, place_ref[pl.ds(8 * half + number, 1), :])
            scores = dot(ks[e, rows, 0:HALF], qt[0, half, :, lanes], 1, 0) * scale
            probs = jnp.exp2(scores + (w - columns[half]))
            if number == 0:
                probs = jnp.where(ahead <= jnp.where(own == d, 0, HALF), probs, 0.0)
            upstream = dot(ks[e, rows, HALF:ROWS], qt[1, half, :, lanes], 1, 0)
            grads = probs * (upstream - delta_ref[half, d : d + 1, :])
            pg[half] += grads
            probs, grads = probs.astype(BF16), grads.astype(BF16)
            zero = jnp.zeros_like(probs)
            for side in range(2):
                probs2[side].append(jnp.where(half == side, probs, zero))
                grads2[side].append(jnp.where(half == side, grads, zero))
        chosen = jnp.concatenate(chosen, 0)
        side_probs, side_grads = (
            [jnp.concatenate(part, 1) for part in parts] for parts in (probs2, grads2)
        )
        value_parts = dot(jnp.concatenate(side_probs, 0), chosen[:, HALF:ROWS], 1, 0)
        key_parts = dot(jnp.concatenate(side_grads, 0), chosen[:, 0:HALF], 1, 0)
        dv = [
            value_parts[0:HALF, :] + dot(jnp.concatenate(probs1, 1), qs[1, :, HALF:ROWS], 1, 0),
            value_parts[HALF:ROWS, :],
        ]
        dk = [
            key_parts[0:HALF, :] + dot(jnp.concatenate(grads1, 1), qs[1, :, 0:HALF], 1, 0),
            key_parts[HALF:ROWS, :],
        ]
        for pair in range(GROUP // 2):
            lanes = slice(ROWS * pair, ROWS * (pair + 1))
            stack = jnp.concatenate([grads1[pair], side_grads[1][:, lanes]], 0)
            dqt[1, :, lanes] += dot(turned, stack, 1, 0)
            dqt[0, :, lanes] += dot(turned[:, 0:HALF], side_grads[0][:, lanes], 1, 0)
        if number == 0:
            lanes = lanes_of(own)
            scores = dot(ks[e, HALF:ROWS, 0:HALF], qt[0, 1, :, lanes], 1, 0) * scale
            probs = jnp.exp2(scores + (gate_ref[1, pl.ds(own, 1), :] - columns[1]))
            probs = jnp.where(ahead <= 0, probs, 0.0)
            upstream = dot(ks[e, HALF:ROWS, HALF:ROWS], qt[1, 1, :, lanes], 1, 0)
            grads = probs * (upstream - delta_ref[1, pl.ds(own, 1), :])
            low_grads, block = grads.astype(BF16), qs[1, lanes_of(own), :]
            dv[1] = dv[1] + dot(probs.astype(BF16), block[:, HALF:ROWS], 1, 0)
            dk[1] = dk[1] + dot(low_grads, block[:, 0:HALF], 1, 0)
            dqt[1, :, lanes] += dot(turned[:, HALF:ROWS], low_grads, 1, 0)
            pg[1] += grads

        for half in range(2):
            rows = slice(HALF * half, HALF * (half + 1))
            key_part, value_part = dk[half] * inverse, dv[half]
            row = -down(jnp.transpose(pg[half]))
            if number < 5:
                row = row + beyond[number : number + 1, rows]
            out, base, keep_aux = outs[e], HALF * half, True
            if number == 7:
                out, base, keep_aux = outs[2 + half], 0, half == 1
            if number in (3, 4):
                arrived = (up3, down3)[number - 3]
                key_part = key_part + arrived[rows, 0:HALF].astype(F32)
                value_part = value_part + arrived[rows, HALF:ROWS].astype(F32)
                row = row + join_rows(arrived[ROWS:PACK, rows])
                if number == 3:
                    row = row + join_rows(up4[HALF : HALF + AUX, rows])
                if half == 4 - number:
                    arrived = (up4, down4)[number - 3]
                    key_part = key_part + arrived[0:HALF, 0:HALF].astype(F32)
                    value_part = value_part + arrived[0:HALF, HALF:ROWS].astype(F32)
            out[base : base + HALF, 0:HALF] = key_part.astype(BF16)
            out[base : base + HALF, HALF:ROWS] = value_part.astype(BF16)
            aux_out = outs[3] if number == 7 else out
            aux_base = HALF if number == 7 else ROWS
            aux_out[aux_base : aux_base + AUX, rows] = split_rows(row).astype(BF16)

    if first == 3:
        for d in range(GROUP):
            for half in range(2):
                part = jnp.transpose(dqt[half, :, HALF * d : HALF * (d + 1)]) * inverse
                dq_ref[d, HALF * half : HALF * (half + 1), :] = part.astype(BF16)


def final_kernel(
    span_ref, dq_parts, p0, p1, p2, p3, p4, dq_ref, dk_ref, dv_ref, f_ref
):
    z, y, core, own = place_of()
    swap = own_swap(span_ref)
    parts = (p0, p1, p2, p3, p4)
    halves = []
    for half in range(2):
        rows = slice(HALF * half, HALF * (half + 1))
        target = half_rows(jnp.bitwise_xor(half, swap))
        total = dq_parts[0, rows, :].astype(F32)
        for b in range(1, GROUP):
            total = total + dq_parts[b, rows, :].astype(F32)
        dq_ref[target, :] = total.astype(BF16)
        total = p0[rows, :].astype(F32)
        for part in parts[1:]:
            total = total + part[rows, :].astype(F32)
        total = total.astype(BF16)
        dk_ref[target, :] = total[:, 0:HALF]
        dv_ref[target, :] = total[:, HALF:ROWS]
        row = join_rows(p0[ROWS:PACK, rows])
        for part in parts[1:]:
            row = row + join_rows(part[ROWS:PACK, rows])
        total = jnp.sum(row, axis=1, keepdims=True)
        halves.append(total - running_sum(row) + row)
    for half in range(2):
        lanes = slice(HALF * half, HALF * (half + 1))
        f_ref[:, lanes] = jnp.where(swap == 1, halves[1 - half], halves[half])


def fetch(x, axis, size, offset):
    return lax.ppermute(x, axis, [((i + offset) % size, i) for i in range(size)])


def local(queries, key_vectors, value_vectors, out_grad, log_forget, span_order):
    scale = LOG2E / math.sqrt(HALF)

    def struct(shape, kind):
        return jax.ShapeDtypeStruct(shape, kind)

    block = struct((PACK, ROWS), BF16)
    table = struct((GROUP, HALF), F32)
    qg, kv = call(
        pack_kernel,
        (block, block),
        [smem] + [hbm] * 4 + [vmem],
        [pltpu.VMEM((PACK, ROWS), BF16)] * 2 + [pltpu.SemaphoreType.DMA((8,))],
        out_spec=(hbm, hbm),
        limit=62 * 1024 * 1024,
    )(span_order, queries[0], key_vectors[0], value_vectors[0], out_grad[0], log_forget)
    ids = call(ids_kernel, struct((GROUP, HALF), jnp.int32), [smem])(span_order)
    up1, down1, up2, down2 = [fetch(kv, Z, 8, o) for o in (1, -1, 2, -2)]
    mine = [qg] + [fetch(qg, Y, 4, o) for o in (1, -1, 2)]
    up3, down3 = fetch(up2, Z, 8, 1), fetch(down2, Z, 8, -1)
    theirs = [fetch(x, C, 2, 1) for x in mine]
    far_low = fetch(down2[:HALF], Z, 8, -2)
    far_high = fetch(up2[HALF:], Z, 8, 2)
    query_blocks = [x for pair in zip(mine, theirs) for x in pair]
    near_keys = [kv, up1, down1, up2, down2]
    far_keys = [up3, down3, far_high, far_low]

    totals = call(
        totals_kernel,
        table,
        [hbm] * 8,
        [pltpu.VMEM((8, AUX, ROWS), BF16), pltpu.SemaphoreType.DMA((8,))],
    )(*near_keys, *far_keys[:3])
    totals = totals + fetch(totals, C, 2, 1)
    totals = [totals] + [fetch(totals, Y, 4, o) for o in (1, -1, 2)]

    def key_scratch(count, sems, more=()):
        return [
            pltpu.VMEM((count, PACK, ROWS), BF16),
            pltpu.VMEM((2, HALF, HALF), F32),
            *more,
            pltpu.SemaphoreType.DMA((sems,)),
        ]

    def tiles(count):
        return struct((count, 3, GROUP * HALF), F32)

    gates = struct((2, GROUP, HALF), F32)
    near1, near2, own, qs, qt, wq = call(
        lambda *refs: stats_kernel(scale, 0, *refs),
        (
            tiles(5),
            tiles(5),
            struct((GROUP, HALF), F32),
            struct((2, GROUP * HALF, ROWS), BF16),
            struct((2, 2, HALF, GROUP * HALF), BF16),
            gates,
        ),
        [smem] + [hbm] * 13,
        key_scratch(5, 29, [pltpu.VMEM((GROUP, AUX, ROWS), BF16)]),
        flops=1 << 31,
    )(span_order, *query_blocks, *near_keys)
    far1, far2 = call(
        lambda *refs: stats_kernel(scale, 5, *refs),
        (tiles(3), tiles(3)),
        [smem, vmem, vmem] + [hbm] * 4,
        key_scratch(3, 4),
        flops=1 << 31,
    )(span_order, qt, wq, *far_keys)
    stats, place = call(
        merge_kernel,
        (struct((GROUP, 32, HALF), F32), struct((32, HALF), F32)),
        [smem] + [vmem] * 10,
    )(span_order, ids, *totals, near1, near2, own, far1, far2)
    stats = lax.all_to_all(stats, COLUMN, 0, 0, tiled=True)
    gate, delta, span_grads = call(
        combine_kernel,
        (gates, gates, struct((GROUP, GROUP, HALF), F32)),
        [smem] + [vmem] * 8,
    )(span_order, stats, place, wq, near1, near2, own, far1, far2)
    span_grads = lax.all_to_all(span_grads, COLUMN, 0, 0, tiled=True)
    square = pltpu.VMEM((2, HALF, HALF), F32)
    sum_t = struct((2, HALF, GROUP * HALF), F32)

    def grads(first, count, keys, more, outs, extra=()):
        return call(
            lambda *refs: grads_kernel(scale, first, count, len(keys), *refs),
            outs,
            [smem] + [vmem] * 5 + [hbm] * len(keys) + [vmem] * len(more),
            list(extra)
            + [
                pltpu.VMEM((count, PACK, ROWS), BF16),
                square,
                square,
                pltpu.SemaphoreType.DMA((len(keys),)),
            ],
            flops=1 << 31,
        )(span_order, qs, qt, gate, delta, place, *keys, *more)

    low_piece, high_piece = struct((HALF, ROWS), BF16), struct((HALF + AUX, ROWS), BF16)
    dqt, part3, part3d, part4, part4d_high = grads(
        5, 3, far_keys, [], (sum_t, block, block, low_piece, high_piece)
    )
    beyond, part3, part3d, part4d_high = call(
        beyond_kernel,
        (struct((GROUP, ROWS), F32), block, block, high_piece),
        [smem] + [vmem] * 5,
    )(span_order, ids, span_grads, part3, part3d, part4d_high)
    arrived_up3, arrived_down3 = fetch(part3, Z, 8, -1), fetch(part3d, Z, 8, 1)
    arrived_up4, arrived_down4 = fetch(part4d_high, Z, 8, -2), fetch(part4, Z, 8, 2)
    dqt, part0, part1, part1d = grads(0, 3, near_keys[:3], [dqt, beyond], (sum_t, block, block, block))
    arrived1, arrived1d = fetch(part1, Z, 8, -1), fetch(part1d, Z, 8, 1)
    dq_parts, part2, part2d = grads(
        3,
        2,
        near_keys[3:],
        [dqt, beyond, arrived_up3, arrived_down3, arrived_up4, arrived_down4],
        (struct((GROUP, ROWS, HALF), BF16), block, block),
        [pltpu.VMEM((2, HALF, GROUP * HALF), F32)],
    )
    arrived2, arrived2d = fetch(part2, Z, 8, -2), fetch(part2d, Z, 8, 2)
    dq_parts = lax.all_to_all(dq_parts, COLUMN, 0, 0, tiled=True)
    rows = struct((ROWS, HALF), BF16)
    dq, dk, dv, forget = call(
        final_kernel, (rows, rows, rows, struct((1, ROWS), F32)), [smem] + [vmem] * 6
    )(span_order, dq_parts, part0, arrived1, arrived1d, arrived2, arrived2d)
    return dq[None], dk[None], dv[None], forget


def solution(mesh):
    fine = Mesh(mesh.devices.reshape(8, 2, 2, 2, 4), ("z", "y_hi", "y_lo", "core", "head"))
    rows = ("z", "y_hi", "y_lo", "core")
    wide, thin = P("head", rows, None), P("head", rows)
    return jax.shard_map(
        local,
        mesh=fine,
        in_specs=(wide, wide, wide, wide, thin, P()),
        out_specs=(wide, wide, wide, thin),
        check_vma=False,
    )
```

time: 148 us -> 110 us (0.74)
  blocking collectives: 42.2 us -> 9.23 us
  starting transfers between devices: 38.7 us -> 55.5 us
  Pallas kernels: 41.4 us -> 31.1 us
  waiting for transfers between devices: 13.8 us -> 7.9 us
  other arithmetic: 3.54 us -> 0.01 us
    all_to_all x1 -> x0, blocking collectives: 33.5 us -> none  [local(): dkv_parts = lax.all_to_all(dkv_parts, Z, 0, 0, tiled=True)]
    ppermute x19 -> x27, starting transfers between devices: 34.4 us -> 45.7 us  [fetch(): lax.ppermute(x, axis, [((i + offset) % size, i) for i in range(size)])]
    pallas_call x7 -> x12, Pallas kernels: 41.4 us -> 31.1 us  [the longest x3 13.1 us: grads(): call(lambda *refs: grads_kernel(scale, first, count, len(keys), *refs), o...]
    all_to_all x1, waiting for transfers between devices: 9.69 us -> 0.01 us  [local(): dq_parts = lax.all_to_all(dq_parts, COLUMN, 0, 0, tiled=True)]
    all_to_all x0 -> x1, starting transfers between devices: none -> 4.11 us  [local(): span_grads = lax.all_to_all(span_grads, COLUMN, 0, 0, tiled=True)]
    ppermute x19 -> x27, waiting for transfers between devices: 4.12 us -> 7.9 us  [fetch(): lax.ppermute(x, axis, [((i + offset) % size, i) for i in range(size)])]
    reduce_sum x3 -> x0, other arithmetic: 1.53 us -> none  [pick(): return jnp.sum(jnp.where(match, table, 0), axis=-1)]
    unnamed x10 -> x16, local copies, waits for them, and re-layouts: 4.03 us -> 4.68 us
  transfers between devices with their start and end apart: 20 -> 29, of which waited for: 4 -> 4; matrix products, arithmetic and copies ran while one was open for 3% -> 0% of each run, Pallas kernels for 7% -> 18%
where the time goes in v2:
time: 110 us; the launch traced here: 109 us
  starting transfers between devices  55.5 us (50%)
  Pallas kernels  31.1 us (28%)
  blocking collectives  9.23 us (8%)
  waiting for transfers between devices  7.9 us (7%)
  local copies, waits for them, and re-layouts  4.7 us (4%)
    ppermute x27, starting transfers between devices, fetch(): lax.ppermute(x, axis, [((i + offset) % size, i) for i in range(size)])  45.7 us
    pallas_call x3, Pallas kernels, grads(): call(lambda *refs: grads_kernel(scale, first, count, len(keys), *refs), o...  13.1 us
    all_to_all x1, blocking collectives, local(): stats = lax.all_to_all(stats, COLUMN, 0, 0, tiled=True)  9.23 us
    ppermute x27, waiting for transfers between devices, fetch(): lax.ppermute(x, axis, [((i + offset) % size, i) for i in range(size)])  7.9 us
    pallas_call x1, Pallas kernels, local(): call(lambda *refs: stats_kernel(scale, 0, *refs), (tiles(5), tiles(5), st...  6.83 us
    all_to_all x1, starting transfers between devices, local(): dq_parts = lax.all_to_all(dq_parts, COLUMN, 0, 0, tiled=True)  5.7 us
    unnamed x16, local copies, waits for them, and re-layouts  4.68 us
    all_to_all x1, starting transfers between devices, local(): span_grads = lax.all_to_all(span_grads, COLUMN, 0, 0, tiled=True)  4.11 us
  transfers between devices with their start and end apart: 29, of which 4 were waited for; matrix products, arithmetic and copies ran while one was open for 0% of the time, Pallas kernels for 18%

profile of v2, /device:TPU:1, one launch (start us, length us, event | category | flops | bytes accessed | tf_op | source)
XLA Modules:
  0.0 109.3 jit_solution(4939726051357085877)
XLA Ops:
  0.6 2.7 %shard_map.93 = (bf16[272,256]{1,0:T(8,128)(2,1)}, bf16[272,256]{1,0:T(8,128)(2,1)}) custom-call(s32[128]{0:T(128)} %span_ref.11, bf16[256,128]{1,0:T(8,128)(2,1)} %bitcast.7, bf16[256,128]{1,0:T(8,128)(2,1)} %bitcast.8, bf16[256,128]{1,0:T(8,128)(2,1)} %bitcast.9, bf16[256,128]{1,0:T(8,128)(2,1)} %bitcast.10, f32[1,256]{1,0:T(1,128)} %f_ref.1), custom_call_target="tpu_custom_call" | custom-call | bytes 4194304 | tf_op jit(solution)/shard_map/pallas_call | solution.py:593
  3.3 3.8 %collective-permute-start.5 = (bf16[272,256]{1,0:T(8,128)(2,1)}, bf16[272,256]{1,0:T(8,128)(2,1)S(1)}, u32[]{:S(2)}, u32[]{:S(2)}) collective-permute-start(bf16[272,256]{1,0:T(8,128)(2,1)} %get-tuple-element.39.refs_1_), channel_id=1, source_target_pairs={{16,0},{24,8},{0,16},{8,24},{17,1},{25,9},{1,17},{9,25},{18,2},{26... | collective-permute-start | bytes 417800 | tf_op jit(solution)/shard_map/ppermute | solution.py:582
  7.2 3.0 %collective-permute-start.10 = (bf16[272,256]{1,0:T(8,128)(2,1)}, bf16[272,256]{1,0:T(8,128)(2,1)S(1)}, u32[]{:S(2)}, u32[]{:S(2)}) collective-permute-start(bf16[272,256]{1,0:T(8,128)(2,1)} %get-tuple-element.40.refs_9_.refs_0_.refs_6_), channel_id=1, source_target_pairs={{192,0},{224,32},{0,64},{32,96},{64,128},{96,160},{128,192},{160,2... | collective-permute-start | bytes 417800 | tf_op jit(solution)/shard_map/ppermute | solution.py:582
  10.2 3.0 %collective-permute-start.9 = (bf16[272,256]{1,0:T(8,128)(2,1)}, bf16[272,256]{1,0:T(8,128)(2,1)S(1)}, u32[]{:S(2)}, u32[]{:S(2)}) collective-permute-start(bf16[272,256]{1,0:T(8,128)(2,1)} %get-tuple-element.40.refs_9_.refs_0_.refs_6_), channel_id=1, source_target_pairs={{64,0},{96,32},{128,64},{160,96},{192,128},{224,160},{0,192},{32,2... | collective-permute-start | bytes 417800 | tf_op jit(solution)/shard_map/ppermute | solution.py:582
  13.6 2.3 %collective-permute-start.1 = (bf16[272,256]{1,0:T(8,128)(2,1)}, bf16[272,256]{1,0:T(8,128)(2,1)S(1)}, u32[]{:S(2)}, u32[]{:S(2)}) collective-permute-start(bf16[272,256]{1,0:T(8,128)(2,1)} %get-tuple-element.39.refs_1_), channel_id=1, source_target_pairs={{8,0},{16,8},{24,16},{0,24},{9,1},{17,9},{25,17},{1,25},{10,2},{18... | collective-permute-start | bytes 417800 | tf_op jit(solution)/shard_map/ppermute | solution.py:582
  17.1 4.5 %collective-permute-start.7 = (bf16[272,256]{1,0:T(8,128)(2,1)}, bf16[272,256]{1,0:T(8,128)(2,1)S(1)}, u32[]{:S(2)}, u32[]{:S(2)}) collective-permute-start(bf16[272,256]{1,0:T(8,128)(2,1)} %get-tuple-element.40.refs_9_.refs_0_.refs_6_), channel_id=1, source_target_pairs={{32,0},{64,32},{96,64},{128,96},{160,128},{192,160},{224,192},{0,2... | collective-permute-start | bytes 417800 | tf_op jit(solution)/shard_map/ppermute | solution.py:582
  21.6 1.7 %collective-permute-start.13 = (bf16[144,256]{1,0:T(8,128)(2,1)S(1)}, bf16[144,256]{1,0:T(8,128)(2,1)S(1)}, u32[]{:S(2)}, u32[]{:S(2)}) collective-permute-start(bf16[144,256]{1,0:T(8,128)(2,1)S(1)} %slice.8), channel_id=1, source_target_pairs={{64,0},{96,32},{128,64},{160,96},{192,128},{224,160},{0,192},{32,2... | collective-permute-start | bytes 221192 | tf_op jit(solution)/shard_map/ppermute | solution.py:582
  24.8 2.9 %collective-permute-start = (bf16[272,256]{1,0:T(8,128)(2,1)}, bf16[272,256]{1,0:T(8,128)(2,1)S(1)}, u32[]{:S(2)}, u32[]{:S(2)}) collective-permute-start(bf16[272,256]{1,0:T(8,128)(2,1)} %get-tuple-element.39.refs_1_), channel_id=1, source_target_pairs={{4,0},{0,4},{5,1},{1,5},{6,2},{2,6},{7,3},{3,7},{12,8},{8,12},{13,... | collective-permute-start | bytes 417800 | tf_op jit(solution)/shard_map/ppermute | solution.py:582
  28.1 2.3 %collective-permute-start.4 = (bf16[272,256]{1,0:T(8,128)(2,1)S(1)}, bf16[272,256]{1,0:T(8,128)(2,1)S(1)}, u32[]{:S(2)}, u32[]{:S(2)}) collective-permute-start(bf16[272,256]{1,0:T(8,128)(2,1)S(1)} %collective-permute-done.3.refs_5_), channel_id=1, source_target_pairs={{4,0},{0,4},{5,1},{1,5},{6,2},{2,6},{7,3},{3,7},{12,8},{8,12},{13,... | collective-permute-start | bytes 417800 | tf_op jit(solution)/shard_map/ppermute | solution.py:582
  31.2 3.4 %collective-permute-start.18 = (bf16[128,256]{1,0:T(8,128)(2,1)S(1)}, bf16[128,256]{1,0:T(8,128)(2,1)S(1)}, u32[]{:S(2)}, u32[]{:S(2)}) collective-permute-start(bf16[128,256]{1,0:T(8,128)(2,1)S(1)} %slice.9), channel_id=1, source_target_pairs={{192,0},{224,32},{0,64},{32,96},{64,128},{96,160},{128,192},{160,2... | collective-permute-start | bytes 196616 | tf_op jit(solution)/shard_map/ppermute | solution.py:582
  35.9 6.8 %shard_map.94 = (f32[5,3,1024]{2,1,0:T(4,128)S(1)}, f32[5,3,1024]{2,1,0:T(4,128)S(1)}, f32[8,128]{1,0:T(8,128)S(1)}, bf16[2,1024,256]{2,1,0:T(8,128)(2,1)S(1)}, ...) custom-call(s32[128]{0:T(128)S(1)} %copy-done.1, bf16[272,256]{1,0:T(8,128)(2,1)S(1)} %copy-done.2, ...), custom_call_target="tpu_custom_call" | custom-call | flops 2147483648 | bytes 4194304 | tf_op jit(solution)/shard_map/pallas_call | solution.py:633
  45.7 2.7 %shard_map.97 = (f32[3,3,1024]{2,1,0:T(4,128)S(1)}, f32[3,3,1024]{2,1,0:T(4,128)S(1)}) custom-call(s32[128]{0:T(128)S(1)} %copy-done.1, bf16[2,2,128,1024]{3,2,1,0:T(8,128)(2,1)S(1)} %get-tuple-element.42.refs_1_.refs_2_, f32[2,8,128]{2,1,0:T(8,128)S(1)} %get-tuple-element.46.refs_2_.wq_ref, ...), custom_call_target="tpu_custom_call" | custom-call | flops 2147483648 | bytes 4194304 | tf_op jit(solution)/shard_map/pallas_call | solution.py:647
  49.4 9.2 %all_to_all.15.stats_ref = f32[8,32,128]{2,1,0:T(8,128)S(1)} all-to-all(f32[8,32,128]{2,1,0:T(8,128)S(1)} %get-tuple-element.49), channel_id=1, replica_groups=mesh['z'=8,'y_hi'=2,'y_lo'=2,'core'=2,'head'=4] {'y_hi','y_lo','core'}, dimensions={0} | all-to-all | bytes 262144 | tf_op jit(solution)/shard_map/all_to_all | solution.py:659
  60.0 4.1 %all-to-all-start.1 = ((f32[8,8,128]{2,1,0:T(8,128)}), f32[8,8,128]{2,1,0:T(8,128)S(1)}, u32[]{:S(2)}, u32[]{:S(2)}) async-start(f32[8,8,128]{2,1,0:T(8,128)} %get-tuple-element.54), calls=%async_computation.1 | async-start | bytes 65536 | tf_op jit(solution)/shard_map/all_to_all | solution.py:665
  65.4 4.3 %shard_map.100 = (f32[2,128,1024]{2,1,0:T(8,128)S(1)}, bf16[272,256]{1,0:T(8,128)(2,1)S(1)}, bf16[272,256]{1,0:T(8,128)(2,1)S(1)}, bf16[128,256]{1,0:T(8,128)(2,1)S(1)}, bf16[144,256]{1,0:T(8,128)(2,1)S(1)}) custom-call(s32[128]{0:T(128)S(1)} %copy-done.1, bf16[2,1024,256]{2,1,0:T(8,128)(2,1)S(1)} %get-tuple-element.41.refs_1_, ...), custom_call_target="tpu_custom_call" | custom-call | flops 2147483648 | bytes 4194304 | tf_op jit(solution)/shard_map/pallas_call | solution.py:670
  72.7 1.7 %collective-permute-start.21 = (bf16[144,256]{1,0:T(8,128)(2,1)S(1)}, bf16[144,256]{1,0:T(8,128)(2,1)S(1)}, u32[]{:S(2)}, u32[]{:S(2)}) collective-permute-start(bf16[144,256]{1,0:T(8,128)(2,1)S(1)} %get-tuple-element.62), channel_id=1, source_target_pairs={{192,0},{224,32},{0,64},{32,96},{64,128},{96,160},{128,192},{160,2... | collective-permute-start | bytes 221192 | tf_op jit(solution)/shard_map/ppermute | solution.py:582
  74.3 2.3 %collective-permute-start.19 = (bf16[272,256]{1,0:T(8,128)(2,1)S(1)}, bf16[272,256]{1,0:T(8,128)(2,1)S(1)}, u32[]{:S(2)}, u32[]{:S(2)}) collective-permute-start(bf16[272,256]{1,0:T(8,128)(2,1)S(1)} %get-tuple-element.60), channel_id=1, source_target_pairs={{224,0},{0,32},{32,64},{64,96},{96,128},{128,160},{160,192},{192,2... | collective-permute-start | bytes 417800 | tf_op jit(solution)/shard_map/ppermute | solution.py:582
  79.4 4.6 %shard_map.102 = (f32[2,128,1024]{2,1,0:T(8,128)S(1)}, bf16[272,256]{1,0:T(8,128)(2,1)S(1)}, bf16[272,256]{1,0:T(8,128)(2,1)S(1)}, bf16[272,256]{1,0:T(8,128)(2,1)S(1)}) custom-call(s32[128]{0:T(128)S(1)} %copy-done.1, bf16[2,1024,256]{2,1,0:T(8,128)(2,1)S(1)} %get-tuple-element.41.refs_1_, bf16[2,2,128,1024]{3,2,1,0:T(8,128)(2,1)S(1)} %copy-done.5, ...), custom_call_target="tpu_custom_call" | custom-call | flops 2147483648 | bytes 4194304 | tf_op jit(solution)/shard_map/pallas_call | solution.py:670
  84.1 4.2 %shard_map.103 = (bf16[8,256,128]{2,1,0:T(8,128)(2,1)}, bf16[272,256]{1,0:T(8,128)(2,1)S(1)}, bf16[272,256]{1,0:T(8,128)(2,1)S(1)}) custom-call(s32[128]{0:T(128)S(1)} %copy-done.1, bf16[2,1024,256]{2,1,0:T(8,128)(2,1)S(1)} %get-tuple-element.41.refs_1_, bf16[2,2,128,1024]{3,2,1,0:T(8,128)(2,1)S(1)} %copy-done.5, ...), custom_call_target="tpu_custom_call" | custom-call | flops 2147483648 | bytes 4194304 | tf_op jit(solution)/shard_map/pallas_call | solution.py:670
  88.3 5.7 %all-to-all-start.2 = ((bf16[8,256,128]{2,1,0:T(8,128)(2,1)}), bf16[8,256,128]{2,1,0:T(8,128)(2,1)S(1)}, u32[]{:S(2)}, u32[]{:S(2)}) async-start(bf16[8,256,128]{2,1,0:T(8,128)(2,1)} %get-tuple-element.64), calls=%async_computation.2 | async-start | bytes 1048576 | tf_op jit(solution)/shard_map/all_to_all | solution.py:706
  98.0 2.2 %collective-permute-start.26 = (bf16[272,256]{1,0:T(8,128)(2,1)S(1)}, bf16[272,256]{1,0:T(8,128)(2,1)S(1)}, u32[]{:S(2)}, u32[]{:S(2)}) collective-permute-start(bf16[272,256]{1,0:T(8,128)(2,1)S(1)} %get-tuple-element.69), channel_id=1, source_target_pairs={{64,0},{96,32},{128,64},{160,96},{192,128},{224,160},{0,192},{32,2... | collective-permute-start | bytes 417800 | tf_op jit(solution)/shard_map/ppermute | solution.py:582
  100.5 3.9 %collective-permute-done.25.p3 = bf16[272,256]{1,0:T(8,128)(2,1)S(1)} collective-permute-done((bf16[272,256]{1,0:T(8,128)(2,1)S(1)}, bf16[272,256]{1,0:T(8,128)(2,1)S(1)}, u32[]{:S(2)}, u32[]{:S(2)}) %collective-permute-start.25) | collective-permute-done | bytes 139296 | tf_op jit(solution)/shard_map/ppermute | solution.py:582
  104.4 3.2 %collective-permute-done.26.p4 = bf16[272,256]{1,0:T(8,128)(2,1)S(1)} collective-permute-done((bf16[272,256]{1,0:T(8,128)(2,1)S(1)}, bf16[272,256]{1,0:T(8,128)(2,1)S(1)}, u32[]{:S(2)}, u32[]{:S(2)}) %collective-permute-start.26) | collective-permute-done | bytes 139296 | tf_op jit(solution)/shard_map/ppermute | solution.py:582
  107.5 1.8 %shard_map.104 = (bf16[256,128]{1,0:T(8,128)(2,1)}, bf16[256,128]{1,0:T(8,128)(2,1)}, bf16[256,128]{1,0:T(8,128)(2,1)}, f32[1,256]{1,0:T(1,128)}) custom-call(s32[128]{0:T(128)S(1)} %copy-done.1, bf16[8,256,128]{2,1,0:T(8,128)(2,1)S(1)} %all-to-all-done.2.dq_parts, bf16[272,256]{1,0:T(8,128)(2,1)S(1)} %get-tuple-element.65.p0, ...), custom_call_target="tpu_custom_call" | custom-call | bytes 4194304 | tf_op jit(solution)/shard_map/pallas_call | solution.py:708
  (66 shorter events, 22.1 us)
Async XLA Ops:
  3.3 12.5 %collective-permute-start.5 = (bf16[272,256]{1,0:T(8,128)(2,1)}, bf16[272,256]{1,0:T(8,128)(2,1)S(1)}, u32[]{:S(2)}, u32[]{:S(2)}) collective-permute-start(bf16[272,256]{1,0:T(8,128)(2,1)} %get-tuple-element.39.refs_1_), channel_id=1, source_target_pairs={{16,0},{24,8},{0,16},{8,24},{17,1},{25,9},{1,17},{9,25},{18,2},{26... | collective-permute-start | bytes 417800 | tf_op jit(solution)/shard_map/ppermute | solution.py:582
  7.2 10.0 %collective-permute-start.10 = (bf16[272,256]{1,0:T(8,128)(2,1)}, bf16[272,256]{1,0:T(8,128)(2,1)S(1)}, u32[]{:S(2)}, u32[]{:S(2)}) collective-permute-start(bf16[272,256]{1,0:T(8,128)(2,1)} %get-tuple-element.40.refs_9_.refs_0_.refs_6_), channel_id=1, source_target_pairs={{192,0},{224,32},{0,64},{32,96},{64,128},{96,160},{128,192},{160,2... | collective-permute-start | bytes 417800 | tf_op jit(solution)/shard_map/ppermute | solution.py:582
  10.2 11.5 %collective-permute-start.9 = (bf16[272,256]{1,0:T(8,128)(2,1)}, bf16[272,256]{1,0:T(8,128)(2,1)S(1)}, u32[]{:S(2)}, u32[]{:S(2)}) collective-permute-start(bf16[272,256]{1,0:T(8,128)(2,1)} %get-tuple-element.40.refs_9_.refs_0_.refs_6_), channel_id=1, source_target_pairs={{64,0},{96,32},{128,64},{160,96},{192,128},{224,160},{0,192},{32,2... | collective-permute-start | bytes 417800 | tf_op jit(solution)/shard_map/ppermute | solution.py:582
  13.2 8.4 %collective-permute-start.3 = (bf16[272,256]{1,0:T(8,128)(2,1)}, bf16[272,256]{1,0:T(8,128)(2,1)S(1)}, u32[]{:S(2)}, u32[]{:S(2)}) collective-permute-start(bf16[272,256]{1,0:T(8,128)(2,1)} %get-tuple-element.39.refs_1_), channel_id=1, source_target_pairs={{24,0},{0,8},{8,16},{16,24},{25,1},{1,9},{9,17},{17,25},{26,2},{2,... | collective-permute-start | bytes 417800 | tf_op jit(solution)/shard_map/ppermute | solution.py:582
  13.6 9.8 %collective-permute-start.1 = (bf16[272,256]{1,0:T(8,128)(2,1)}, bf16[272,256]{1,0:T(8,128)(2,1)S(1)}, u32[]{:S(2)}, u32[]{:S(2)}) collective-permute-start(bf16[272,256]{1,0:T(8,128)(2,1)} %get-tuple-element.39.refs_1_), channel_id=1, source_target_pairs={{8,0},{16,8},{24,16},{0,24},{9,1},{17,9},{25,17},{1,25},{10,2},{18... | collective-permute-start | bytes 417800 | tf_op jit(solution)/shard_map/ppermute | solution.py:582
  15.9 9.0 %collective-permute-start.8 = (bf16[272,256]{1,0:T(8,128)(2,1)}, bf16[272,256]{1,0:T(8,128)(2,1)S(1)}, u32[]{:S(2)}, u32[]{:S(2)}) collective-permute-start(bf16[272,256]{1,0:T(8,128)(2,1)} %get-tuple-element.40.refs_9_.refs_0_.refs_6_), channel_id=1, source_target_pairs={{224,0},{0,32},{32,64},{64,96},{96,128},{128,160},{160,192},{192,2... | collective-permute-start | bytes 417800 | tf_op jit(solution)/shard_map/ppermute | solution.py:582
  17.1 10.6 %collective-permute-start.7 = (bf16[272,256]{1,0:T(8,128)(2,1)}, bf16[272,256]{1,0:T(8,128)(2,1)S(1)}, u32[]{:S(2)}, u32[]{:S(2)}) collective-permute-start(bf16[272,256]{1,0:T(8,128)(2,1)} %get-tuple-element.40.refs_9_.refs_0_.refs_6_), channel_id=1, source_target_pairs={{32,0},{64,32},{96,64},{128,96},{160,128},{192,160},{224,192},{0,2... | collective-permute-start | bytes 417800 | tf_op jit(solution)/shard_map/ppermute | solution.py:582
  21.6 8.8 %collective-permute-start.12 = (bf16[272,256]{1,0:T(8,128)(2,1)S(1)}, bf16[272,256]{1,0:T(8,128)(2,1)S(1)}, u32[]{:S(2)}, u32[]{:S(2)}) collective-permute-start(bf16[272,256]{1,0:T(8,128)(2,1)S(1)} %collective-permute-done.10.refs_13_.refs_4_.refs_7_), channel_id=1, source_target_pairs={{224,0},{0,32},{32,64},{64,96},{96,128},{128,160},{160,192},{192,2... | collective-permute-start | bytes 417800 | tf_op jit(solution)/shard_map/ppermute | solution.py:582
  21.6 6.5 %collective-permute-start.13 = (bf16[144,256]{1,0:T(8,128)(2,1)S(1)}, bf16[144,256]{1,0:T(8,128)(2,1)S(1)}, u32[]{:S(2)}, u32[]{:S(2)}) collective-permute-start(bf16[144,256]{1,0:T(8,128)(2,1)S(1)} %slice.8), channel_id=1, source_target_pairs={{64,0},{96,32},{128,64},{160,96},{192,128},{224,160},{0,192},{32,2... | collective-permute-start | bytes 221192 | tf_op jit(solution)/shard_map/ppermute | solution.py:582
  23.4 7.8 %collective-permute-start.11 = (bf16[272,256]{1,0:T(8,128)(2,1)S(1)}, bf16[272,256]{1,0:T(8,128)(2,1)S(1)}, u32[]{:S(2)}, u32[]{:S(2)}) collective-permute-start(bf16[272,256]{1,0:T(8,128)(2,1)S(1)} %collective-permute-done.9.refs_12_.refs_3_.refs_6_), channel_id=1, source_target_pairs={{32,0},{64,32},{96,64},{128,96},{160,128},{192,160},{224,192},{0,2... | collective-permute-start | bytes 417800 | tf_op jit(solution)/shard_map/ppermute | solution.py:582
  24.8 10.0 %collective-permute-start = (bf16[272,256]{1,0:T(8,128)(2,1)}, bf16[272,256]{1,0:T(8,128)(2,1)S(1)}, u32[]{:S(2)}, u32[]{:S(2)}) collective-permute-start(bf16[272,256]{1,0:T(8,128)(2,1)} %get-tuple-element.39.refs_1_), channel_id=1, source_target_pairs={{4,0},{0,4},{5,1},{1,5},{6,2},{2,6},{7,3},{3,7},{12,8},{8,12},{13,... | collective-permute-start | bytes 417800 | tf_op jit(solution)/shard_map/ppermute | solution.py:582
  27.8 8.1 %collective-permute-start.6 = (bf16[272,256]{1,0:T(8,128)(2,1)S(1)}, bf16[272,256]{1,0:T(8,128)(2,1)S(1)}, u32[]{:S(2)}, u32[]{:S(2)}) collective-permute-start(bf16[272,256]{1,0:T(8,128)(2,1)S(1)} %collective-permute-done.5.refs_7_), channel_id=1, source_target_pairs={{4,0},{0,4},{5,1},{1,5},{6,2},{2,6},{7,3},{3,7},{12,8},{8,12},{13,... | collective-permute-start | bytes 417800 | tf_op jit(solution)/shard_map/ppermute | solution.py:582
  28.1 7.7 %collective-permute-start.4 = (bf16[272,256]{1,0:T(8,128)(2,1)S(1)}, bf16[272,256]{1,0:T(8,128)(2,1)S(1)}, u32[]{:S(2)}, u32[]{:S(2)}) collective-permute-start(bf16[272,256]{1,0:T(8,128)(2,1)S(1)} %collective-permute-done.3.refs_5_), channel_id=1, source_target_pairs={{4,0},{0,4},{5,1},{1,5},{6,2},{2,6},{7,3},{3,7},{12,8},{8,12},{13,... | collective-permute-start | bytes 417800 | tf_op jit(solution)/shard_map/ppermute | solution.py:582
  31.2 14.5 %collective-permute-start.18 = (bf16[128,256]{1,0:T(8,128)(2,1)S(1)}, bf16[128,256]{1,0:T(8,128)(2,1)S(1)}, u32[]{:S(2)}, u32[]{:S(2)}) collective-permute-start(bf16[128,256]{1,0:T(8,128)(2,1)S(1)} %slice.9), channel_id=1, source_target_pairs={{192,0},{224,32},{0,64},{32,96},{64,128},{96,160},{128,192},{160,2... | collective-permute-start | bytes 196616 | tf_op jit(solution)/shard_map/ppermute | solution.py:582
  34.8 7.9 %collective-permute-start.14 = (f32[8,128]{1,0:T(8,128)S(1)}, f32[8,128]{1,0:T(8,128)S(1)}, u32[]{:S(2)}, u32[]{:S(2)}) collective-permute-start(f32[8,128]{1,0:T(8,128)S(1)} %shard_map.96), channel_id=1, source_target_pairs={{4,0},{0,4},{5,1},{1,5},{6,2},{2,6},{7,3},{3,7},{12,8},{8,12},{13,... | collective-permute-start | bytes 12296 | tf_op jit(solution)/shard_map/ppermute | solution.py:582
  60.0 11.9 %all-to-all-start.1 = ((f32[8,8,128]{2,1,0:T(8,128)}), f32[8,8,128]{2,1,0:T(8,128)S(1)}, u32[]{:S(2)}, u32[]{:S(2)}) async-start(f32[8,8,128]{2,1,0:T(8,128)} %get-tuple-element.54), calls=%async_computation.1 | async-start | bytes 65536 | tf_op jit(solution)/shard_map/all_to_all | solution.py:665
  70.7 13.3 %collective-permute-start.22 = (bf16[128,256]{1,0:T(8,128)(2,1)S(1)}, bf16[128,256]{1,0:T(8,128)(2,1)S(1)}, u32[]{:S(2)}, u32[]{:S(2)}) collective-permute-start(bf16[128,256]{1,0:T(8,128)(2,1)S(1)} %get-tuple-element.63), channel_id=1, source_target_pairs={{64,0},{96,32},{128,64},{160,96},{192,128},{224,160},{0,192},{32,2... | collective-permute-start | bytes 196616 | tf_op jit(solution)/shard_map/ppermute | solution.py:582
  72.7 11.4 %collective-permute-start.21 = (bf16[144,256]{1,0:T(8,128)(2,1)S(1)}, bf16[144,256]{1,0:T(8,128)(2,1)S(1)}, u32[]{:S(2)}, u32[]{:S(2)}) collective-permute-start(bf16[144,256]{1,0:T(8,128)(2,1)S(1)} %get-tuple-element.62), channel_id=1, source_target_pairs={{192,0},{224,32},{0,64},{32,96},{64,128},{96,160},{128,192},{160,2... | collective-permute-start | bytes 221192 | tf_op jit(solution)/shard_map/ppermute | solution.py:582
  74.3 9.7 %collective-permute-start.19 = (bf16[272,256]{1,0:T(8,128)(2,1)S(1)}, bf16[272,256]{1,0:T(8,128)(2,1)S(1)}, u32[]{:S(2)}, u32[]{:S(2)}) collective-permute-start(bf16[272,256]{1,0:T(8,128)(2,1)S(1)} %get-tuple-element.60), channel_id=1, source_target_pairs={{224,0},{0,32},{32,64},{64,96},{96,128},{128,160},{160,192},{192,2... | collective-permute-start | bytes 417800 | tf_op jit(solution)/shard_map/ppermute | solution.py:582
  76.6 7.4 %collective-permute-start.20 = (bf16[272,256]{1,0:T(8,128)(2,1)S(1)}, bf16[272,256]{1,0:T(8,128)(2,1)S(1)}, u32[]{:S(2)}, u32[]{:S(2)}) collective-permute-start(bf16[272,256]{1,0:T(8,128)(2,1)S(1)} %get-tuple-element.61), channel_id=1, source_target_pairs={{32,0},{64,32},{96,64},{128,96},{160,128},{192,160},{224,192},{0,2... | collective-permute-start | bytes 417800 | tf_op jit(solution)/shard_map/ppermute | solution.py:582
  88.3 19.3 %all-to-all-start.2 = ((bf16[8,256,128]{2,1,0:T(8,128)(2,1)}), bf16[8,256,128]{2,1,0:T(8,128)(2,1)S(1)}, u32[]{:S(2)}, u32[]{:S(2)}) async-start(bf16[8,256,128]{2,1,0:T(8,128)(2,1)} %get-tuple-element.64), calls=%async_computation.2 | async-start | bytes 1048576 | tf_op jit(solution)/shard_map/all_to_all | solution.py:706
  94.0 6.5 %collective-permute-start.23 = (bf16[272,256]{1,0:T(8,128)(2,1)S(1)}, bf16[272,256]{1,0:T(8,128)(2,1)S(1)}, u32[]{:S(2)}, u32[]{:S(2)}) collective-permute-start(bf16[272,256]{1,0:T(8,128)(2,1)S(1)} %get-tuple-element.66), channel_id=1, source_target_pairs={{224,0},{0,32},{32,64},{64,96},{96,128},{128,160},{160,192},{192,2... | collective-permute-start | bytes 417800 | tf_op jit(solution)/shard_map/ppermute | solution.py:582
  96.7 7.7 %collective-permute-start.25 = (bf16[272,256]{1,0:T(8,128)(2,1)S(1)}, bf16[272,256]{1,0:T(8,128)(2,1)S(1)}, u32[]{:S(2)}, u32[]{:S(2)}) collective-permute-start(bf16[272,256]{1,0:T(8,128)(2,1)S(1)} %get-tuple-element.68), channel_id=1, source_target_pairs={{192,0},{224,32},{0,64},{32,96},{64,128},{96,160},{128,192},{160,2... | collective-permute-start | bytes 417800 | tf_op jit(solution)/shard_map/ppermute | solution.py:582
  98.0 9.5 %collective-permute-start.26 = (bf16[272,256]{1,0:T(8,128)(2,1)S(1)}, bf16[272,256]{1,0:T(8,128)(2,1)S(1)}, u32[]{:S(2)}, u32[]{:S(2)}) collective-permute-start(bf16[272,256]{1,0:T(8,128)(2,1)S(1)} %get-tuple-element.69), channel_id=1, source_target_pairs={{64,0},{96,32},{128,64},{160,96},{192,128},{224,160},{0,192},{32,2... | collective-permute-start | bytes 417800 | tf_op jit(solution)/shard_map/ppermute | solution.py:582
  (13 other events, 91.7 us)

commit v3 on v2

--- a/solution.py
+++ b/solution.py
@@ -99,7 +99,7 @@
 
 
 def pack_kernel(
-    span_ref, q_ref, k_ref, v_ref, g_ref, f_ref, qg_ref, kv_ref, qg, kv, sems
+    span_ref, q_ref, k_ref, v_ref, g_ref, f_ref, qg_ref, kv_ref, ids_ref, qg, kv, sems
 ):
     swap = own_swap(span_ref)
     copies = []
@@ -117,11 +117,18 @@
     for copy in copies:
         copy.start()
     gates = [f_ref[0:1, 0:HALF], f_ref[0:1, HALF:ROWS]]
+    gates = [jnp.where(swap == 1, gates[1 - half], gates[half]) for half in range(2)]
+    gates = running_sum(jnp.concatenate(gates, 0))
     for half in range(2):
-        gate = running_sum(jnp.where(swap == 1, gates[1 - half], gates[half]))
-        rows = split_rows(gate).astype(BF16)
+        rows = split_rows(gates[half : half + 1, :]).astype(BF16)
         qg[ROWS:PACK, HALF * half : HALF * (half + 1)] = rows
         kv[ROWS:PACK, HALF * half : HALF * (half + 1)] = rows
+    ids = jnp.zeros((GROUP, HALF), jnp.int32)
+    for z in range(GROUP):
+        for b in range(GROUP):
+            low = slot_low(span_ref, z * GROUP + b)
+            ids = table_lanes(ids, z, b, low, 127 - low)
+    ids_ref[...] = ids
     for copy in copies:
         copy.wait()
     run_copies([(kv, kv_ref), (qg, qg_ref)], sems)
@@ -143,6 +150,22 @@
     out_ref[...] = table
 
 
+def totals_kernel(*refs):
+    blocks, out_ref, aux, sems = refs[:8], refs[8], refs[9], refs[10]
+    z, _, _, own = place_of()
+    copies = []
+    for at, block in enumerate(blocks):
+        last = block.shape[0] - AUX
+        copies.append((block.at[pl.ds(last, AUX), :], aux.at[at]))
+    run_copies(copies, sems)
+    table = jnp.zeros((GROUP, HALF), F32)
+    for e in range(GROUP):
+        row = join_rows(aux[e])
+        ends = [row[:, HALF * (half + 1) - 1 : HALF * (half + 1)] for half in range(2)]
+        table = table_lanes(table, near_z(z, e), own, *ends)
+    out_ref[...] = table
+
+
 def ids_kernel(span_ref, out_ref):
     table = jnp.zeros((GROUP, HALF), jnp.int32)
     for z in range(GROUP):
@@ -160,22 +183,16 @@
         copy.wait()
 
 
-def key_copies(key_refs, ks):
-    copies, at = [], 0
-    for ref in key_refs:
-        if ref.shape[0] == HALF + AUX:
-            copies.append((ref, ks.at[at, pl.ds(HALF, HALF + AUX), :]))
-        elif ref.shape[0] == HALF:
-            copies.append((ref, ks.at[at, pl.ds(0, HALF), :]))
-            at += 1
-        else:
-            copies.append((ref, ks.at[at]))
-            at += 1
-    return copies
+def whole_keys(key_refs, last):
+    if len(key_refs) == 4:
+        last[HALF:PACK, :] = key_refs[2][...]
+        last[0:HALF, :] = key_refs[3][...]
+        return [*key_refs[:2], last]
+    return key_refs
 
 
 def gate_columns(ks, e, columns):
-    row = join_rows(ks[e, ROWS:PACK, :]) * LOG2E
+    row = join_rows(ks[e][ROWS:PACK, :]) * LOG2E
     for half in range(2):
         part = row[:, HALF * half : HALF * (half + 1)]
         columns[half] = jnp.transpose(jnp.broadcast_to(part, (HALF, HALF)))
@@ -207,13 +224,13 @@
         qt, wq = refs[:2]
         rest, refs = refs[2:], ()
         count = 3
-        key_refs, (one_ref, two_ref), (ks, columns, sems) = rest[:4], rest[4:6], rest[6:]
-        run_copies(key_copies(key_refs, ks), sems)
+        key_refs, (one_ref, two_ref), (last, columns) = rest[:4], rest[4:6], rest[6:]
+        ks = whole_keys(key_refs, last)
     else:
         count = 5
-        query_refs, key_refs = refs[:8], refs[8:13]
-        one_ref, two_ref, own_ref, qs, qt, wq, ks, columns, gates, sems = refs[13:]
-        run_copies(load_queries(query_refs, y, core, qs, gates) + key_copies(key_refs, ks), sems)
+        query_refs, ks = refs[:8], refs[8:13]
+        one_ref, two_ref, own_ref, qs, qt, wq, columns, gates, sems = refs[13:]
+        run_copies(load_queries(query_refs, y, core, qs, gates), sems)
         for d in range(GROUP):
             rows = slice(HALF * d, HALF * (d + 1))
             row = join_rows(gates[d]) * LOG2E
@@ -237,7 +254,7 @@
     for e in range(count):
         gate_columns(ks, e, columns)
         key_span = slot_low(span_ref, near_z(z, first + e) * GROUP + own)
-        key_low, value_low = ks[e, 0:HALF, 0:HALF], ks[e, 0:HALF, HALF:ROWS]
+        key_low, value_low = ks[e][0:HALF, 0:HALF], ks[e][0:HALF, HALF:ROWS]
         column = columns[0]
         column2 = jnp.concatenate([column, column], 1)
         for pair in range(GROUP // 2):
@@ -250,19 +267,19 @@
         for d in range(GROUP):
             half = (key_span > lows[d]).astype(jnp.int32)
             rows, lanes = half_rows(half), slice(HALF * d, HALF * (d + 1))
-            scores = dot(ks[e, rows, 0:HALF], qt[0, half, :, lanes], 1, 0) * scale + (
+            scores = dot(ks[e][rows, 0:HALF], qt[0, half, :, lanes], 1, 0) * scale + (
                 wq[half, d : d + 1, :] - columns[half]
             )
             if first + e == 0:
                 scores = jnp.where(ahead <= jnp.where(own == d, 0, HALF), scores, NEG)
-            upstream = dot(ks[e, rows, HALF:ROWS], qt[1, half, :, lanes], 1, 0)
+            upstream = dot(ks[e][rows, HALF:ROWS], qt[1, half, :, lanes], 1, 0)
             for at, row in enumerate(tile_stats(scores, upstream)):
                 two_ref[e, at : at + 1, lanes] = row
         if first + e == 0:
             w, lanes = wq[1, pl.ds(own, 1), :], lanes_of(own)
-            scores = dot(ks[0, HALF:ROWS, 0:HALF], qt[0, 1, :, lanes], 1, 0) * scale
+            scores = dot(ks[0][HALF:ROWS, 0:HALF], qt[0, 1, :, lanes], 1, 0) * scale
             scores = jnp.where(ahead <= 0, scores + (w - columns[1]), NEG)
-            upstream = dot(ks[0, HALF:ROWS, HALF:ROWS], qt[1, 1, :, lanes], 1, 0)
+            upstream = dot(ks[0][HALF:ROWS, HALF:ROWS], qt[1, 1, :, lanes], 1, 0)
             for at, row in enumerate(tile_stats(scores, upstream)):
                 own_ref[at : at + 1, :] = row
 
@@ -421,20 +438,22 @@
     z, y, core, own = place_of()
     key_refs, refs = refs[:pieces], refs[pieces:]
     if first == 5:
-        dqt, refs = refs[0], refs[1:]
+        dqt_out, refs = refs[0], refs[1:]
+        outs, scratch = refs[:4], refs[4:]
+        dqt, scratch = scratch[0], scratch[1:]
         dqt[...] = jnp.zeros_like(dqt)
-        outs, scratch = refs[:4], refs[4:]
     elif first == 0:
-        before, beyond, dqt, refs = refs[0], refs[1], refs[2], refs[3:]
-        dqt[...] = before[...]
+        before, beyond, dqt_out, refs = refs[0], refs[1], refs[2], refs[3:]
         outs, scratch = refs[:3], refs[3:]
+        dqt, scratch = scratch[0], scratch[1:]
+        dqt[...] = before[...].astype(F32)
     else:
         before, beyond, up3, down3, up4, down4, dq_ref = refs[:7]
         outs, scratch = refs[7:9], refs[9:]
         dqt, scratch = scratch[0], scratch[1:]
-        dqt[...] = before[...]
-    ks, columns, pg, sems = scratch
-    run_copies(key_copies(key_refs, ks), sems)
+        dqt[...] = before[...].astype(F32)
+    last, columns, pg = scratch
+    ks = whole_keys(key_refs, last)
     ahead = ahead_of()
     inverse = 1.0 / math.sqrt(HALF)
     lows = [slot_low(span_ref, z * GROUP + d) for d in range(GROUP)]
@@ -447,8 +466,8 @@
         number = first + e
         gate_columns(ks, e, columns)
         key_span = slot_low(span_ref, near_z(z, number) * GROUP + own)
-        key_low, value_low = ks[e, 0:HALF, 0:HALF], ks[e, 0:HALF, HALF:ROWS]
-        turned = jnp.transpose(ks[e, :ROWS, 0:HALF])
+        key_low, value_low = ks[e][0:HALF, 0:HALF], ks[e][0:HALF, HALF:ROWS]
+        turned = jnp.transpose(ks[e][0:ROWS, 0:HALF])
         column = columns[0]
         column2 = jnp.concatenate([column, column], 1)
         place = place_ref[number : number + 1, :]
@@ -471,11 +490,11 @@
             rows, lanes = half_rows(half), slice(HALF * d, HALF * (d + 1))
             chosen.append(qs[half, lanes, :])
             w = query_gate(half, d, place_ref[pl.ds(8 * half + number, 1), :])
-            scores = dot(ks[e, rows, 0:HALF], qt[0, half, :, lanes], 1, 0) * scale
+            scores = dot(ks[e][rows, 0:HALF], qt[0, half, :, lanes], 1, 0) * scale
             probs = jnp.exp2(scores + (w - columns[half]))
             if number == 0:
                 probs = jnp.where(ahead <= jnp.where(own == d, 0, HALF), probs, 0.0)
-            upstream = dot(ks[e, rows, HALF:ROWS], qt[1, half, :, lanes], 1, 0)
+            upstream = dot(ks[e][rows, HALF:ROWS], qt[1, half, :, lanes], 1, 0)
             grads = probs * (upstream - delta_ref[half, d : d + 1, :])
             pg[half] += grads
             probs, grads = probs.astype(BF16), grads.astype(BF16)
@@ -504,10 +523,10 @@
             dqt[0, :, lanes] += dot(turned[:, 0:HALF], side_grads[0][:, lanes], 1, 0)
         if number == 0:
             lanes = lanes_of(own)
-            scores = dot(ks[e, HALF:ROWS, 0:HALF], qt[0, 1, :, lanes], 1, 0) * scale
+            scores = dot(ks[e][HALF:ROWS, 0:HALF], qt[0, 1, :, lanes], 1, 0) * scale
             probs = jnp.exp2(scores + (gate_ref[1, pl.ds(own, 1), :] - columns[1]))
             probs = jnp.where(ahead <= 0, probs, 0.0)
-            upstream = dot(ks[e, HALF:ROWS, HALF:ROWS], qt[1, 1, :, lanes], 1, 0)
+            upstream = dot(ks[e][HALF:ROWS, HALF:ROWS], qt[1, 1, :, lanes], 1, 0)
             grads = probs * (upstream - delta_ref[1, pl.ds(own, 1), :])
             low_grads, block = grads.astype(BF16), qs[1, lanes_of(own), :]
             dv[1] = dv[1] + dot(probs.astype(BF16), block[:, HALF:ROWS], 1, 0)
@@ -541,7 +560,9 @@
             aux_base = HALF if number == 7 else ROWS
             aux_out[aux_base : aux_base + AUX, rows] = split_rows(row).astype(BF16)
 
-    if first == 3:
+    if first != 3:
+        dqt_out[...] = dqt[...].astype(BF16)
+    else:
         for d in range(GROUP):
             for half in range(2):
                 part = jnp.transpose(dqt[half, :, HALF * d : HALF * (d + 1)]) * inverse
@@ -571,11 +592,12 @@
         row = join_rows(p0[ROWS:PACK, rows])
         for part in parts[1:]:
             row = row + join_rows(part[ROWS:PACK, rows])
-        total = jnp.sum(row, axis=1, keepdims=True)
-        halves.append(total - running_sum(row) + row)
+        halves.append(row)
+    both = jnp.concatenate(halves, 0)
+    both = jnp.sum(both, axis=1, keepdims=True) - running_sum(both) + both
     for half in range(2):
         lanes = slice(HALF * half, HALF * (half + 1))
-        f_ref[:, lanes] = jnp.where(swap == 1, halves[1 - half], halves[half])
+        f_ref[:, lanes] = jnp.where(swap == 1, both[1 - half : 2 - half, :], both[half : half + 1, :])
 
 
 def fetch(x, axis, size, offset):
@@ -590,15 +612,14 @@
 
     block = struct((PACK, ROWS), BF16)
     table = struct((GROUP, HALF), F32)
-    qg, kv = call(
+    qg, kv, ids = call(
         pack_kernel,
-        (block, block),
+        (block, block, struct((GROUP, HALF), jnp.int32)),
         [smem] + [hbm] * 4 + [vmem],
         [pltpu.VMEM((PACK, ROWS), BF16)] * 2 + [pltpu.SemaphoreType.DMA((8,))],
-        out_spec=(hbm, hbm),
+        out_spec=(hbm, hbm, vmem),
         limit=62 * 1024 * 1024,
     )(span_order, queries[0], key_vectors[0], value_vectors[0], out_grad[0], log_forget)
-    ids = call(ids_kernel, struct((GROUP, HALF), jnp.int32), [smem])(span_order)
     up1, down1, up2, down2 = [fetch(kv, Z, 8, o) for o in (1, -1, 2, -2)]
     mine = [qg] + [fetch(qg, Y, 4, o) for o in (1, -1, 2)]
     up3, down3 = fetch(up2, Z, 8, 1), fetch(down2, Z, 8, -1)
@@ -617,14 +638,6 @@
     )(*near_keys, *far_keys[:3])
     totals = totals + fetch(totals, C, 2, 1)
     totals = [totals] + [fetch(totals, Y, 4, o) for o in (1, -1, 2)]
-
-    def key_scratch(count, sems, more=()):
-        return [
-            pltpu.VMEM((count, PACK, ROWS), BF16),
-            pltpu.VMEM((2, HALF, HALF), F32),
-            *more,
-            pltpu.SemaphoreType.DMA((sems,)),
-        ]
 
     def tiles(count):
         return struct((count, 3, GROUP * HALF), F32)
@@ -640,15 +653,19 @@
             struct((2, 2, HALF, GROUP * HALF), BF16),
             gates,
         ),
-        [smem] + [hbm] * 13,
-        key_scratch(5, 29, [pltpu.VMEM((GROUP, AUX, ROWS), BF16)]),
+        [smem] + [hbm] * 8 + [vmem] * 5,
+        [
+            pltpu.VMEM((2, HALF, HALF), F32),
+            pltpu.VMEM((GROUP, AUX, ROWS), BF16),
+            pltpu.SemaphoreType.DMA((24,)),
+        ],
         flops=1 << 31,
     )(span_order, *query_blocks, *near_keys)
     far1, far2 = call(
         lambda *refs: stats_kernel(scale, 5, *refs),
         (tiles(3), tiles(3)),
-        [smem, vmem, vmem] + [hbm] * 4,
-        key_scratch(3, 4),
+        [smem] + [vmem] * 6,
+        [pltpu.VMEM((PACK, ROWS), BF16), pltpu.VMEM((2, HALF, HALF), F32)],
         flops=1 << 31,
     )(span_order, qt, wq, *far_keys)
     stats, place = call(
@@ -664,19 +681,18 @@
     )(span_order, stats, place, wq, near1, near2, own, far1, far2)
     span_grads = lax.all_to_all(span_grads, COLUMN, 0, 0, tiled=True)
     square = pltpu.VMEM((2, HALF, HALF), F32)
-    sum_t = struct((2, HALF, GROUP * HALF), F32)
-
-    def grads(first, count, keys, more, outs, extra=()):
+    sum_t = struct((2, HALF, GROUP * HALF), BF16)
+
+    def grads(first, count, keys, more, outs):
         return call(
             lambda *refs: grads_kernel(scale, first, count, len(keys), *refs),
             outs,
-            [smem] + [vmem] * 5 + [hbm] * len(keys) + [vmem] * len(more),
-            list(extra)
-            + [
-                pltpu.VMEM((count, PACK, ROWS), BF16),
+            [smem] + [vmem] * (5 + len(keys) + len(more)),
+            [
+                pltpu.VMEM((2, HALF, GROUP * HALF), F32),
+                pltpu.VMEM((PACK, ROWS), BF16),
                 square,
                 square,
-                pltpu.SemaphoreType.DMA((len(keys),)),
             ],
             flops=1 << 31,
         )(span_order, qs, qt, gate, delta, place, *keys, *more)
@@ -700,7 +716,6 @@
         near_keys[3:],
         [dqt, beyond, arrived_up3, arrived_down3, arrived_up4, arrived_down4],
         (struct((GROUP, ROWS, HALF), BF16), block, block),
-        [pltpu.VMEM((2, HALF, GROUP * HALF), F32)],
     )
     arrived2, arrived2d = fetch(part2, Z, 8, -2), fetch(part2d, Z, 8, 2)
     dq_parts = lax.all_to_all(dq_parts, COLUMN, 0, 0, tiled=True)

time: 110 us -> 106 us (0.964)
  Pallas kernels: 31.1 us -> 27.7 us
  local copies, waits for them, and re-layouts: 4.7 us -> 3.16 us
    pallas_call x3, Pallas kernels: 13.1 us -> 11.5 us  [grads(): call(lambda *refs: grads_kernel(scale, first, count, len(keys), *refs), o...]
    unnamed x16 -> x14, local copies, waits for them, and re-layouts: 4.68 us -> 3.15 us
    pallas_call x1, Pallas kernels: 6.83 us -> 5.68 us  [local(): call(lambda *refs: stats_kernel(scale, 0, *refs), (tiles(5), tiles(5), st...]
    pallas_call x2 -> x1, Pallas kernels: 3.37 us -> 3.34 us  [local(): call(pack_kernel, (block, block, struct((GROUP, HALF), jnp.int32)), [smem...]
  transfers between devices with their start and end apart: 29 -> 29, of which waited for: 4 -> 5; matrix products, arithmetic and copies ran while one was open for 0% -> 0% of each run, Pallas kernels for 18% -> 16%
where the time goes in v3:
time: 106 us
  starting transfers between devices  56.1 us (53%)
  Pallas kernels  27.7 us (26%)
  blocking collectives  9.77 us (9%)
  waiting for transfers between devices  8.41 us (8%)
  local copies, waits for them, and re-layouts  3.16 us (3%)
    ppermute x27, starting transfers between devices, fetch(): lax.ppermute(x, axis, [((i + offset) % size, i) for i in range(size)])  46.4 us
    pallas_call x3, Pallas kernels, grads(): call(lambda *refs: grads_kernel(scale, first, count, len(keys), *refs), o...  11.5 us
    all_to_all x1, blocking collectives, local(): stats = lax.all_to_all(stats, COLUMN, 0, 0, tiled=True)  9.77 us
    ppermute x27, waiting for transfers between devices, fetch(): lax.ppermute(x, axis, [((i + offset) % size, i) for i in range(size)])  8.41 us
    pallas_call x1, Pallas kernels, local(): call(lambda *refs: stats_kernel(scale, 0, *refs), (tiles(5), tiles(5), st...  5.68 us
    all_to_all x1, starting transfers between devices, local(): dq_parts = lax.all_to_all(dq_parts, COLUMN, 0, 0, tiled=True)  5.55 us
    all_to_all x1, starting transfers between devices, local(): span_grads = lax.all_to_all(span_grads, COLUMN, 0, 0, tiled=True)  4.11 us
    pallas_call x1, Pallas kernels, local(): call(pack_kernel, (block, block, struct((GROUP, HALF), jnp.int32)), [smem...  3.34 us
  transfers between devices with their start and end apart: 29, of which 5 were waited for; matrix products, arithmetic and copies ran while one was open for 0% of the time, Pallas kernels for 16%

profile of v3, /device:TPU:1, one launch (start us, length us, event | category | flops | bytes accessed | tf_op | source)
XLA Modules:
  0.0 106.0 jit_solution(11808880037925040847)
XLA Ops:
  0.6 3.3 %shard_map.93 = (bf16[272,256]{1,0:T(8,128)(2,1)}, bf16[272,256]{1,0:T(8,128)(2,1)}, s32[8,128]{1,0:T(8,128)}) custom-call(s32[128]{0:T(128)} %span_ref.9, bf16[256,128]{1,0:T(8,128)(2,1)} %bitcast.7, bf16[256,128]{1,0:T(8,128)(2,1)} %bitcast.8, bf16[256,128]{1,0:T(8,128)(2,1)} %bitcast.9, bf16[256,128]{1,0:T(8,128)(2,1)} %bitcast.10, f32[1,256]{1,0:T(1,128)} %f_ref.1), custom_call_target="tpu_custom_call" | custom-call | bytes 4194304 | tf_op jit(solution)/shard_map/pallas_call | solution.py:615
  4.0 3.8 %collective-permute-start.5 = (bf16[272,256]{1,0:T(8,128)(2,1)}, bf16[272,256]{1,0:T(8,128)(2,1)S(1)}, u32[]{:S(2)}, u32[]{:S(2)}) collective-permute-start(bf16[272,256]{1,0:T(8,128)(2,1)} %get-tuple-element.40.refs_1_), channel_id=1, source_target_pairs={{16,0},{24,8},{0,16},{8,24},{17,1},{25,9},{1,17},{9,25},{18,2},{26... | collective-permute-start | bytes 417800 | tf_op jit(solution)/shard_map/ppermute | solution.py:604
  7.8 3.0 %collective-permute-start.10 = (bf16[272,256]{1,0:T(8,128)(2,1)}, bf16[272,256]{1,0:T(8,128)(2,1)S(1)}, u32[]{:S(2)}, u32[]{:S(2)}) collective-permute-start(bf16[272,256]{1,0:T(8,128)(2,1)} %get-tuple-element.41.refs_9_.refs_0_.refs_6_), channel_id=1, source_target_pairs={{192,0},{224,32},{0,64},{32,96},{64,128},{96,160},{128,192},{160,2... | collective-permute-start | bytes 417800 | tf_op jit(solution)/shard_map/ppermute | solution.py:604
  10.8 3.0 %collective-permute-start.9 = (bf16[272,256]{1,0:T(8,128)(2,1)}, bf16[272,256]{1,0:T(8,128)(2,1)S(1)}, u32[]{:S(2)}, u32[]{:S(2)}) collective-permute-start(bf16[272,256]{1,0:T(8,128)(2,1)} %get-tuple-element.41.refs_9_.refs_0_.refs_6_), channel_id=1, source_target_pairs={{64,0},{96,32},{128,64},{160,96},{192,128},{224,160},{0,192},{32,2... | collective-permute-start | bytes 417800 | tf_op jit(solution)/shard_map/ppermute | solution.py:604
  14.2 2.3 %collective-permute-start.1 = (bf16[272,256]{1,0:T(8,128)(2,1)}, bf16[272,256]{1,0:T(8,128)(2,1)S(1)}, u32[]{:S(2)}, u32[]{:S(2)}) collective-permute-start(bf16[272,256]{1,0:T(8,128)(2,1)} %get-tuple-element.40.refs_1_), channel_id=1, source_target_pairs={{8,0},{16,8},{24,16},{0,24},{9,1},{17,9},{25,17},{1,25},{10,2},{18... | collective-permute-start | bytes 417800 | tf_op jit(solution)/shard_map/ppermute | solution.py:604
  17.8 4.4 %collective-permute-start.7 = (bf16[272,256]{1,0:T(8,128)(2,1)}, bf16[272,256]{1,0:T(8,128)(2,1)S(1)}, u32[]{:S(2)}, u32[]{:S(2)}) collective-permute-start(bf16[272,256]{1,0:T(8,128)(2,1)} %get-tuple-element.41.refs_9_.refs_0_.refs_6_), channel_id=1, source_target_pairs={{32,0},{64,32},{96,64},{128,96},{160,128},{192,160},{224,192},{0,2... | collective-permute-start | bytes 417800 | tf_op jit(solution)/shard_map/ppermute | solution.py:604
  22.3 1.7 %collective-permute-start.13 = (bf16[144,256]{1,0:T(8,128)(2,1)S(1)}, bf16[144,256]{1,0:T(8,128)(2,1)S(1)}, u32[]{:S(2)}, u32[]{:S(2)}) collective-permute-start(bf16[144,256]{1,0:T(8,128)(2,1)S(1)} %slice.8), channel_id=1, source_target_pairs={{64,0},{96,32},{128,64},{160,96},{192,128},{224,160},{0,192},{32,2... | collective-permute-start | bytes 221192 | tf_op jit(solution)/shard_map/ppermute | solution.py:604
  25.5 2.9 %collective-permute-start = (bf16[272,256]{1,0:T(8,128)(2,1)S(1)}, bf16[272,256]{1,0:T(8,128)(2,1)S(1)}, u32[]{:S(2)}, u32[]{:S(2)}) collective-permute-start(bf16[272,256]{1,0:T(8,128)(2,1)S(1)} %copy-done.3), channel_id=1, source_target_pairs={{4,0},{0,4},{5,1},{1,5},{6,2},{2,6},{7,3},{3,7},{12,8},{8,12},{13,... | collective-permute-start | bytes 417800 | tf_op jit(solution)/shard_map/ppermute | solution.py:604
  28.8 2.3 %collective-permute-start.4 = (bf16[272,256]{1,0:T(8,128)(2,1)S(1)}, bf16[272,256]{1,0:T(8,128)(2,1)S(1)}, u32[]{:S(2)}, u32[]{:S(2)}) collective-permute-start(bf16[272,256]{1,0:T(8,128)(2,1)S(1)} %collective-permute-done.3.refs_5_), channel_id=1, source_target_pairs={{4,0},{0,4},{5,1},{1,5},{6,2},{2,6},{7,3},{3,7},{12,8},{8,12},{13,... | collective-permute-start | bytes 417800 | tf_op jit(solution)/shard_map/ppermute | solution.py:604
  31.2 3.3 %collective-permute-start.18 = (bf16[128,256]{1,0:T(8,128)(2,1)S(1)}, bf16[128,256]{1,0:T(8,128)(2,1)S(1)}, u32[]{:S(2)}, u32[]{:S(2)}) collective-permute-start(bf16[128,256]{1,0:T(8,128)(2,1)S(1)} %slice.9), channel_id=1, source_target_pairs={{192,0},{224,32},{0,64},{32,96},{64,128},{96,160},{128,192},{160,2... | collective-permute-start | bytes 196616 | tf_op jit(solution)/shard_map/ppermute | solution.py:604
  36.2 5.7 %shard_map.94 = (f32[5,3,1024]{2,1,0:T(4,128)S(1)}, f32[5,3,1024]{2,1,0:T(4,128)S(1)}, f32[8,128]{1,0:T(8,128)S(1)}, bf16[2,1024,256]{2,1,0:T(8,128)(2,1)S(1)}, ...) custom-call(s32[128]{0:T(128)S(1)} %copy-done.2, bf16[272,256]{1,0:T(8,128)(2,1)S(1)} %copy-done.3, ...), custom_call_target="tpu_custom_call" | custom-call | flops 2147483648 | bytes 4194304 | tf_op jit(solution)/shard_map/pallas_call | solution.py:646
  44.8 2.2 %shard_map.96 = (f32[3,3,1024]{2,1,0:T(4,128)S(1)}, f32[3,3,1024]{2,1,0:T(4,128)S(1)}) custom-call(s32[128]{0:T(128)S(1)} %copy-done.2, bf16[2,2,128,1024]{3,2,1,0:T(8,128)(2,1)S(1)} %get-tuple-element.43.refs_1_.refs_2_, f32[2,8,128]{2,1,0:T(8,128)S(1)} %get-tuple-element.48.refs_2_.wq_ref, ...), custom_call_target="tpu_custom_call" | custom-call | flops 2147483648 | bytes 4194304 | tf_op jit(solution)/shard_map/pallas_call | solution.py:664
  48.7 9.8 %all_to_all.15.stats_ref = f32[8,32,128]{2,1,0:T(8,128)S(1)} all-to-all(f32[8,32,128]{2,1,0:T(8,128)S(1)} %get-tuple-element.51), channel_id=1, replica_groups=mesh['z'=8,'y_hi'=2,'y_lo'=2,'core'=2,'head'=4] {'y_hi','y_lo','core'}, dimensions={0} | all-to-all | bytes 262144 | tf_op jit(solution)/shard_map/all_to_all | solution.py:676
  59.9 4.1 %all-to-all-start.1 = ((f32[8,8,128]{2,1,0:T(8,128)}), f32[8,8,128]{2,1,0:T(8,128)S(1)}, u32[]{:S(2)}, u32[]{:S(2)}) async-start(f32[8,8,128]{2,1,0:T(8,128)} %get-tuple-element.56), calls=%async_computation.1 | async-start | bytes 65536 | tf_op jit(solution)/shard_map/all_to_all | solution.py:682
  65.2 3.7 %shard_map.99 = (bf16[2,128,1024]{2,1,0:T(8,128)(2,1)S(1)}, bf16[272,256]{1,0:T(8,128)(2,1)S(1)}, bf16[272,256]{1,0:T(8,128)(2,1)S(1)}, bf16[128,256]{1,0:T(8,128)(2,1)S(1)}, bf16[144,256]{1,0:T(8,128)(2,1)S(1)}) custom-call(s32[128]{0:T(128)S(1)} %copy-done.2, bf16[2,1024,256]{2,1,0:T(8,128)(2,1)S(1)} %get-tuple-element.42.refs_1_, ...), custom_call_target="tpu_custom_call" | custom-call | flops 2147483648 | bytes 4194304 | tf_op jit(solution)/shard_map/pallas_call | solution.py:687
  71.3 1.7 %collective-permute-start.21 = (bf16[144,256]{1,0:T(8,128)(2,1)S(1)}, bf16[144,256]{1,0:T(8,128)(2,1)S(1)}, u32[]{:S(2)}, u32[]{:S(2)}) collective-permute-start(bf16[144,256]{1,0:T(8,128)(2,1)S(1)} %get-tuple-element.64), channel_id=1, source_target_pairs={{192,0},{224,32},{0,64},{32,96},{64,128},{96,160},{128,192},{160,2... | collective-permute-start | bytes 221192 | tf_op jit(solution)/shard_map/ppermute | solution.py:604
  76.9 4.0 %shard_map.101 = (bf16[2,128,1024]{2,1,0:T(8,128)(2,1)S(1)}, bf16[272,256]{1,0:T(8,128)(2,1)S(1)}, bf16[272,256]{1,0:T(8,128)(2,1)S(1)}, bf16[272,256]{1,0:T(8,128)(2,1)S(1)}) custom-call(s32[128]{0:T(128)S(1)} %copy-done.2, bf16[2,1024,256]{2,1,0:T(8,128)(2,1)S(1)} %get-tuple-element.42.refs_1_, bf16[2,2,128,1024]{3,2,1,0:T(8,128)(2,1)S(1)} %copy-done.6, ...), custom_call_target="tpu_custom_call" | custom-call | flops 2147483648 | bytes 4194304 | tf_op jit(solution)/shard_map/pallas_call | solution.py:687
  81.9 3.7 %shard_map.102 = (bf16[8,256,128]{2,1,0:T(8,128)(2,1)}, bf16[272,256]{1,0:T(8,128)(2,1)S(1)}, bf16[272,256]{1,0:T(8,128)(2,1)S(1)}) custom-call(s32[128]{0:T(128)S(1)} %copy-done.2, bf16[2,1024,256]{2,1,0:T(8,128)(2,1)S(1)} %get-tuple-element.42.refs_1_, bf16[2,2,128,1024]{3,2,1,0:T(8,128)(2,1)S(1)} %copy-done.6, ...), custom_call_target="tpu_custom_call" | custom-call | flops 2147483648 | bytes 4194304 | tf_op jit(solution)/shard_map/pallas_call | solution.py:687
  85.6 5.6 %all-to-all-start.2 = ((bf16[8,256,128]{2,1,0:T(8,128)(2,1)}), bf16[8,256,128]{2,1,0:T(8,128)(2,1)S(1)}, u32[]{:S(2)}, u32[]{:S(2)}) async-start(bf16[8,256,128]{2,1,0:T(8,128)(2,1)} %get-tuple-element.66), calls=%async_computation.2 | async-start | bytes 1048576 | tf_op jit(solution)/shard_map/all_to_all | solution.py:721
  91.5 2.3 %collective-permute-start.24 = (bf16[272,256]{1,0:T(8,128)(2,1)S(1)}, bf16[272,256]{1,0:T(8,128)(2,1)S(1)}, u32[]{:S(2)}, u32[]{:S(2)}) collective-permute-start(bf16[272,256]{1,0:T(8,128)(2,1)S(1)} %get-tuple-element.69), channel_id=1, source_target_pairs={{32,0},{64,32},{96,64},{128,96},{160,128},{192,160},{224,192},{0,2... | collective-permute-start | bytes 417800 | tf_op jit(solution)/shard_map/ppermute | solution.py:604
  94.5 3.0 %collective-permute-start.26 = (bf16[272,256]{1,0:T(8,128)(2,1)S(1)}, bf16[272,256]{1,0:T(8,128)(2,1)S(1)}, u32[]{:S(2)}, u32[]{:S(2)}) collective-permute-start(bf16[272,256]{1,0:T(8,128)(2,1)S(1)} %get-tuple-element.71), channel_id=1, source_target_pairs={{64,0},{96,32},{128,64},{160,96},{192,128},{224,160},{0,192},{32,2... | collective-permute-start | bytes 417800 | tf_op jit(solution)/shard_map/ppermute | solution.py:604
  97.7 3.3 %collective-permute-done.25.p3 = bf16[272,256]{1,0:T(8,128)(2,1)S(1)} collective-permute-done((bf16[272,256]{1,0:T(8,128)(2,1)S(1)}, bf16[272,256]{1,0:T(8,128)(2,1)S(1)}, u32[]{:S(2)}, u32[]{:S(2)}) %collective-permute-start.25) | collective-permute-done | bytes 139296 | tf_op jit(solution)/shard_map/ppermute | solution.py:604
  101.0 3.2 %collective-permute-done.26.p4 = bf16[272,256]{1,0:T(8,128)(2,1)S(1)} collective-permute-done((bf16[272,256]{1,0:T(8,128)(2,1)S(1)}, bf16[272,256]{1,0:T(8,128)(2,1)S(1)}, u32[]{:S(2)}, u32[]{:S(2)}) %collective-permute-start.26) | collective-permute-done | bytes 139296 | tf_op jit(solution)/shard_map/ppermute | solution.py:604
  104.2 1.7 %shard_map.103 = (bf16[256,128]{1,0:T(8,128)(2,1)}, bf16[256,128]{1,0:T(8,128)(2,1)}, bf16[256,128]{1,0:T(8,128)(2,1)}, f32[1,256]{1,0:T(1,128)}) custom-call(s32[128]{0:T(128)S(1)} %copy-done.2, bf16[8,256,128]{2,1,0:T(8,128)(2,1)S(1)} %all-to-all-done.2.dq_parts, bf16[272,256]{1,0:T(8,128)(2,1)S(1)} %get-tuple-element.67.p0, ...), custom_call_target="tpu_custom_call" | custom-call | bytes 4194304 | tf_op jit(solution)/shard_map/pallas_call | solution.py:723
  (63 shorter events, 20.9 us)
Async XLA Ops:
  4.0 12.5 %collective-permute-start.5 = (bf16[272,256]{1,0:T(8,128)(2,1)}, bf16[272,256]{1,0:T(8,128)(2,1)S(1)}, u32[]{:S(2)}, u32[]{:S(2)}) collective-permute-start(bf16[272,256]{1,0:T(8,128)(2,1)} %get-tuple-element.40.refs_1_), channel_id=1, source_target_pairs={{16,0},{24,8},{0,16},{8,24},{17,1},{25,9},{1,17},{9,25},{18,2},{26... | collective-permute-start | bytes 417800 | tf_op jit(solution)/shard_map/ppermute | solution.py:604
  7.8 10.0 %collective-permute-start.10 = (bf16[272,256]{1,0:T(8,128)(2,1)}, bf16[272,256]{1,0:T(8,128)(2,1)S(1)}, u32[]{:S(2)}, u32[]{:S(2)}) collective-permute-start(bf16[272,256]{1,0:T(8,128)(2,1)} %get-tuple-element.41.refs_9_.refs_0_.refs_6_), channel_id=1, source_target_pairs={{192,0},{224,32},{0,64},{32,96},{64,128},{96,160},{128,192},{160,2... | collective-permute-start | bytes 417800 | tf_op jit(solution)/shard_map/ppermute | solution.py:604
  10.8 11.5 %collective-permute-start.9 = (bf16[272,256]{1,0:T(8,128)(2,1)}, bf16[272,256]{1,0:T(8,128)(2,1)S(1)}, u32[]{:S(2)}, u32[]{:S(2)}) collective-permute-start(bf16[272,256]{1,0:T(8,128)(2,1)} %get-tuple-element.41.refs_9_.refs_0_.refs_6_), channel_id=1, source_target_pairs={{64,0},{96,32},{128,64},{160,96},{192,128},{224,160},{0,192},{32,2... | collective-permute-start | bytes 417800 | tf_op jit(solution)/shard_map/ppermute | solution.py:604
  13.9 8.4 %collective-permute-start.3 = (bf16[272,256]{1,0:T(8,128)(2,1)}, bf16[272,256]{1,0:T(8,128)(2,1)S(1)}, u32[]{:S(2)}, u32[]{:S(2)}) collective-permute-start(bf16[272,256]{1,0:T(8,128)(2,1)} %get-tuple-element.40.refs_1_), channel_id=1, source_target_pairs={{24,0},{0,8},{8,16},{16,24},{25,1},{1,9},{9,17},{17,25},{26,2},{2,... | collective-permute-start | bytes 417800 | tf_op jit(solution)/shard_map/ppermute | solution.py:604
  14.2 9.8 %collective-permute-start.1 = (bf16[272,256]{1,0:T(8,128)(2,1)}, bf16[272,256]{1,0:T(8,128)(2,1)S(1)}, u32[]{:S(2)}, u32[]{:S(2)}) collective-permute-start(bf16[272,256]{1,0:T(8,128)(2,1)} %get-tuple-element.40.refs_1_), channel_id=1, source_target_pairs={{8,0},{16,8},{24,16},{0,24},{9,1},{17,9},{25,17},{1,25},{10,2},{18... | collective-permute-start | bytes 417800 | tf_op jit(solution)/shard_map/ppermute | solution.py:604
  16.5 9.0 %collective-permute-start.8 = (bf16[272,256]{1,0:T(8,128)(2,1)}, bf16[272,256]{1,0:T(8,128)(2,1)S(1)}, u32[]{:S(2)}, u32[]{:S(2)}) collective-permute-start(bf16[272,256]{1,0:T(8,128)(2,1)} %get-tuple-element.41.refs_9_.refs_0_.refs_6_), channel_id=1, source_target_pairs={{224,0},{0,32},{32,64},{64,96},{96,128},{128,160},{160,192},{192,2... | collective-permute-start | bytes 417800 | tf_op jit(solution)/shard_map/ppermute | solution.py:604
  17.8 10.6 %collective-permute-start.7 = (bf16[272,256]{1,0:T(8,128)(2,1)}, bf16[272,256]{1,0:T(8,128)(2,1)S(1)}, u32[]{:S(2)}, u32[]{:S(2)}) collective-permute-start(bf16[272,256]{1,0:T(8,128)(2,1)} %get-tuple-element.41.refs_9_.refs_0_.refs_6_), channel_id=1, source_target_pairs={{32,0},{64,32},{96,64},{128,96},{160,128},{192,160},{224,192},{0,2... | collective-permute-start | bytes 417800 | tf_op jit(solution)/shard_map/ppermute | solution.py:604
  22.3 8.8 %collective-permute-start.12 = (bf16[272,256]{1,0:T(8,128)(2,1)S(1)}, bf16[272,256]{1,0:T(8,128)(2,1)S(1)}, u32[]{:S(2)}, u32[]{:S(2)}) collective-permute-start(bf16[272,256]{1,0:T(8,128)(2,1)S(1)} %collective-permute-done.10.refs_13_.refs_4_.refs_7_), channel_id=1, source_target_pairs={{224,0},{0,32},{32,64},{64,96},{96,128},{128,160},{160,192},{192,2... | collective-permute-start | bytes 417800 | tf_op jit(solution)/shard_map/ppermute | solution.py:604
  22.3 6.5 %collective-permute-start.13 = (bf16[144,256]{1,0:T(8,128)(2,1)S(1)}, bf16[144,256]{1,0:T(8,128)(2,1)S(1)}, u32[]{:S(2)}, u32[]{:S(2)}) collective-permute-start(bf16[144,256]{1,0:T(8,128)(2,1)S(1)} %slice.8), channel_id=1, source_target_pairs={{64,0},{96,32},{128,64},{160,96},{192,128},{224,160},{0,192},{32,2... | collective-permute-start | bytes 221192 | tf_op jit(solution)/shard_map/ppermute | solution.py:604
  24.1 7.1 %collective-permute-start.11 = (bf16[272,256]{1,0:T(8,128)(2,1)S(1)}, bf16[272,256]{1,0:T(8,128)(2,1)S(1)}, u32[]{:S(2)}, u32[]{:S(2)}) collective-permute-start(bf16[272,256]{1,0:T(8,128)(2,1)S(1)} %collective-permute-done.9.refs_12_.refs_3_.refs_6_), channel_id=1, source_target_pairs={{32,0},{64,32},{96,64},{128,96},{160,128},{192,160},{224,192},{0,2... | collective-permute-start | bytes 417800 | tf_op jit(solution)/shard_map/ppermute | solution.py:604
  25.5 9.3 %collective-permute-start = (bf16[272,256]{1,0:T(8,128)(2,1)S(1)}, bf16[272,256]{1,0:T(8,128)(2,1)S(1)}, u32[]{:S(2)}, u32[]{:S(2)}) collective-permute-start(bf16[272,256]{1,0:T(8,128)(2,1)S(1)} %copy-done.3), channel_id=1, source_target_pairs={{4,0},{0,4},{5,1},{1,5},{6,2},{2,6},{7,3},{3,7},{12,8},{8,12},{13,... | collective-permute-start | bytes 417800 | tf_op jit(solution)/shard_map/ppermute | solution.py:604
  28.4 7.8 %collective-permute-start.6 = (bf16[272,256]{1,0:T(8,128)(2,1)S(1)}, bf16[272,256]{1,0:T(8,128)(2,1)S(1)}, u32[]{:S(2)}, u32[]{:S(2)}) collective-permute-start(bf16[272,256]{1,0:T(8,128)(2,1)S(1)} %collective-permute-done.5.refs_7_), channel_id=1, source_target_pairs={{4,0},{0,4},{5,1},{1,5},{6,2},{2,6},{7,3},{3,7},{12,8},{8,12},{13,... | collective-permute-start | bytes 417800 | tf_op jit(solution)/shard_map/ppermute | solution.py:604
  28.8 7.4 %collective-permute-start.4 = (bf16[272,256]{1,0:T(8,128)(2,1)S(1)}, bf16[272,256]{1,0:T(8,128)(2,1)S(1)}, u32[]{:S(2)}, u32[]{:S(2)}) collective-permute-start(bf16[272,256]{1,0:T(8,128)(2,1)S(1)} %collective-permute-done.3.refs_5_), channel_id=1, source_target_pairs={{4,0},{0,4},{5,1},{1,5},{6,2},{2,6},{7,3},{3,7},{12,8},{8,12},{13,... | collective-permute-start | bytes 417800 | tf_op jit(solution)/shard_map/ppermute | solution.py:604
  31.2 13.7 %collective-permute-start.18 = (bf16[128,256]{1,0:T(8,128)(2,1)S(1)}, bf16[128,256]{1,0:T(8,128)(2,1)S(1)}, u32[]{:S(2)}, u32[]{:S(2)}) collective-permute-start(bf16[128,256]{1,0:T(8,128)(2,1)S(1)} %slice.9), channel_id=1, source_target_pairs={{192,0},{224,32},{0,64},{32,96},{64,128},{96,160},{128,192},{160,2... | collective-permute-start | bytes 196616 | tf_op jit(solution)/shard_map/ppermute | solution.py:604
  34.8 7.1 %collective-permute-start.14 = (f32[8,128]{1,0:T(8,128)S(1)}, f32[8,128]{1,0:T(8,128)S(1)}, u32[]{:S(2)}, u32[]{:S(2)}) collective-permute-start(f32[8,128]{1,0:T(8,128)S(1)} %shard_map.95), channel_id=1, source_target_pairs={{4,0},{0,4},{5,1},{1,5},{6,2},{2,6},{7,3},{3,7},{12,8},{8,12},{13,... | collective-permute-start | bytes 12296 | tf_op jit(solution)/shard_map/ppermute | solution.py:604
  59.9 10.7 %all-to-all-start.1 = ((f32[8,8,128]{2,1,0:T(8,128)}), f32[8,8,128]{2,1,0:T(8,128)S(1)}, u32[]{:S(2)}, u32[]{:S(2)}) async-start(f32[8,8,128]{2,1,0:T(8,128)} %get-tuple-element.56), calls=%async_computation.1 | async-start | bytes 65536 | tf_op jit(solution)/shard_map/all_to_all | solution.py:682
  69.0 11.9 %collective-permute-start.22 = (bf16[128,256]{1,0:T(8,128)(2,1)S(1)}, bf16[128,256]{1,0:T(8,128)(2,1)S(1)}, u32[]{:S(2)}, u32[]{:S(2)}) collective-permute-start(bf16[128,256]{1,0:T(8,128)(2,1)S(1)} %get-tuple-element.65), channel_id=1, source_target_pairs={{64,0},{96,32},{128,64},{160,96},{192,128},{224,160},{0,192},{32,2... | collective-permute-start | bytes 196616 | tf_op jit(solution)/shard_map/ppermute | solution.py:604
  71.3 9.6 %collective-permute-start.21 = (bf16[144,256]{1,0:T(8,128)(2,1)S(1)}, bf16[144,256]{1,0:T(8,128)(2,1)S(1)}, u32[]{:S(2)}, u32[]{:S(2)}) collective-permute-start(bf16[144,256]{1,0:T(8,128)(2,1)S(1)} %get-tuple-element.64), channel_id=1, source_target_pairs={{192,0},{224,32},{0,64},{32,96},{64,128},{96,160},{128,192},{160,2... | collective-permute-start | bytes 221192 | tf_op jit(solution)/shard_map/ppermute | solution.py:604
  73.0 8.9 %collective-permute-start.19 = (bf16[272,256]{1,0:T(8,128)(2,1)S(1)}, bf16[272,256]{1,0:T(8,128)(2,1)S(1)}, u32[]{:S(2)}, u32[]{:S(2)}) collective-permute-start(bf16[272,256]{1,0:T(8,128)(2,1)S(1)} %get-tuple-element.62), channel_id=1, source_target_pairs={{224,0},{0,32},{32,64},{64,96},{96,128},{128,160},{160,192},{192,2... | collective-permute-start | bytes 417800 | tf_op jit(solution)/shard_map/ppermute | solution.py:604
  74.6 7.3 %collective-permute-start.20 = (bf16[272,256]{1,0:T(8,128)(2,1)S(1)}, bf16[272,256]{1,0:T(8,128)(2,1)S(1)}, u32[]{:S(2)}, u32[]{:S(2)}) collective-permute-start(bf16[272,256]{1,0:T(8,128)(2,1)S(1)} %get-tuple-element.63), channel_id=1, source_target_pairs={{32,0},{64,32},{96,64},{128,96},{160,128},{192,160},{224,192},{0,2... | collective-permute-start | bytes 417800 | tf_op jit(solution)/shard_map/ppermute | solution.py:604
  85.6 18.6 %all-to-all-start.2 = ((bf16[8,256,128]{2,1,0:T(8,128)(2,1)}), bf16[8,256,128]{2,1,0:T(8,128)(2,1)S(1)}, u32[]{:S(2)}, u32[]{:S(2)}) async-start(bf16[8,256,128]{2,1,0:T(8,128)(2,1)} %get-tuple-element.66), calls=%async_computation.2 | async-start | bytes 1048576 | tf_op jit(solution)/shard_map/all_to_all | solution.py:721
  91.2 6.5 %collective-permute-start.23 = (bf16[272,256]{1,0:T(8,128)(2,1)S(1)}, bf16[272,256]{1,0:T(8,128)(2,1)S(1)}, u32[]{:S(2)}, u32[]{:S(2)}) collective-permute-start(bf16[272,256]{1,0:T(8,128)(2,1)S(1)} %get-tuple-element.68), channel_id=1, source_target_pairs={{224,0},{0,32},{32,64},{64,96},{96,128},{128,160},{160,192},{192,2... | collective-permute-start | bytes 417800 | tf_op jit(solution)/shard_map/ppermute | solution.py:604
  93.8 7.2 %collective-permute-start.25 = (bf16[272,256]{1,0:T(8,128)(2,1)S(1)}, bf16[272,256]{1,0:T(8,128)(2,1)S(1)}, u32[]{:S(2)}, u32[]{:S(2)}) collective-permute-start(bf16[272,256]{1,0:T(8,128)(2,1)S(1)} %get-tuple-element.70), channel_id=1, source_target_pairs={{192,0},{224,32},{0,64},{32,96},{64,128},{96,160},{128,192},{160,2... | collective-permute-start | bytes 417800 | tf_op jit(solution)/shard_map/ppermute | solution.py:604
  94.5 9.8 %collective-permute-start.26 = (bf16[272,256]{1,0:T(8,128)(2,1)S(1)}, bf16[272,256]{1,0:T(8,128)(2,1)S(1)}, u32[]{:S(2)}, u32[]{:S(2)}) collective-permute-start(bf16[272,256]{1,0:T(8,128)(2,1)S(1)} %get-tuple-element.71), channel_id=1, source_target_pairs={{64,0},{96,32},{128,64},{160,96},{192,128},{224,160},{0,192},{32,2... | collective-permute-start | bytes 417800 | tf_op jit(solution)/shard_map/ppermute | solution.py:604
  (12 other events, 86.5 us)

commit v4 on v3

--- a/solution.py
+++ b/solution.py
@@ -208,14 +208,15 @@
     return pl.ds(pl.multiple_of(HALF * d, HALF), HALF)
 
 
-def load_queries(query_refs, y, core, qs, gates):
-    copies = []
+def place_queries(query_refs, y, core, qs, qt, gates):
     for at, ref in enumerate(query_refs):
         d = near_column(y, core, at)
         for half in range(2):
-            copies.append((ref.at[pl.ds(HALF * half, HALF), :], qs.at[half, lanes_of(d), :]))
-        copies.append((ref.at[pl.ds(ROWS, AUX), :], gates.at[d]))
-    return copies
+            block = ref[HALF * half : HALF * (half + 1), :]
+            qs[half, lanes_of(d), :] = block
+            qt[0, half, :, lanes_of(d)] = jnp.transpose(block[:, 0:HALF])
+            qt[1, half, :, lanes_of(d)] = jnp.transpose(block[:, HALF:ROWS])
+        gates[d] = ref[ROWS:PACK, :]
 
 
 def stats_kernel(scale, first, span_ref, *refs):
@@ -229,16 +230,12 @@
     else:
         count = 5
         query_refs, ks = refs[:8], refs[8:13]
-        one_ref, two_ref, own_ref, qs, qt, wq, columns, gates, sems = refs[13:]
-        run_copies(load_queries(query_refs, y, core, qs, gates), sems)
+        one_ref, two_ref, own_ref, qs, qt, wq, columns, gates = refs[13:]
+        place_queries(query_refs, y, core, qs, qt, gates)
         for d in range(GROUP):
-            rows = slice(HALF * d, HALF * (d + 1))
             row = join_rows(gates[d]) * LOG2E
             wq[0, d : d + 1, :] = row[:, 0:HALF]
             wq[1, d : d + 1, :] = row[:, HALF:ROWS]
-            for half in range(2):
-                qt[0, half, :, rows] = jnp.transpose(qs[half, rows, 0:HALF])
-                qt[1, half, :, rows] = jnp.transpose(qs[half, rows, HALF:ROWS])
     ahead = ahead_of()
     lows = [slot_low(span_ref, z * GROUP + d) for d in range(GROUP)]
 
@@ -653,12 +650,8 @@
             struct((2, 2, HALF, GROUP * HALF), BF16),
             gates,
         ),
-        [smem] + [hbm] * 8 + [vmem] * 5,
-        [
-            pltpu.VMEM((2, HALF, HALF), F32),
-            pltpu.VMEM((GROUP, AUX, ROWS), BF16),
-            pltpu.SemaphoreType.DMA((24,)),
-        ],
+        [smem] + [vmem] * 13,
+        [pltpu.VMEM((2, HALF, HALF), F32), pltpu.VMEM((GROUP, AUX, ROWS), BF16)],
         flops=1 << 31,
     )(span_order, *query_blocks, *near_keys)
     far1, far2 = call(

time: 106 us -> 104 us (0.981)
  Pallas kernels: 27.7 us -> 25.9 us
    pallas_call x1, Pallas kernels: 5.68 us -> 3.88 us  [local(): call(lambda *refs: stats_kernel(scale, 0, *refs), (tiles(5), tiles(5), st...]
  transfers between devices with their start and end apart: 29 -> 29, of which waited for: 5 -> 5; matrix products, arithmetic and copies ran while one was open for 0% -> 0% of each run, Pallas kernels for 16% -> 14%
where the time goes in v4:
time: 104 us
  starting transfers between devices  55.8 us (54%)
  Pallas kernels  25.9 us (25%)
  blocking collectives  9.77 us (9%)
  waiting for transfers between devices  8.41 us (8%)
  local copies, waits for them, and re-layouts  3.16 us (3%)
    ppermute x27, starting transfers between devices, fetch(): lax.ppermute(x, axis, [((i + offset) % size, i) for i in range(size)])  46.2 us
    pallas_call x3, Pallas kernels, grads(): call(lambda *refs: grads_kernel(scale, first, count, len(keys), *refs), o...  11.5 us
    all_to_all x1, blocking collectives, local(): stats = lax.all_to_all(stats, COLUMN, 0, 0, tiled=True)  9.77 us
    ppermute x27, waiting for transfers between devices, fetch(): lax.ppermute(x, axis, [((i + offset) % size, i) for i in range(size)])  8.4 us
    all_to_all x1, starting transfers between devices, local(): dq_parts = lax.all_to_all(dq_parts, COLUMN, 0, 0, tiled=True)  5.55 us
    all_to_all x1, starting transfers between devices, local(): span_grads = lax.all_to_all(span_grads, COLUMN, 0, 0, tiled=True)  4.11 us
    pallas_call x1, Pallas kernels, local(): call(lambda *refs: stats_kernel(scale, 0, *refs), (tiles(5), tiles(5), st...  3.88 us
    pallas_call x1, Pallas kernels, local(): call(pack_kernel, (block, block, struct((GROUP, HALF), jnp.int32)), [smem...  3.34 us
  transfers between devices with their start and end apart: 29, of which 5 were waited for; matrix products, arithmetic and copies ran while one was open for 0% of the time, Pallas kernels for 14%

profile of v4, /device:TPU:1, one launch (start us, length us, event | category | flops | bytes accessed | tf_op | source)
XLA Modules:
  0.0 103.9 jit_solution(979957929119290705)
XLA Ops:
  0.6 3.3 %shard_map.93 = (bf16[272,256]{1,0:T(8,128)(2,1)}, bf16[272,256]{1,0:T(8,128)(2,1)}, s32[8,128]{1,0:T(8,128)}) custom-call(s32[128]{0:T(128)} %span_ref.9, bf16[256,128]{1,0:T(8,128)(2,1)} %bitcast.7, bf16[256,128]{1,0:T(8,128)(2,1)} %bitcast.8, bf16[256,128]{1,0:T(8,128)(2,1)} %bitcast.9, bf16[256,128]{1,0:T(8,128)(2,1)} %bitcast.10, f32[1,256]{1,0:T(1,128)} %f_ref.1), custom_call_target="tpu_custom_call" | custom-call | bytes 4194304 | tf_op jit(solution)/shard_map/pallas_call | solution.py:612
  4.0 3.8 %collective-permute-start.5 = (bf16[272,256]{1,0:T(8,128)(2,1)}, bf16[272,256]{1,0:T(8,128)(2,1)S(1)}, u32[]{:S(2)}, u32[]{:S(2)}) collective-permute-start(bf16[272,256]{1,0:T(8,128)(2,1)} %get-tuple-element.40.refs_1_), channel_id=1, source_target_pairs={{16,0},{24,8},{0,16},{8,24},{17,1},{25,9},{1,17},{9,25},{18,2},{26... | collective-permute-start | bytes 417800 | tf_op jit(solution)/shard_map/ppermute | solution.py:601
  7.8 3.0 %collective-permute-start.10 = (bf16[272,256]{1,0:T(8,128)(2,1)}, bf16[272,256]{1,0:T(8,128)(2,1)S(1)}, u32[]{:S(2)}, u32[]{:S(2)}) collective-permute-start(bf16[272,256]{1,0:T(8,128)(2,1)} %get-tuple-element.41.refs_9_.refs_0_.refs_6_), channel_id=1, source_target_pairs={{192,0},{224,32},{0,64},{32,96},{64,128},{96,160},{128,192},{160,2... | collective-permute-start | bytes 417800 | tf_op jit(solution)/shard_map/ppermute | solution.py:601
  10.8 3.0 %collective-permute-start.9 = (bf16[272,256]{1,0:T(8,128)(2,1)}, bf16[272,256]{1,0:T(8,128)(2,1)S(1)}, u32[]{:S(2)}, u32[]{:S(2)}) collective-permute-start(bf16[272,256]{1,0:T(8,128)(2,1)} %get-tuple-element.41.refs_9_.refs_0_.refs_6_), channel_id=1, source_target_pairs={{64,0},{96,32},{128,64},{160,96},{192,128},{224,160},{0,192},{32,2... | collective-permute-start | bytes 417800 | tf_op jit(solution)/shard_map/ppermute | solution.py:601
  14.2 2.3 %collective-permute-start.1 = (bf16[272,256]{1,0:T(8,128)(2,1)}, bf16[272,256]{1,0:T(8,128)(2,1)S(1)}, u32[]{:S(2)}, u32[]{:S(2)}) collective-permute-start(bf16[272,256]{1,0:T(8,128)(2,1)} %get-tuple-element.40.refs_1_), channel_id=1, source_target_pairs={{8,0},{16,8},{24,16},{0,24},{9,1},{17,9},{25,17},{1,25},{10,2},{18... | collective-permute-start | bytes 417800 | tf_op jit(solution)/shard_map/ppermute | solution.py:601
  17.8 4.4 %collective-permute-start.7 = (bf16[272,256]{1,0:T(8,128)(2,1)}, bf16[272,256]{1,0:T(8,128)(2,1)S(1)}, u32[]{:S(2)}, u32[]{:S(2)}) collective-permute-start(bf16[272,256]{1,0:T(8,128)(2,1)} %get-tuple-element.41.refs_9_.refs_0_.refs_6_), channel_id=1, source_target_pairs={{32,0},{64,32},{96,64},{128,96},{160,128},{192,160},{224,192},{0,2... | collective-permute-start | bytes 417800 | tf_op jit(solution)/shard_map/ppermute | solution.py:601
  22.3 1.7 %collective-permute-start.13 = (bf16[144,256]{1,0:T(8,128)(2,1)S(1)}, bf16[144,256]{1,0:T(8,128)(2,1)S(1)}, u32[]{:S(2)}, u32[]{:S(2)}) collective-permute-start(bf16[144,256]{1,0:T(8,128)(2,1)S(1)} %slice.8), channel_id=1, source_target_pairs={{64,0},{96,32},{128,64},{160,96},{192,128},{224,160},{0,192},{32,2... | collective-permute-start | bytes 221192 | tf_op jit(solution)/shard_map/ppermute | solution.py:601
  25.5 2.9 %collective-permute-start = (bf16[272,256]{1,0:T(8,128)(2,1)S(1)}, bf16[272,256]{1,0:T(8,128)(2,1)S(1)}, u32[]{:S(2)}, u32[]{:S(2)}) collective-permute-start(bf16[272,256]{1,0:T(8,128)(2,1)S(1)} %copy-done.3), channel_id=1, source_target_pairs={{4,0},{0,4},{5,1},{1,5},{6,2},{2,6},{7,3},{3,7},{12,8},{8,12},{13,... | collective-permute-start | bytes 417800 | tf_op jit(solution)/shard_map/ppermute | solution.py:601
  28.8 2.3 %collective-permute-start.4 = (bf16[272,256]{1,0:T(8,128)(2,1)S(1)}, bf16[272,256]{1,0:T(8,128)(2,1)S(1)}, u32[]{:S(2)}, u32[]{:S(2)}) collective-permute-start(bf16[272,256]{1,0:T(8,128)(2,1)S(1)} %collective-permute-done.3.refs_5_), channel_id=1, source_target_pairs={{4,0},{0,4},{5,1},{1,5},{6,2},{2,6},{7,3},{3,7},{12,8},{8,12},{13,... | collective-permute-start | bytes 417800 | tf_op jit(solution)/shard_map/ppermute | solution.py:601
  31.2 3.3 %collective-permute-start.18 = (bf16[128,256]{1,0:T(8,128)(2,1)S(1)}, bf16[128,256]{1,0:T(8,128)(2,1)S(1)}, u32[]{:S(2)}, u32[]{:S(2)}) collective-permute-start(bf16[128,256]{1,0:T(8,128)(2,1)S(1)} %slice.9), channel_id=1, source_target_pairs={{192,0},{224,32},{0,64},{32,96},{64,128},{96,160},{128,192},{160,2... | collective-permute-start | bytes 196616 | tf_op jit(solution)/shard_map/ppermute | solution.py:601
  36.2 3.9 %shard_map.94 = (f32[5,3,1024]{2,1,0:T(4,128)S(1)}, f32[5,3,1024]{2,1,0:T(4,128)S(1)}, f32[8,128]{1,0:T(8,128)S(1)}, bf16[2,1024,256]{2,1,0:T(8,128)(2,1)S(1)}, ...) custom-call(s32[128]{0:T(128)S(1)} %copy-done.2, bf16[272,256]{1,0:T(8,128)(2,1)S(1)} %copy-done.3, ...), custom_call_target="tpu_custom_call" | custom-call | flops 2147483648 | bytes 4194304 | tf_op jit(solution)/shard_map/pallas_call | solution.py:643
  43.0 2.2 %shard_map.96 = (f32[3,3,1024]{2,1,0:T(4,128)S(1)}, f32[3,3,1024]{2,1,0:T(4,128)S(1)}) custom-call(s32[128]{0:T(128)S(1)} %copy-done.2, bf16[2,2,128,1024]{3,2,1,0:T(8,128)(2,1)S(1)} %get-tuple-element.43.refs_1_.refs_2_, f32[2,8,128]{2,1,0:T(8,128)S(1)} %get-tuple-element.48.refs_2_.wq_ref, ...), custom_call_target="tpu_custom_call" | custom-call | flops 2147483648 | bytes 4194304 | tf_op jit(solution)/shard_map/pallas_call | solution.py:657
  46.9 9.8 %all_to_all.15.stats_ref = f32[8,32,128]{2,1,0:T(8,128)S(1)} all-to-all(f32[8,32,128]{2,1,0:T(8,128)S(1)} %get-tuple-element.51), channel_id=1, replica_groups=mesh['z'=8,'y_hi'=2,'y_lo'=2,'core'=2,'head'=4] {'y_hi','y_lo','core'}, dimensions={0} | all-to-all | bytes 262144 | tf_op jit(solution)/shard_map/all_to_all | solution.py:669
  58.1 4.1 %all-to-all-start.1 = ((f32[8,8,128]{2,1,0:T(8,128)}), f32[8,8,128]{2,1,0:T(8,128)S(1)}, u32[]{:S(2)}, u32[]{:S(2)}) async-start(f32[8,8,128]{2,1,0:T(8,128)} %get-tuple-element.56), calls=%async_computation.1 | async-start | bytes 65536 | tf_op jit(solution)/shard_map/all_to_all | solution.py:675
  63.4 3.7 %shard_map.99 = (bf16[2,128,1024]{2,1,0:T(8,128)(2,1)S(1)}, bf16[272,256]{1,0:T(8,128)(2,1)S(1)}, bf16[272,256]{1,0:T(8,128)(2,1)S(1)}, bf16[128,256]{1,0:T(8,128)(2,1)S(1)}, bf16[144,256]{1,0:T(8,128)(2,1)S(1)}) custom-call(s32[128]{0:T(128)S(1)} %copy-done.2, bf16[2,1024,256]{2,1,0:T(8,128)(2,1)S(1)} %get-tuple-element.42.refs_1_, ...), custom_call_target="tpu_custom_call" | custom-call | flops 2147483648 | bytes 4194304 | tf_op jit(solution)/shard_map/pallas_call | solution.py:680
  67.2 1.7 %collective-permute-start.22 = (bf16[128,256]{1,0:T(8,128)(2,1)S(1)}, bf16[128,256]{1,0:T(8,128)(2,1)S(1)}, u32[]{:S(2)}, u32[]{:S(2)}) collective-permute-start(bf16[128,256]{1,0:T(8,128)(2,1)S(1)} %get-tuple-element.65), channel_id=1, source_target_pairs={{64,0},{96,32},{128,64},{160,96},{192,128},{224,160},{0,192},{32,2... | collective-permute-start | bytes 196616 | tf_op jit(solution)/shard_map/ppermute | solution.py:601
  74.9 4.0 %shard_map.101 = (bf16[2,128,1024]{2,1,0:T(8,128)(2,1)S(1)}, bf16[272,256]{1,0:T(8,128)(2,1)S(1)}, bf16[272,256]{1,0:T(8,128)(2,1)S(1)}, bf16[272,256]{1,0:T(8,128)(2,1)S(1)}) custom-call(s32[128]{0:T(128)S(1)} %copy-done.2, bf16[2,1024,256]{2,1,0:T(8,128)(2,1)S(1)} %get-tuple-element.42.refs_1_, bf16[2,2,128,1024]{3,2,1,0:T(8,128)(2,1)S(1)} %copy-done.6, ...), custom_call_target="tpu_custom_call" | custom-call | flops 2147483648 | bytes 4194304 | tf_op jit(solution)/shard_map/pallas_call | solution.py:680
  79.8 3.7 %shard_map.102 = (bf16[8,256,128]{2,1,0:T(8,128)(2,1)}, bf16[272,256]{1,0:T(8,128)(2,1)S(1)}, bf16[272,256]{1,0:T(8,128)(2,1)S(1)}) custom-call(s32[128]{0:T(128)S(1)} %copy-done.2, bf16[2,1024,256]{2,1,0:T(8,128)(2,1)S(1)} %get-tuple-element.42.refs_1_, bf16[2,2,128,1024]{3,2,1,0:T(8,128)(2,1)S(1)} %copy-done.6, ...), custom_call_target="tpu_custom_call" | custom-call | flops 2147483648 | bytes 4194304 | tf_op jit(solution)/shard_map/pallas_call | solution.py:680
  83.6 5.5 %all-to-all-start.2 = ((bf16[8,256,128]{2,1,0:T(8,128)(2,1)}), bf16[8,256,128]{2,1,0:T(8,128)(2,1)S(1)}, u32[]{:S(2)}, u32[]{:S(2)}) async-start(bf16[8,256,128]{2,1,0:T(8,128)(2,1)} %get-tuple-element.66), calls=%async_computation.2 | async-start | bytes 1048576 | tf_op jit(solution)/shard_map/all_to_all | solution.py:714
  89.5 2.3 %collective-permute-start.24 = (bf16[272,256]{1,0:T(8,128)(2,1)S(1)}, bf16[272,256]{1,0:T(8,128)(2,1)S(1)}, u32[]{:S(2)}, u32[]{:S(2)}) collective-permute-start(bf16[272,256]{1,0:T(8,128)(2,1)S(1)} %get-tuple-element.69), channel_id=1, source_target_pairs={{32,0},{64,32},{96,64},{128,96},{160,128},{192,160},{224,192},{0,2... | collective-permute-start | bytes 417800 | tf_op jit(solution)/shard_map/ppermute | solution.py:601
  92.4 3.0 %collective-permute-start.26 = (bf16[272,256]{1,0:T(8,128)(2,1)S(1)}, bf16[272,256]{1,0:T(8,128)(2,1)S(1)}, u32[]{:S(2)}, u32[]{:S(2)}) collective-permute-start(bf16[272,256]{1,0:T(8,128)(2,1)S(1)} %get-tuple-element.71), channel_id=1, source_target_pairs={{64,0},{96,32},{128,64},{160,96},{192,128},{224,160},{0,192},{32,2... | collective-permute-start | bytes 417800 | tf_op jit(solution)/shard_map/ppermute | solution.py:601
  95.6 3.4 %collective-permute-done.25.p3 = bf16[272,256]{1,0:T(8,128)(2,1)S(1)} collective-permute-done((bf16[272,256]{1,0:T(8,128)(2,1)S(1)}, bf16[272,256]{1,0:T(8,128)(2,1)S(1)}, u32[]{:S(2)}, u32[]{:S(2)}) %collective-permute-start.25) | collective-permute-done | bytes 139296 | tf_op jit(solution)/shard_map/ppermute | solution.py:601
  99.0 3.2 %collective-permute-done.26.p4 = bf16[272,256]{1,0:T(8,128)(2,1)S(1)} collective-permute-done((bf16[272,256]{1,0:T(8,128)(2,1)S(1)}, bf16[272,256]{1,0:T(8,128)(2,1)S(1)}, u32[]{:S(2)}, u32[]{:S(2)}) %collective-permute-start.26) | collective-permute-done | bytes 139296 | tf_op jit(solution)/shard_map/ppermute | solution.py:601
  102.2 1.7 %shard_map.103 = (bf16[256,128]{1,0:T(8,128)(2,1)}, bf16[256,128]{1,0:T(8,128)(2,1)}, bf16[256,128]{1,0:T(8,128)(2,1)}, f32[1,256]{1,0:T(1,128)}) custom-call(s32[128]{0:T(128)S(1)} %copy-done.2, bf16[8,256,128]{2,1,0:T(8,128)(2,1)S(1)} %all-to-all-done.2.dq_parts, bf16[272,256]{1,0:T(8,128)(2,1)S(1)} %get-tuple-element.67.p0, ...), custom_call_target="tpu_custom_call" | custom-call | bytes 4194304 | tf_op jit(solution)/shard_map/pallas_call | solution.py:716
  (63 shorter events, 20.7 us)
Async XLA Ops:
  4.0 12.5 %collective-permute-start.5 = (bf16[272,256]{1,0:T(8,128)(2,1)}, bf16[272,256]{1,0:T(8,128)(2,1)S(1)}, u32[]{:S(2)}, u32[]{:S(2)}) collective-permute-start(bf16[272,256]{1,0:T(8,128)(2,1)} %get-tuple-element.40.refs_1_), channel_id=1, source_target_pairs={{16,0},{24,8},{0,16},{8,24},{17,1},{25,9},{1,17},{9,25},{18,2},{26... | collective-permute-start | bytes 417800 | tf_op jit(solution)/shard_map/ppermute | solution.py:601
  7.8 10.0 %collective-permute-start.10 = (bf16[272,256]{1,0:T(8,128)(2,1)}, bf16[272,256]{1,0:T(8,128)(2,1)S(1)}, u32[]{:S(2)}, u32[]{:S(2)}) collective-permute-start(bf16[272,256]{1,0:T(8,128)(2,1)} %get-tuple-element.41.refs_9_.refs_0_.refs_6_), channel_id=1, source_target_pairs={{192,0},{224,32},{0,64},{32,96},{64,128},{96,160},{128,192},{160,2... | collective-permute-start | bytes 417800 | tf_op jit(solution)/shard_map/ppermute | solution.py:601
  10.8 11.5 %collective-permute-start.9 = (bf16[272,256]{1,0:T(8,128)(2,1)}, bf16[272,256]{1,0:T(8,128)(2,1)S(1)}, u32[]{:S(2)}, u32[]{:S(2)}) collective-permute-start(bf16[272,256]{1,0:T(8,128)(2,1)} %get-tuple-element.41.refs_9_.refs_0_.refs_6_), channel_id=1, source_target_pairs={{64,0},{96,32},{128,64},{160,96},{192,128},{224,160},{0,192},{32,2... | collective-permute-start | bytes 417800 | tf_op jit(solution)/shard_map/ppermute | solution.py:601
  13.9 8.4 %collective-permute-start.3 = (bf16[272,256]{1,0:T(8,128)(2,1)}, bf16[272,256]{1,0:T(8,128)(2,1)S(1)}, u32[]{:S(2)}, u32[]{:S(2)}) collective-permute-start(bf16[272,256]{1,0:T(8,128)(2,1)} %get-tuple-element.40.refs_1_), channel_id=1, source_target_pairs={{24,0},{0,8},{8,16},{16,24},{25,1},{1,9},{9,17},{17,25},{26,2},{2,... | collective-permute-start | bytes 417800 | tf_op jit(solution)/shard_map/ppermute | solution.py:601
  14.2 9.8 %collective-permute-start.1 = (bf16[272,256]{1,0:T(8,128)(2,1)}, bf16[272,256]{1,0:T(8,128)(2,1)S(1)}, u32[]{:S(2)}, u32[]{:S(2)}) collective-permute-start(bf16[272,256]{1,0:T(8,128)(2,1)} %get-tuple-element.40.refs_1_), channel_id=1, source_target_pairs={{8,0},{16,8},{24,16},{0,24},{9,1},{17,9},{25,17},{1,25},{10,2},{18... | collective-permute-start | bytes 417800 | tf_op jit(solution)/shard_map/ppermute | solution.py:601
  16.5 9.0 %collective-permute-start.8 = (bf16[272,256]{1,0:T(8,128)(2,1)}, bf16[272,256]{1,0:T(8,128)(2,1)S(1)}, u32[]{:S(2)}, u32[]{:S(2)}) collective-permute-start(bf16[272,256]{1,0:T(8,128)(2,1)} %get-tuple-element.41.refs_9_.refs_0_.refs_6_), channel_id=1, source_target_pairs={{224,0},{0,32},{32,64},{64,96},{96,128},{128,160},{160,192},{192,2... | collective-permute-start | bytes 417800 | tf_op jit(solution)/shard_map/ppermute | solution.py:601
  17.8 10.6 %collective-permute-start.7 = (bf16[272,256]{1,0:T(8,128)(2,1)}, bf16[272,256]{1,0:T(8,128)(2,1)S(1)}, u32[]{:S(2)}, u32[]{:S(2)}) collective-permute-start(bf16[272,256]{1,0:T(8,128)(2,1)} %get-tuple-element.41.refs_9_.refs_0_.refs_6_), channel_id=1, source_target_pairs={{32,0},{64,32},{96,64},{128,96},{160,128},{192,160},{224,192},{0,2... | collective-permute-start | bytes 417800 | tf_op jit(solution)/shard_map/ppermute | solution.py:601
  22.3 8.8 %collective-permute-start.12 = (bf16[272,256]{1,0:T(8,128)(2,1)S(1)}, bf16[272,256]{1,0:T(8,128)(2,1)S(1)}, u32[]{:S(2)}, u32[]{:S(2)}) collective-permute-start(bf16[272,256]{1,0:T(8,128)(2,1)S(1)} %collective-permute-done.10.refs_13_.refs_4_.refs_7_), channel_id=1, source_target_pairs={{224,0},{0,32},{32,64},{64,96},{96,128},{128,160},{160,192},{192,2... | collective-permute-start | bytes 417800 | tf_op jit(solution)/shard_map/ppermute | solution.py:601
  22.3 6.5 %collective-permute-start.13 = (bf16[144,256]{1,0:T(8,128)(2,1)S(1)}, bf16[144,256]{1,0:T(8,128)(2,1)S(1)}, u32[]{:S(2)}, u32[]{:S(2)}) collective-permute-start(bf16[144,256]{1,0:T(8,128)(2,1)S(1)} %slice.8), channel_id=1, source_target_pairs={{64,0},{96,32},{128,64},{160,96},{192,128},{224,160},{0,192},{32,2... | collective-permute-start | bytes 221192 | tf_op jit(solution)/shard_map/ppermute | solution.py:601
  24.1 7.1 %collective-permute-start.11 = (bf16[272,256]{1,0:T(8,128)(2,1)S(1)}, bf16[272,256]{1,0:T(8,128)(2,1)S(1)}, u32[]{:S(2)}, u32[]{:S(2)}) collective-permute-start(bf16[272,256]{1,0:T(8,128)(2,1)S(1)} %collective-permute-done.9.refs_12_.refs_3_.refs_6_), channel_id=1, source_target_pairs={{32,0},{64,32},{96,64},{128,96},{160,128},{192,160},{224,192},{0,2... | collective-permute-start | bytes 417800 | tf_op jit(solution)/shard_map/ppermute | solution.py:601
  25.5 9.3 %collective-permute-start = (bf16[272,256]{1,0:T(8,128)(2,1)S(1)}, bf16[272,256]{1,0:T(8,128)(2,1)S(1)}, u32[]{:S(2)}, u32[]{:S(2)}) collective-permute-start(bf16[272,256]{1,0:T(8,128)(2,1)S(1)} %copy-done.3), channel_id=1, source_target_pairs={{4,0},{0,4},{5,1},{1,5},{6,2},{2,6},{7,3},{3,7},{12,8},{8,12},{13,... | collective-permute-start | bytes 417800 | tf_op jit(solution)/shard_map/ppermute | solution.py:601
  28.4 7.8 %collective-permute-start.6 = (bf16[272,256]{1,0:T(8,128)(2,1)S(1)}, bf16[272,256]{1,0:T(8,128)(2,1)S(1)}, u32[]{:S(2)}, u32[]{:S(2)}) collective-permute-start(bf16[272,256]{1,0:T(8,128)(2,1)S(1)} %collective-permute-done.5.refs_7_), channel_id=1, source_target_pairs={{4,0},{0,4},{5,1},{1,5},{6,2},{2,6},{7,3},{3,7},{12,8},{8,12},{13,... | collective-permute-start | bytes 417800 | tf_op jit(solution)/shard_map/ppermute | solution.py:601
  28.8 7.4 %collective-permute-start.4 = (bf16[272,256]{1,0:T(8,128)(2,1)S(1)}, bf16[272,256]{1,0:T(8,128)(2,1)S(1)}, u32[]{:S(2)}, u32[]{:S(2)}) collective-permute-start(bf16[272,256]{1,0:T(8,128)(2,1)S(1)} %collective-permute-done.3.refs_5_), channel_id=1, source_target_pairs={{4,0},{0,4},{5,1},{1,5},{6,2},{2,6},{7,3},{3,7},{12,8},{8,12},{13,... | collective-permute-start | bytes 417800 | tf_op jit(solution)/shard_map/ppermute | solution.py:601
  31.2 11.9 %collective-permute-start.18 = (bf16[128,256]{1,0:T(8,128)(2,1)S(1)}, bf16[128,256]{1,0:T(8,128)(2,1)S(1)}, u32[]{:S(2)}, u32[]{:S(2)}) collective-permute-start(bf16[128,256]{1,0:T(8,128)(2,1)S(1)} %slice.9), channel_id=1, source_target_pairs={{192,0},{224,32},{0,64},{32,96},{64,128},{96,160},{128,192},{160,2... | collective-permute-start | bytes 196616 | tf_op jit(solution)/shard_map/ppermute | solution.py:601
  58.1 10.7 %all-to-all-start.1 = ((f32[8,8,128]{2,1,0:T(8,128)}), f32[8,8,128]{2,1,0:T(8,128)S(1)}, u32[]{:S(2)}, u32[]{:S(2)}) async-start(f32[8,8,128]{2,1,0:T(8,128)} %get-tuple-element.56), calls=%async_computation.1 | async-start | bytes 65536 | tf_op jit(solution)/shard_map/all_to_all | solution.py:675
  67.2 11.7 %collective-permute-start.22 = (bf16[128,256]{1,0:T(8,128)(2,1)S(1)}, bf16[128,256]{1,0:T(8,128)(2,1)S(1)}, u32[]{:S(2)}, u32[]{:S(2)}) collective-permute-start(bf16[128,256]{1,0:T(8,128)(2,1)S(1)} %get-tuple-element.65), channel_id=1, source_target_pairs={{64,0},{96,32},{128,64},{160,96},{192,128},{224,160},{0,192},{32,2... | collective-permute-start | bytes 196616 | tf_op jit(solution)/shard_map/ppermute | solution.py:601
  69.5 9.4 %collective-permute-start.21 = (bf16[144,256]{1,0:T(8,128)(2,1)S(1)}, bf16[144,256]{1,0:T(8,128)(2,1)S(1)}, u32[]{:S(2)}, u32[]{:S(2)}) collective-permute-start(bf16[144,256]{1,0:T(8,128)(2,1)S(1)} %get-tuple-element.64), channel_id=1, source_target_pairs={{192,0},{224,32},{0,64},{32,96},{64,128},{96,160},{128,192},{160,2... | collective-permute-start | bytes 221192 | tf_op jit(solution)/shard_map/ppermute | solution.py:601
  70.9 8.9 %collective-permute-start.19 = (bf16[272,256]{1,0:T(8,128)(2,1)S(1)}, bf16[272,256]{1,0:T(8,128)(2,1)S(1)}, u32[]{:S(2)}, u32[]{:S(2)}) collective-permute-start(bf16[272,256]{1,0:T(8,128)(2,1)S(1)} %get-tuple-element.62), channel_id=1, source_target_pairs={{224,0},{0,32},{32,64},{64,96},{96,128},{128,160},{160,192},{192,2... | collective-permute-start | bytes 417800 | tf_op jit(solution)/shard_map/ppermute | solution.py:601
  72.5 7.3 %collective-permute-start.20 = (bf16[272,256]{1,0:T(8,128)(2,1)S(1)}, bf16[272,256]{1,0:T(8,128)(2,1)S(1)}, u32[]{:S(2)}, u32[]{:S(2)}) collective-permute-start(bf16[272,256]{1,0:T(8,128)(2,1)S(1)} %get-tuple-element.63), channel_id=1, source_target_pairs={{32,0},{64,32},{96,64},{128,96},{160,128},{192,160},{224,192},{0,2... | collective-permute-start | bytes 417800 | tf_op jit(solution)/shard_map/ppermute | solution.py:601
  83.6 18.6 %all-to-all-start.2 = ((bf16[8,256,128]{2,1,0:T(8,128)(2,1)}), bf16[8,256,128]{2,1,0:T(8,128)(2,1)S(1)}, u32[]{:S(2)}, u32[]{:S(2)}) async-start(bf16[8,256,128]{2,1,0:T(8,128)(2,1)} %get-tuple-element.66), calls=%async_computation.2 | async-start | bytes 1048576 | tf_op jit(solution)/shard_map/all_to_all | solution.py:714
  89.1 6.5 %collective-permute-start.23 = (bf16[272,256]{1,0:T(8,128)(2,1)S(1)}, bf16[272,256]{1,0:T(8,128)(2,1)S(1)}, u32[]{:S(2)}, u32[]{:S(2)}) collective-permute-start(bf16[272,256]{1,0:T(8,128)(2,1)S(1)} %get-tuple-element.68), channel_id=1, source_target_pairs={{224,0},{0,32},{32,64},{64,96},{96,128},{128,160},{160,192},{192,2... | collective-permute-start | bytes 417800 | tf_op jit(solution)/shard_map/ppermute | solution.py:601
  89.5 6.1 %collective-permute-start.24 = (bf16[272,256]{1,0:T(8,128)(2,1)S(1)}, bf16[272,256]{1,0:T(8,128)(2,1)S(1)}, u32[]{:S(2)}, u32[]{:S(2)}) collective-permute-start(bf16[272,256]{1,0:T(8,128)(2,1)S(1)} %get-tuple-element.69), channel_id=1, source_target_pairs={{32,0},{64,32},{96,64},{128,96},{160,128},{192,160},{224,192},{0,2... | collective-permute-start | bytes 417800 | tf_op jit(solution)/shard_map/ppermute | solution.py:601
  91.8 7.2 %collective-permute-start.25 = (bf16[272,256]{1,0:T(8,128)(2,1)S(1)}, bf16[272,256]{1,0:T(8,128)(2,1)S(1)}, u32[]{:S(2)}, u32[]{:S(2)}) collective-permute-start(bf16[272,256]{1,0:T(8,128)(2,1)S(1)} %get-tuple-element.70), channel_id=1, source_target_pairs={{192,0},{224,32},{0,64},{32,96},{64,128},{96,160},{128,192},{160,2... | collective-permute-start | bytes 417800 | tf_op jit(solution)/shard_map/ppermute | solution.py:601
  92.4 9.8 %collective-permute-start.26 = (bf16[272,256]{1,0:T(8,128)(2,1)S(1)}, bf16[272,256]{1,0:T(8,128)(2,1)S(1)}, u32[]{:S(2)}, u32[]{:S(2)}) collective-permute-start(bf16[272,256]{1,0:T(8,128)(2,1)S(1)} %get-tuple-element.71), channel_id=1, source_target_pairs={{64,0},{96,32},{128,64},{160,96},{192,128},{224,160},{0,192},{32,2... | collective-permute-start | bytes 417800 | tf_op jit(solution)/shard_map/ppermute | solution.py:601
  (12 other events, 85.7 us)
